TPU v7x, 256 devices: a whole 4x4x8 slice. The times are simulated.
256 devices in a mesh: row: 16 (over y, z_lo, core), col: 16 (over z_hi, x).
Axes of the slice: x: 4, y: 4, z: 8 (z_hi: 4, z_lo: 2; z = z_hi * 2 + z_lo), core: 2. Of those that a mesh axis runs over, the one named last changes fastest.
Arguments:
- pair: bfloat16 [256, 256, 128], P('row', 'col'), may hold values from -6 to 6
- pair_cot: bfloat16 [256, 256, 128], P('row', 'col'), may hold values from -6 to 6
- mask: int32 [256], replicated, may hold values 0 or 1
- chain_ids: int32 [256], replicated, may hold values from 0 to 3, never falling along the last dimension, each value on 1 to 128 neighbouring positions
- chain_bias: float32 [128], replicated, may hold values from -4 to 4
- in_weight: bfloat16 [2, 128, 512], replicated, may hold values from -0.5 to 0.5
- gate_weight: bfloat16 [2, 128, 128], replicated, may hold values from -0.5 to 0.5
- out_weight: bfloat16 [2, 128, 128], replicated, may hold values from -0.5 to 0.5
- in_gain: float32 [2, 128], replicated, may hold values from 0.1 to 1.9
- out_gain: float32 [2, 128], replicated, may hold values from 0.1 to 1.9
Outputs:
- new_pair: bfloat16 [256, 256, 128], P('row', 'col')
- pair_grad: float32 [256, 256, 128], P('row', 'col')
- in_weight_grad: float32 [2, 128, 512], replicated
- gate_weight_grad: float32 [2, 128, 128], replicated
- out_weight_grad: float32 [2, 128, 128], replicated
Inputs may be any that keep to these rules, and one draw needn't show every extreme that they name: `chain_ids`: chain numbers never fall along the residues; each of the 4 chains has 1 to 128 residues, one exactly 128.
All inputs are finite; a program needn't handle non-finite values.
Results may differ from a plain program's by a relative error of at most 0.027.
Values may be sent and summed in bfloat16 or wider, within the bound.
No kernel may reach another device: no remote copies, remote signals or barrier semaphores. Data moves between devices by JAX's collectives and lax.ppermute only.
A program may use at most 64 MiB of HBM per device.

v0:
```python
import jax
import jax.numpy as jnp
from jax import lax
from jax.sharding import PartitionSpec as P


def layer_norm(value, gain):
    mean = jnp.mean(value, axis=-1, keepdims=True)
    centered = value - mean
    var = jnp.mean(centered * centered, axis=-1, keepdims=True)
    return centered * lax.rsqrt(var + 1e-05) * gain


def prepare(field, w_in, w_gate, gain, mask_rows, mask_cols):
    normed = layer_norm(field, gain).astype(jnp.bfloat16)
    proj = jnp.dot(normed, w_in, preferred_element_type=jnp.float32)
    width = w_in.shape[1] // 4
    pair_mask = mask_rows[:, None, None] * mask_cols[None, :, None]
    left = pair_mask * jax.nn.sigmoid(proj[..., 0:width]) * proj[..., width : 2 * width]
    right = (
        pair_mask
        * jax.nn.sigmoid(proj[..., 2 * width : 3 * width])
        * proj[..., 3 * width : 4 * width]
    )
    gating = jax.nn.sigmoid(jnp.dot(normed, w_gate, preferred_element_type=jnp.float32))
    return (left.astype(jnp.bfloat16), right.astype(jnp.bfloat16), gating)


def finish(product, gating, field, gain, w_out):
    normed = layer_norm(product, gain).astype(jnp.bfloat16)
    return field + gating * jnp.dot(normed, w_out, preferred_element_type=jnp.float32)


def row_panel(value):
    return lax.all_gather(value, "row", axis=0, tiled=True)


def col_panel(value):
    return lax.all_gather(value, "col", axis=1, tiled=True)


def row_total(term_fn, rows):
    return lax.psum_scatter(
        term_fn(jnp.int32(0), rows * lax.axis_size("row")).astype(jnp.bfloat16),
        "row",
        scatter_dimension=0,
        tiled=True,
    ).astype(jnp.float32)


def col_total(term_fn, rows):
    return lax.psum_scatter(
        term_fn(jnp.int32(0), rows * lax.axis_size("col")).astype(jnp.bfloat16),
        "col",
        scatter_dimension=0,
        tiled=True,
    ).astype(jnp.float32)


def sync_update(grads):
    return lax.psum((grads[0], grads[1], grads[2]), ("row", "col"))


def shards(
    pair,
    pair_cot,
    mask,
    chain_ids,
    chain_bias,
    in_weight,
    gate_weight,
    out_weight,
    in_gain,
    out_gain,
):
    rows_here = pair.shape[0]
    cols_here = pair.shape[1]
    row_start = lax.axis_index("row") * rows_here
    col_start = lax.axis_index("col") * cols_here
    mask_f = mask.astype(jnp.float32)
    mask_rows = lax.dynamic_slice_in_dim(mask_f, row_start, rows_here)
    mask_cols = lax.dynamic_slice_in_dim(mask_f, col_start, cols_here)
    chain_rows = lax.dynamic_slice_in_dim(chain_ids, row_start, rows_here)
    chain_cols = lax.dynamic_slice_in_dim(chain_ids, col_start, cols_here)
    same = (chain_rows[:, None] == chain_cols[None, :]).astype(jnp.float32)
    start = pair.astype(jnp.float32) + same[:, :, None] * chain_bias

    def pre0(field, wi, wg):
        return prepare(field, wi, wg, in_gain[0], mask_rows, mask_cols)

    def pre1(field, wi, wg):
        return prepare(field, wi, wg, in_gain[1], mask_rows, mask_cols)

    def fin0(xx, gg, zz, ww):
        return finish(xx, gg, zz, out_gain[0], ww)

    def fin1(xx, gg, zz, ww):
        return finish(xx, gg, zz, out_gain[1], ww)

    (left0, right0, gate0), back_pre0 = jax.vjp(pre0, start, in_weight[0], gate_weight[0])
    right0_full = row_panel(right0)

    def out_term(begin, count):
        return jnp.einsum("jkc,ikc->jic", right0_full, left0, preferred_element_type=jnp.float32)

    prod0 = jnp.swapaxes(col_total(out_term, cols_here), 0, 1)
    first, back_fin0 = jax.vjp(fin0, prod0, gate0, start, out_weight[0])
    (left1, right1, gate1), back_pre1 = jax.vjp(pre1, first, in_weight[1], gate_weight[1])
    left1_full = col_panel(left1)

    def in_term(begin, count):
        return jnp.einsum("kic,kjc->ijc", left1_full, right1, preferred_element_type=jnp.float32)

    prod1 = row_total(in_term, rows_here)
    second, back_fin1 = jax.vjp(fin1, prod1, gate1, first, out_weight[1])
    new_pair = second.astype(jnp.bfloat16)
    gx1, gg1, gz_fin1, gwo1 = back_fin1(pair_cot.astype(jnp.float32))
    gx1 = gx1.astype(jnp.bfloat16)
    gx1_full = row_panel(gx1)
    gb1 = jnp.einsum(
        "kic,ijc->kjc", left1_full, gx1_full, preferred_element_type=jnp.float32
    ).astype(jnp.bfloat16)

    def in_back_term(begin, count):
        return jnp.einsum("ijc,kjc->ikc", gx1_full, right1, preferred_element_type=jnp.float32)

    ga1 = jnp.swapaxes(col_total(in_back_term, cols_here), 0, 1).astype(jnp.bfloat16)
    gz_pre1, gwi1, gwg1 = back_pre1((ga1, gb1, gg1))
    grad_first = gz_fin1 + gz_pre1
    grads_one = (gwi1.astype(jnp.float32), gwg1.astype(jnp.float32), gwo1.astype(jnp.float32))
    grads_one = sync_update(grads_one)
    gx0, gg0, gz_fin0, gwo0 = back_fin0(grad_first)
    gx0 = gx0.astype(jnp.bfloat16)
    gx0_full = col_panel(gx0)
    ga0 = jnp.einsum(
        "ijc,jkc->ikc", gx0_full, right0_full, preferred_element_type=jnp.float32
    ).astype(jnp.bfloat16)

    def out_back_term(begin, count):
        return jnp.einsum("ijc,ikc->jkc", gx0_full, left0, preferred_element_type=jnp.float32)

    gb0 = row_total(out_back_term, rows_here).astype(jnp.bfloat16)
    gz_pre0, gwi0, gwg0 = back_pre0((ga0, gb0, gg0))
    pair_grad = gz_fin0 + gz_pre0
    grads_zero = (gwi0.astype(jnp.float32), gwg0.astype(jnp.float32), gwo0.astype(jnp.float32))
    grads_zero = sync_update(grads_zero)
    in_weight_grad = jnp.stack([grads_zero[0], grads_one[0]])
    gate_weight_grad = jnp.stack([grads_zero[1], grads_one[1]])
    out_weight_grad = jnp.stack([grads_zero[2], grads_one[2]])
    return (new_pair, pair_grad, in_weight_grad, gate_weight_grad, out_weight_grad)


def solution(mesh):
    return jax.shard_map(
        shards,
        mesh=mesh,
        in_specs=(
            P("row", "col", None),
            P("row", "col", None),
            P(),
            P(),
            P(),
            P(),
            P(),
            P(),
            P(),
            P(),
        ),
        out_specs=(P("row", "col", None), P("row", "col", None), P(), P(), P()),
        check_vma=False,
    )
```

profile of v0, /device:TPU:1, one launch (start us, length us, event | category | flops | bytes accessed | tf_op | source)
XLA Modules:
  0.0 816.6 jit_solution(4805964152072713189)
XLA Ops:
  15.3 38.9 %all-gather.5.cloned.1.call-done = bf16[256,16,128]{2,1,0:T(8,128)(2,1)} async-done(((bf16[16,16,128]{2,1,0:T(8,128)(2,1)}), bf16[256,16,128]{2,1,0:T(8,128)(2,1)}) %all-gather.5.cloned.1.call-update) | async-done | bytes 1048592 | tf_op jit(solution)/shard_map/all_gather | solution.py:35
  54.2 2.2 copy.103
  56.9 2.4 copy.80
  59.9 83.6 %reduce-scatter.5.cloned.1.call-done = bf16[16,16,128]{2,1,0:T(8,128)(2,1)} async-done(((bf16[256,16,128]{2,1,0:T(8,128)(2,1)}), bf16[16,16,128]{2,1,0:T(8,128)(2,1)}) %reduce-scatter.5.cloned.1.call-update) | async-done | bytes 65552 | tf_op jit(solution)/shard_map/reduce_scatter | solution.py:52
  150.9 52.7 %all-gather.7.cloned.1.call-done = bf16[16,256,128]{2,1,0:T(8,128)(2,1)} async-done(((bf16[16,16,128]{2,1,0:T(8,128)(2,1)}), bf16[16,256,128]{2,1,0:T(8,128)(2,1)}) %all-gather.7.cloned.1.call-update) | async-done | bytes 1048592 | tf_op jit(solution)/shard_map/all_gather | solution.py:39
  203.6 1.9 copy.83
  206.9 3.2 copy.84
  211.3 58.3 %reduce-scatter.7.cloned.1.call-done = bf16[16,16,128]{2,1,0:T(8,128)(2,1)} async-done(((bf16[256,16,128]{2,1,0:T(8,128)(2,1)}), bf16[16,16,128]{2,1,0:T(8,128)(2,1)}) %reduce-scatter.7.cloned.1.call-update) | async-done | bytes 65552 | tf_op jit(solution)/shard_map/reduce_scatter | solution.py:43
  274.5 36.8 %all-gather.9.cloned.1.call-done = bf16[256,16,128]{2,1,0:T(8,128)(2,1)} async-done(((bf16[16,16,128]{2,1,0:T(8,128)(2,1)}), bf16[256,16,128]{2,1,0:T(8,128)(2,1)}) %all-gather.9.cloned.1.call-update) | async-done | bytes 1048592 | tf_op jit(solution)/shard_map/all_gather | solution.py:35
  311.3 7.6 copy.97
  318.8 6.6 fusion.134
  325.5 2.7 copy.98
  330.3 6.5 fusion.133
  338.3 74.2 %reduce-scatter.9.cloned.1.call-done = bf16[16,16,128]{2,0,1:T(8,128)(2,1)} async-done(((bf16[256,16,128]{2,0,1:T(8,128)(2,1)}), bf16[16,16,128]{2,0,1:T(8,128)(2,1)}) %reduce-scatter.9.cloned.1.call-update) | async-done | bytes 65552 | tf_op jit(solution)/shard_map/reduce_scatter | solution.py:52
  424.6 52.0 %all-gather.11.cloned.1.call-done = bf16[16,256,128]{2,0,1:T(8,128)(2,1)} async-done(((bf16[16,16,128]{2,0,1:T(8,128)(2,1)}), bf16[16,256,128]{2,0,1:T(8,128)(2,1)}) %all-gather.11.cloned.1.call-update) | async-done | bytes 1048592 | tf_op jit(solution)/shard_map/all_gather | solution.py:39
  476.6 2.2 copy.101
  480.2 3.2 copy.102
  483.4 1.8 fusion.29
  487.0 2.1 fusion.5
  489.1 1.9 fusion.31
  491.0 2.0 fusion.35
  493.9 49.0 %reduce-scatter.11.cloned.1.call-done = bf16[16,16,128]{2,1,0:T(8,128)(2,1)} async-done(((bf16[256,16,128]{2,1,0:T(8,128)(2,1)}), bf16[16,16,128]{2,1,0:T(8,128)(2,1)}) %reduce-scatter.11.cloned.1.call-update) | async-done | bytes 65552 | tf_op jit(solution)/shard_map/reduce_scatter | solution.py:43
  551.3 255.2 %all-reduce.11.cloned.1.call-done = (f32[1,128,512]{2,1,0:T(8,128)}, f32[1,128,512]{2,1,0:T(8,128)}, f32[1,128,128]{2,1,0:T(8,128)}, f32[1,128,128]{2,1,0:T(8,12...) async-done(((f32[1,128,512]{2,1,0:T(8,128)}, f32[1,128,512]{2,1,0:T(8,128)}, f32[1,128,128]{2,1,0:T(8,128)}, f32[1,128,128]{2,1,0:T(8,128)}, f32[1,128,128]{2,1,0:T(8,128)}, ...) | async-done | bytes 786448 | tf_op jit(solution)/shard_map/psum | solution.py:61
  806.5 1.9 pad_maximum_fusion
  (153 shorter events, 53.4 us)
Async XLA Ops:
  7.2 139.5 %copy-start.4 = (bf16[16,16,128]{2,1,0:T(8,128)(2,1)S(1)}, bf16[16,16,128]{2,1,0:T(8,128)(2,1)}, u32[]{:S(2)}) copy-start(bf16[16,16,128]{2,1,0:T(8,128)(2,1)} %param.10) | copy-start | bytes 196612
  7.2 139.5 %copy-start.30 = (f32[128]{0:T(128)S(1)}, f32[128]{0:T(128)}, u32[]{:S(2)}) copy-start(f32[128]{0:T(128)} %param.14) | copy-start | bytes 1540
  7.2 141.5 %copy-start.11 = (bf16[2,128,512]{2,1,0:T(8,128)(2,1)S(1)}, bf16[2,128,512]{2,1,0:T(8,128)(2,1)}, u32[]{:S(2)}) copy-start(bf16[2,128,512]{2,1,0:T(8,128)(2,1)} %param.15) | copy-start | bytes 786436
  7.2 138.3 %copy-start.29 = (bf16[2,128,128]{2,1,0:T(8,128)(2,1)S(1)}, bf16[2,128,128]{2,1,0:T(8,128)(2,1)}, u32[]{:S(2)}) copy-start(bf16[2,128,128]{2,1,0:T(8,128)(2,1)} %param.17) | copy-start | bytes 196612
  7.2 139.4 %copy-start.28 = (bf16[2,128,128]{2,1,0:T(8,128)(2,1)S(1)}, bf16[2,128,128]{2,1,0:T(8,128)(2,1)}, u32[]{:S(2)}) copy-start(bf16[2,128,128]{2,1,0:T(8,128)(2,1)} %param.16) | copy-start | bytes 196612
  7.2 46.9 %all-gather.5.cloned.1.call-start = ((), (), s32[]{:S(2)}) async-start(), calls=%async_computation.4 | async-start | bytes 1114112 | tf_op jit(solution)/shard_map/all_gather | solution.py:35
  8.0 198.9 %copy-start.31 = (f32[128]{0:T(128)}, f32[128]{0:T(128)S(1)}, u32[]{:S(2)}) copy-start(f32[128]{0:T(128)S(1)} %get-tuple-element.37) | copy-start | bytes 1540
  8.1 198.9 %copy-start.32 = (f32[128]{0:T(128)}, f32[128]{0:T(128)S(1)}, u32[]{:S(2)}) copy-start(f32[128]{0:T(128)S(1)} %get-tuple-element.38) | copy-start | bytes 1540
  11.1 136.8 %copy-start.15 = (f32[16,16]{1,0:T(8,128)}, f32[16,16]{1,0:T(8,128)S(1)}, u32[]{:S(2)}) copy-start(f32[16,16]{1,0:T(8,128)S(1)} %fusion.116) | copy-start | bytes 3076
  11.9 195.0 %copy-start.14 = (f32[16,16]{1,0:T(8,128)}, f32[16,16]{1,0:T(8,128)S(1)}, u32[]{:S(2)}) copy-start(f32[16,16]{1,0:T(8,128)S(1)} %broadcast_multiply_fusion) | copy-start | bytes 3076
  14.8 128.7 %reduce-scatter.5.cloned.1.call-start = ((), (), s32[]{:S(2)}) async-start(), calls=%async_computation.5 | async-start | bytes 1114112 | tf_op jit(solution)/shard_map/reduce_scatter | solution.py:52
  56.9 213.6 %copy-start.8 = (bf16[16,16,128]{2,1,0:T(8,128)(2,1)S(1)}, bf16[16,16,128]{2,1,0:T(8,128)(2,1)}, u32[]{:S(2)}) copy-start(bf16[16,16,128]{2,1,0:T(8,128)(2,1)} %param.11) | copy-start | bytes 196612
  59.3 144.3 %all-gather.7.cloned.1.call-start = ((), (), s32[]{:S(2)}) async-start(), calls=%async_computation.6 | async-start | bytes 1114112 | tf_op jit(solution)/shard_map/all_gather | solution.py:39
  59.9 85.7 %copy-start.33 = (f32[128]{0:T(128)}, f32[128]{0:T(128)S(1)}, u32[]{:S(2)}) copy-start(f32[128]{0:T(128)S(1)} %get-tuple-element.36) | copy-start | bytes 1540
  150.4 119.1 %reduce-scatter.7.cloned.1.call-start = ((), (), s32[]{:S(2)}) async-start(), calls=%async_computation.7 | async-start | bytes 1114112 | tf_op jit(solution)/shard_map/reduce_scatter | solution.py:43
  210.2 101.1 %all-gather.9.cloned.1.call-start = ((), (), s32[]{:S(2)}) async-start(), calls=%async_computation.8 | async-start | bytes 1114112 | tf_op jit(solution)/shard_map/all_gather | solution.py:35
  211.3 204.0 %copy-start.6 = (f32[16,16,128]{2,1,0:T(8,128)}, f32[16,16,128]{2,1,0:T(8,128)S(1)}, u32[]{:S(2)}) copy-start(f32[16,16,128]{2,1,0:T(8,128)S(1)} %fusion.13) | copy-start | bytes 393220
  274.5 138.0 %reduce-scatter.9.cloned.1.call-start = ((), (), s32[]{:S(2)}) async-start(), calls=%async_computation.9 | async-start | bytes 1114112 | tf_op jit(solution)/shard_map/reduce_scatter | solution.py:52
  325.5 86.9 %copy-start.3 = (f32[16,16,512]{2,1,0:T(8,128)S(1)}, f32[16,16,512]{2,1,0:T(8,128)}, u32[]{:S(2)}) copy-start(f32[16,16,512]{2,1,0:T(8,128)} %copy-done.2) | copy-start | bytes 1572868
  328.2 91.8 %copy-start.5 = (bf16[16,16,128]{2,1,0:T(8,128)(2,1)S(1)}, bf16[16,16,128]{2,1,0:T(8,128)(2,1)}, u32[]{:S(2)}) copy-start(bf16[16,16,128]{2,1,0:T(8,128)(2,1)} %reduce-scatter.5.cloned.1.call-done) | copy-start | bytes 196612
  328.2 148.3 %all-gather.11.cloned.1.call-start = ((), (), s32[]{:S(2)}) async-start(), calls=%async_computation.10 | async-start | bytes 1114112 | tf_op jit(solution)/shard_map/all_gather | solution.py:39
  416.5 126.4 %copy-start.1 = (f32[16,16,512]{2,1,0:T(8,128)S(1)}, f32[16,16,512]{2,1,0:T(8,128)}, u32[]{:S(2)}) copy-start(f32[16,16,512]{2,1,0:T(8,128)} %copy-done) | copy-start | bytes 1572868
  424.5 118.3 %reduce-scatter.11.cloned.1.call-start = ((), (), s32[]{:S(2)}) async-start(), calls=%async_computation.11 | async-start | bytes 1114112 | tf_op jit(solution)/shard_map/reduce_scatter | solution.py:43
  483.4 323.1 %all-reduce.11.cloned.1.call-start = ((), (), s32[]{:S(2)}) async-start(), calls=%async_computation.12 | async-start | bytes 1572864 | tf_op jit(solution)/shard_map/psum | solution.py:61
  (20 other events, 501.3 us)
Sparse Core Ops, SparseCore 0:
  14.9 39.2 all-gather.4
  59.4 84.0 reduce-scatter.4
  150.5 52.9 all-gather.6
  210.3 59.2 reduce-scatter.6
  274.6 36.6 all-gather.8
  328.4 84.0 reduce-scatter.8
  424.7 51.8 all-gather.10
  483.5 59.3 reduce-scatter.10
  549.8 256.6 all-reduce.10
where the time goes:
time: 819 us; the launch traced here: 817 us
  waiting for transfers between devices  701 us (86%)
  matrix products  41.5 us (5%)
  local copies, waits for them, and re-layouts  33.9 us (4%)
  other arithmetic  25.3 us (3%)
  between operations  14.5 us (2%)
    psum x1, waiting for transfers between devices, sync_update(): return lax.psum((grads[0], grads[1], grads[2]), ('row', 'col'))  255 us
    reduce_scatter x2, waiting for transfers between devices, col_total(): lax.psum_scatter(term_fn(jnp.int32(0), rows * lax.axis_size('col')).astyp...  158 us
    reduce_scatter x2, waiting for transfers between devices, row_total(): lax.psum_scatter(term_fn(jnp.int32(0), rows * lax.axis_size('row')).astyp...  107 us
    all_gather x2, waiting for transfers between devices, col_panel(): return lax.all_gather(value, 'col', axis=1, tiled=True)  105 us
    all_gather x2, waiting for transfers between devices, row_panel(): return lax.all_gather(value, 'row', axis=0, tiled=True)  75.7 us
  transfers between devices with their start and end apart: 9, of which 9 were waited for; matrix products, arithmetic and copies ran while one was open for 3% of the time, Pallas kernels for 0%

commit v1 on v0

v1 whole, which is shorter than its diff:
```python
import functools

import jax
import jax.numpy as jnp
from jax import lax
from jax.experimental import pallas as pl
from jax.experimental.pallas import tpu as pltpu
from jax.sharding import Mesh, PartitionSpec as P

F32 = jnp.float32
BF16 = jnp.bfloat16
POS = 256
CH = 128
EPS = 1e-05
CHIPS = ("g", "q")
ALL = ("g", "h", "q")


def dot(a, b, ca, cb):
    return lax.dot_general(
        a.astype(BF16), b.astype(BF16), (((ca,), (cb,)), ((), ())), preferred_element_type=F32
    )


def swap_blocks(tiles):
    block = lax.broadcasted_iota(jnp.int32, tiles[0].shape, 1) // 16
    for d in (1, 2, 4):
        high = (block & d) != 0
        out = list(tiles)
        for t in range(8):
            if t & d == 0:
                lo, hi = tiles[t], tiles[t | d]
                out[t] = jnp.where(high, pltpu.roll(hi, 16 * d, 1), lo)
                out[t | d] = jnp.where(high, hi, pltpu.roll(lo, 128 - 16 * d, 1))
        tiles = out
    return tiles


def messages_to_matrix(src, off, w, dst):
    for half in range(2):
        for qh in range(2):
            tiles = [
                src[pl.ds((qh * 8 + t) * w + off + half, 16, stride=16 * w), :] for t in range(8)
            ]
            for t, tile in enumerate(swap_blocks(tiles)):
                dst[qh, pl.ds(half * 8 + t, 16, stride=16), :] = tile


def half_to_messages(src, dst, off, w):
    for half in range(2):
        for qh in range(2):
            tiles = [src[qh, pl.ds(half * 8 + t, 8, stride=16), :] for t in range(8)]
            for t, tile in enumerate(swap_blocks(tiles)):
                dst[pl.ds((qh * 8 + t) * w + off + half, 8, stride=16 * w), :] = tile


def put(ref, value):
    for qh in range(2):
        ref[qh] = value[:, qh * 128 : (qh + 1) * 128]


def get(ref):
    return jnp.concatenate([ref[0], ref[1]], axis=1)


def my_rows(ref):
    h = lax.axis_index("h")
    return jnp.concatenate(
        [
            jnp.concatenate(
                [ref[qh, pl.ds(pl.multiple_of((2 * g + h) * 16, 16), 16), :] for g in range(8)],
                axis=0,
            )
            for qh in range(2)
        ],
        axis=1,
    )


def channels_to_messages(v, dst, off, w):
    for g in range(8):
        for h in range(2):
            for half in range(2):
                dst[pl.ds((g * 32 + h * 16) * w + off + half, 16, stride=w), :] = v[
                    g * 16 : (g + 1) * 16, half * 128 : (half + 1) * 128
                ]


def messages_to_channels(src, off, w):
    return jnp.concatenate(
        [src[pl.ds(off + half, CH, stride=w), :] for half in range(2)], axis=1
    )


def column(row):
    square = jnp.broadcast_to(row, (CH, CH)).T
    return jnp.concatenate([square, square], axis=1)


def normalise(z):
    centered = z - jnp.mean(z, axis=0, keepdims=True)
    rstd = lax.rsqrt(jnp.mean(centered * centered, axis=0, keepdims=True) + EPS)
    return centered * rstd, rstd


def normalise_back(cot, hat, rstd):
    return rstd * (
        cot
        - jnp.mean(cot, axis=0, keepdims=True)
        - hat * jnp.mean(cot * hat, axis=0, keepdims=True)
    )


def prepare(z, gain, w_in, w_gate, m, n_ref, g_ref, send, send_ref):
    hat, _ = normalise(z)
    normed = (hat * gain).astype(BF16)
    n_ref[...] = normed
    p = dot(w_in, normed, 0, 0)
    a = m * jax.nn.sigmoid(p[0:128]) * p[128:256]
    b = m * jax.nn.sigmoid(p[256:384]) * p[384:512]
    g_ref[...] = jax.nn.sigmoid(dot(w_gate, normed, 0, 0))
    channels_to_messages(a, send, 0, 4)
    channels_to_messages(b, send, 2, 4)
    send_ref[...] = send[...].astype(BF16)


def prepare_back(recv, z, normed, gain, w_in, w_gate, m, dpg, dp):
    p = dot(w_in, normed, 0, 0)
    for k in range(2):
        cot = messages_to_channels(recv, 2 * k, 4) * m
        s = jax.nn.sigmoid(p[256 * k : 256 * k + 128])
        v = p[256 * k + 128 : 256 * k + 256]
        dp[256 * k : 256 * k + 128, :] = (cot * v * s * (1.0 - s)).astype(BF16)
        dp[256 * k + 128 : 256 * k + 256, :] = (cot * s).astype(BF16)
    dn = dot(w_in, dp[...], 1, 0) + dot(w_gate, dpg, 1, 0)
    hat, rstd = normalise(z)
    return normalise_back(dn * gain, hat, rstd)


def finish_back(x, dy, gain, w_out):
    hat, rstd = normalise(x)
    normed = (hat * gain).astype(BF16)
    gx = normalise_back(dot(w_out, dy, 1, 0) * gain, hat, rstd)
    return gx, dot(normed, dy, 1, 1)


def start_kernel(pair, mask, chain, bias, in_gain, w_in, w_gate, z_ref, n_ref, g_ref, m_ref, send_ref, send):
    row = 2 * lax.axis_index("g") + lax.axis_index("h")
    col = lax.axis_index("q")
    res = lax.broadcasted_iota(jnp.int32, (256, POS), 0)
    pos = lax.broadcasted_iota(jnp.int32, (256, POS), 1)
    both = jnp.concatenate(
        [
            jnp.broadcast_to(mask[...].astype(F32), (8, 256)),
            jnp.broadcast_to(chain[...].astype(F32), (8, 256)),
        ],
        axis=0,
    )
    of_row = dot(both, (res == row * 16 + pos // 16).astype(F32), 1, 0)
    of_col = dot(both, (res == col * 16 + pos % 16).astype(F32), 1, 0)
    m8 = of_row[0:8] * of_col[0:8]
    m_ref[...] = m8
    same = (of_row[8:9] == of_col[8:9]).astype(F32)
    z = pair[...].astype(F32).T + same * column(bias[...])
    z_ref[...] = z
    prepare(z, column(in_gain[0:1]), w_in[0], w_gate[0], m8[0:1], n_ref, g_ref, send, send_ref)


def middle_kernel(x_in, z0, g0, m, in_gain, out_gain, w_in, w_gate, w_out, z_ref, y_ref, n_ref, g_ref, send_ref, xs, send):
    xs[...] = x_in[...].astype(F32)
    hat, _ = normalise(messages_to_channels(xs, 0, 2))
    y = dot(w_out[0], hat * column(out_gain[0:1]), 0, 0)
    y_ref[...] = y
    z = z0[...] + g0[...] * y
    z_ref[...] = z
    prepare(z, column(in_gain[1:2]), w_in[1], w_gate[1], m[0:1], n_ref, g_ref, send, send_ref)


def turn_kernel(x_in, z1, g1, n1, cot_in, out_gain, w_out, new_ref, cot_ref, dpg_ref, gw_ref, send_ref, xs, send):
    xs[...] = x_in[...].astype(F32)
    x = messages_to_channels(xs, 0, 2)
    gain = column(out_gain[1:2])
    hat, _ = normalise(x)
    y = dot(w_out[1], hat * gain, 0, 0)
    g = g1[...]
    new_ref[...] = (z1[...] + g * y).T.astype(BF16)
    cot = cot_in[...].astype(F32).T
    cot_ref[...] = cot
    gx, gwo = finish_back(x, cot * g, gain, w_out[1])
    dpg = (cot * y * g * (1.0 - g)).astype(BF16)
    dpg_ref[...] = dpg
    gw_ref[0:128, :] = dot(n1[...], dpg, 1, 1)
    gw_ref[128:256, :] = gwo
    channels_to_messages(gx, send, 0, 2)
    send_ref[...] = send[...].astype(BF16)


def back_kernel(gab, n1, z1, m, dpg1, cot, gw1, x_in, g0, y0, n0, in_gain, out_gain, w_in, w_gate, w_out, dz_ref, dpg_ref, send_ref, rs, dp, xs, send):
    rs[...] = gab[...].astype(F32)
    dz = cot[...] + prepare_back(
        rs, z1[...], n1[...], column(in_gain[1:2]), w_in[1], w_gate[1], m[0:1], dpg1[...], dp
    )
    dz_ref[...] = dz
    w1 = [dot(n1[...], dp[128 * e : 128 * (e + 1), :], 1, 1) for e in range(4)]
    g = g0[...]
    dpg = (dz * y0[...] * g * (1.0 - g)).astype(BF16)
    dpg_ref[...] = dpg
    xs[...] = x_in[...].astype(F32)
    gx, gwo = finish_back(
        messages_to_channels(xs, 0, 2), dz * g, column(out_gain[0:1]), w_out[0]
    )
    gwg = dot(n0[...], dpg, 1, 1)
    channels_to_messages(gx, send, 0, 6)
    parts = w1 + [gw1[0:128, :], gw1[128:256, :], gwg, gwo]
    for k, part in enumerate(parts):
        send[pl.ds((k % 2) * 128 * 6 + 2 + k // 2, 128, stride=6), :] = part
    send_ref[...] = send[...].astype(BF16)


def end_kernel(gab, n0, z0, m, dpg0, dz1, in_gain, w_in, w_gate, grad_ref, send_ref, rs, dp, send):
    rs[...] = gab[...].astype(F32)
    dz = dz1[...] + prepare_back(
        rs, z0[...], n0[...], column(in_gain[0:1]), w_in[0], w_gate[0], m[0:1], dpg0[...], dp
    )
    grad_ref[...] = dz.T
    for e in range(4):
        send[pl.ds((e % 2) * 256 + e // 2, 128, stride=2), :] = dot(
            n0[...], dp[128 * e : 128 * (e + 1), :], 1, 1
        )
    send_ref[...] = send[...].astype(BF16)


def sum_kernel(recv, others, send_ref, rs, send):
    rs[...] = recv[...].astype(F32)
    for k in range(6):
        if k < 2:
            total = jnp.sum(rs[pl.ds(k, 256, stride=2), :], axis=0, keepdims=True)
        else:
            total = others[k - 2 : k - 1, :]
        send[pl.ds(k, 256, stride=6), :] = jnp.broadcast_to(total, (256, 128))
    send_ref[...] = send[...].astype(BF16)


def place_kernel(recv, in_ref, gate_ref, out_ref, rs):
    rs[...] = recv[...].astype(F32)
    rows = [rs[pl.ds(k, 256, stride=6), :] for k in range(6)]
    for u, base in ((0, 0), (1, 2)):
        for e in range(4):
            in_ref[u, :, 128 * e : 128 * (e + 1)] = rows[base + e // 2][
                128 * (e % 2) : 128 * (e % 2) + 128
            ]
    for u, k in ((0, 5), (1, 4)):
        gate_ref[u] = rows[k][0:128]
        out_ref[u] = rows[k][128:256]


def product_kernel(incoming, recv, a_ref, b_ref, send_ref, rs, mat, res, send):
    rs[...] = recv[...].astype(F32)
    messages_to_matrix(rs, 2, 4, mat)
    b = get(mat).astype(BF16)
    b_ref[...] = b
    messages_to_matrix(rs, 0, 4, mat)
    a = get(mat).astype(BF16)
    a_ref[...] = a
    if incoming:
        put(mat, dot(a, b, 0, 0))
        put(res, my_rows(mat))
    else:
        put(res, dot(my_rows(mat), b, 1, 1))
    half_to_messages(res, send, 0, 2)
    send_ref[...] = send[...].astype(BF16)


def product_back_kernel(incoming, w, recv, a_in, b_in, *refs):
    if w > 2:
        send_ref, sum_ref, rs, mat, res, send = refs
    else:
        send_ref, rs, mat, res, send = refs
    rs[...] = recv[...].astype(F32)
    messages_to_matrix(rs, 0, w, mat)
    gx = get(mat).astype(BF16)
    if incoming:
        put(mat, b_in[...].astype(F32))
        put(res, dot(my_rows(mat), gx, 1, 1))
    else:
        put(res, dot(my_rows(mat), b_in[...], 1, 0))
    half_to_messages(res, send, 0, 4)
    if incoming:
        put(mat, a_in[...].astype(F32))
        put(res, dot(my_rows(mat), gx, 1, 0))
    else:
        put(mat, dot(gx, a_in[...], 0, 0))
        put(res, my_rows(mat))
    half_to_messages(res, send, 2, 4)
    send_ref[...] = send[...].astype(BF16)
    if w > 2:
        sum_ref[...] = jnp.zeros((8, 128), F32)
        for k in range(2, w):
            sum_ref[k - 2 : k - 1, :] = jnp.sum(
                rs[pl.ds(k, 256, stride=w), :], axis=0, keepdims=True
            )


def call(kernel, name, outs, scratch, *args):
    return pl.pallas_call(
        kernel,
        name=name,
        out_shape=[jax.ShapeDtypeStruct(s, d) for s, d in outs],
        scratch_shapes=[pltpu.VMEM(s, d) for s, d in scratch],
        compiler_params=pltpu.CompilerParams(vmem_limit_bytes=24 * 1024 * 1024),
    )(*args)


def exchange(value, axes):
    return lax.all_to_all(value, axes, 0, 0, tiled=True)


def shards(pair, pair_cot, mask, chain_ids, chain_bias, w_in, w_gate, w_out, in_gain, out_gain):
    block = pair.shape
    pair = pair.reshape(POS, CH)
    cot_in = pair_cot.reshape(POS, CH)
    mask, chain, bias = mask[None, :], chain_ids[None, :], chain_bias[None, :]
    field, field16 = ((CH, POS), F32), ((CH, POS), BF16)
    matrix, matrix16, part = ((2, 256, 128), F32), ((256, 256), BF16), ((2, 128, 128), F32)

    def rows(n, dtype=F32):
        return ((n, 128), dtype)

    z0, n0, g0, m, send = call(
        start_kernel, "start", [field, field16, field, ((8, POS), F32), rows(1024, BF16)], [rows(1024)],
        pair, mask, chain, bias, in_gain, w_in, w_gate,
    )
    a0, b0, send = call(
        functools.partial(product_kernel, False), "outgoing", [matrix16, matrix16, rows(256, BF16)],
        [rows(1024), matrix, part, rows(256)], exchange(send, ALL),
    )
    x0 = exchange(send, CHIPS)
    z1, y0, n1, g1, send = call(
        middle_kernel, "middle", [field, field, field16, field, rows(1024, BF16)], [rows(256), rows(1024)],
        x0, z0, g0, m, in_gain, out_gain, w_in, w_gate, w_out,
    )
    a1, b1, send = call(
        functools.partial(product_kernel, True), "incoming", [matrix16, matrix16, rows(256, BF16)],
        [rows(1024), matrix, part, rows(256)], exchange(send, ALL),
    )
    new_pair, cot, dpg1, gw1, send = call(
        turn_kernel, "turn", [rows(POS, BF16), field, field16, rows(256), rows(512, BF16)],
        [rows(256), rows(512)], exchange(send, CHIPS), z1, g1, n1, cot_in, out_gain, w_out,
    )
    (send,) = call(
        functools.partial(product_back_kernel, True, 2), "incoming_back", [rows(512, BF16)],
        [rows(512), matrix, part, rows(512)], exchange(send, ALL), a1, b1,
    )
    dz1, dpg0, send = call(
        back_kernel, "back", [field, field16, rows(1536, BF16)],
        [rows(512), ((512, POS), BF16), rows(256), rows(1536)],
        exchange(send, CHIPS), n1, z1, m, dpg1, cot, gw1, x0, g0, y0, n0, in_gain, out_gain, w_in, w_gate, w_out,
    )
    send, sums = call(
        functools.partial(product_back_kernel, False, 6), "outgoing_back", [rows(512, BF16), rows(8)],
        [rows(1536), matrix, part, rows(512)], exchange(send, ALL), a0, b0,
    )
    pair_grad, send = call(
        end_kernel, "end", [rows(POS), rows(512, BF16)], [rows(512), ((512, POS), BF16), rows(512)],
        exchange(send, CHIPS), n0, z0, m, dpg0, dz1, in_gain, w_in, w_gate,
    )
    (send,) = call(
        sum_kernel, "sum", [rows(1536, BF16)], [rows(512), rows(1536)], exchange(send, ALL), sums
    )
    in_grad, gate_grad, out_grad = call(
        place_kernel, "place",
        [((2, 128, 512), F32), ((2, 128, 128), F32), ((2, 128, 128), F32)], [rows(1536)],
        exchange(send, ALL),
    )
    return (new_pair.reshape(block), pair_grad.reshape(block), in_grad, gate_grad, out_grad)


def solution(mesh):
    devices = mesh.devices.reshape(8, 2, 16)
    split = P(("g", "h"), "q", None)
    return jax.shard_map(
        shards,
        mesh=Mesh(devices, ALL),
        in_specs=(split, split) + (P(),) * 8,
        out_specs=(split, split, P(), P(), P()),
        check_vma=False,
    )
```

time: 819 us -> 231 us (0.28)
  waiting for transfers between devices: 701 us -> 0 us
  blocking collectives: 0 us -> 215 us
  matrix products: 41.5 us -> 0 us
  local copies, waits for them, and re-layouts: 33.9 us -> 4.53 us
  other arithmetic: 25.3 us -> 0 us
  between operations: 14.5 us -> 0.79 us
  Pallas kernels: 0 us -> 9.72 us
    reduce_scatter x4 -> x0, waiting for transfers between devices: 265 us -> none  [the longest x2 158 us: col_total(): lax.psum_scatter(term_fn(jnp.int32(0), rows * lax.axis_size('col')).astyp...]
    psum x1 -> x0, waiting for transfers between devices: 255 us -> none  [sync_update(): return lax.psum((grads[0], grads[1], grads[2]), ('row', 'col'))]
    all_to_all x0 -> x10, blocking collectives: none -> 215 us  [exchange(): return lax.all_to_all(value, axes, 0, 0, tiled=True)]
    all_gather x4 -> x0, waiting for transfers between devices: 180 us -> none  [the longest x2 105 us: col_panel(): return lax.all_gather(value, 'col', axis=1, tiled=True)]
    dot_general x24 -> x0, matrix products: 41.5 us -> none  [the longest x6 8.92 us: finish(): jnp.dot(normed, w_out, preferred_element_type=jnp.float32)]
    all_gather x4 -> x0, local copies, waits for them, and re-layouts: 13.8 us -> none  [the longest x2 9.77 us: row_panel(): return lax.all_gather(value, 'row', axis=0, tiled=True)]
    pallas_call x0 -> x11, Pallas kernels: none -> 9.72 us  [call(): pl.pallas_call(kernel, name=name, out_shape=[jax.ShapeDtypeStruct(s, d) f...]
    reduce_sum x10 -> x0, other arithmetic: 9.18 us -> none  [the longest x4 3.99 us: layer_norm(): centered = value - mean]
  transfers between devices with their start and end apart: 9 -> 0, of which waited for: 9 -> 0; matrix products, arithmetic and copies ran while one was open for 3% -> 0% of each run, Pallas kernels for 0% -> 0%
where the time goes in v1:
time: 231 us; the launch traced here: 230 us
  blocking collectives  215 us (93%)
  Pallas kernels  9.72 us (4%)
  local copies, waits for them, and re-layouts  4.53 us (2%)
    all_to_all x10, blocking collectives, exchange(): return lax.all_to_all(value, axes, 0, 0, tiled=True)  215 us
    pallas_call x11, Pallas kernels, call(): pl.pallas_call(kernel, name=name, out_shape=[jax.ShapeDtypeStruct(s, d) f...  9.72 us

profile of v1, /device:TPU:1, one launch (start us, length us, event | category | flops | bytes accessed | tf_op | source)
XLA Modules:
  0.0 229.9 jit_solution(3293256513292055167)
XLA Ops:
  0.7 0.6 copy-done.9
  1.3 0.9 copy-done
  2.3 0.8 copy-done.2
  3.1 0.8 copy-done.5
  4.5 31.1 %all_to_all.110 = bf16[256,4,128]{2,1,0:T(4,128)(2,1)S(1)} all-to-all(bf16[256,4,128]{2,1,0:T(4,128)(2,1)S(1)} %bitcast.32), channel_id=1, replica_groups=mesh['g'=8,'h'=2,'q'=16] {'g','h','q'}, dimensions={0} | all-to-all | bytes 524288 | tf_op jit(solution)/shard_map/all_to_all | solution.py:315
  35.6 1.2 outgoing.1
  36.8 16.5 %all_to_all.111 = bf16[128,2,128]{2,1,0:T(2,128)(2,1)S(1)} all-to-all(bf16[128,2,128]{2,1,0:T(2,128)(2,1)S(1)} %bitcast.39), channel_id=1, replica_groups=mesh['g'=8,'h'=2,'q'=16] {'g','q'}, dimensions={0} | all-to-all | bytes 131072 | tf_op jit(solution)/shard_map/all_to_all | solution.py:315
  53.3 0.7 copy-done.8
  54.0 0.6 middle.1
  54.5 22.7 %all_to_all.112 = bf16[256,4,128]{2,1,0:T(4,128)(2,1)S(1)} all-to-all(bf16[256,4,128]{2,1,0:T(4,128)(2,1)S(1)} %bitcast.33), channel_id=1, replica_groups=mesh['g'=8,'h'=2,'q'=16] {'g','h','q'}, dimensions={0} | all-to-all | bytes 524288 | tf_op jit(solution)/shard_map/all_to_all | solution.py:315
  77.2 1.3 incoming.1
  78.6 16.5 %all_to_all.113 = bf16[128,2,128]{2,1,0:T(2,128)(2,1)S(1)} all-to-all(bf16[128,2,128]{2,1,0:T(2,128)(2,1)S(1)} %bitcast.40), channel_id=1, replica_groups=mesh['g'=8,'h'=2,'q'=16] {'g','q'}, dimensions={0} | all-to-all | bytes 131072 | tf_op jit(solution)/shard_map/all_to_all | solution.py:315
  95.0 1.0 turn.1
  96.0 20.1 %all_to_all.114 = bf16[256,2,128]{2,1,0:T(2,128)(2,1)S(1)} all-to-all(bf16[256,2,128]{2,1,0:T(2,128)(2,1)S(1)} %bitcast.36), channel_id=1, replica_groups=mesh['g'=8,'h'=2,'q'=16] {'g','h','q'}, dimensions={0} | all-to-all | bytes 262144 | tf_op jit(solution)/shard_map/all_to_all | solution.py:315
  116.1 1.0 incoming_back.1
  117.1 16.9 %all_to_all.115 = bf16[128,4,128]{2,1,0:T(4,128)(2,1)S(1)} all-to-all(bf16[128,4,128]{2,1,0:T(4,128)(2,1)S(1)} %bitcast.29), channel_id=1, replica_groups=mesh['g'=8,'h'=2,'q'=16] {'g','q'}, dimensions={0} | all-to-all | bytes 262144 | tf_op jit(solution)/shard_map/all_to_all | solution.py:315
  134.0 0.8 back.1
  134.9 27.9 %all_to_all.116 = bf16[256,6,128]{2,1,0:T(8,128)(2,1)S(1)} all-to-all(bf16[256,6,128]{2,1,0:T(8,128)(2,1)S(1)} %all_to_all.88), channel_id=1, replica_groups=mesh['g'=8,'h'=2,'q'=16] {'g','h','q'}, dimensions={0} | all-to-all | bytes 786432 | tf_op jit(solution)/shard_map/all_to_all | solution.py:315
  162.9 1.0 outgoing_back.1
  164.0 17.1 %all_to_all.117 = bf16[128,4,128]{2,1,0:T(4,128)(2,1)S(1)} all-to-all(bf16[128,4,128]{2,1,0:T(4,128)(2,1)S(1)} %bitcast.37), channel_id=1, replica_groups=mesh['g'=8,'h'=2,'q'=16] {'g','q'}, dimensions={0} | all-to-all | bytes 262144 | tf_op jit(solution)/shard_map/all_to_all | solution.py:315
  181.0 1.3 end.1
  182.3 20.1 %all_to_all.118 = bf16[256,2,128]{2,1,0:T(2,128)(2,1)S(1)} all-to-all(bf16[256,2,128]{2,1,0:T(2,128)(2,1)S(1)} %bitcast.35), channel_id=1, replica_groups=mesh['g'=8,'h'=2,'q'=16] {'g','h','q'}, dimensions={0} | all-to-all | bytes 262144 | tf_op jit(solution)/shard_map/all_to_all | solution.py:315
  202.7 26.2 %all_to_all.119 = bf16[256,6,128]{2,1,0:T(8,128)(2,1)S(1)} all-to-all(bf16[256,6,128]{2,1,0:T(8,128)(2,1)S(1)} %all_to_all.97), channel_id=1, replica_groups=mesh['g'=8,'h'=2,'q'=16] {'g','h','q'}, dimensions={0} | all-to-all | bytes 786432 | tf_op jit(solution)/shard_map/all_to_all | solution.py:315
  229.0 1.0 place.1
  (25 shorter events, 1.2 us)
Async XLA Ops:
  0.6 0.7 copy-start.9
  0.6 0.7 copy-start.10
  0.7 0.7 copy-start.7
  0.7 0.7 copy-start.11
  1.3 1.0 copy-start
  2.3 0.8 copy-start.2
  3.1 0.8 copy-start.5
  35.6 17.6 %copy-start.1 = (bf16[2,128,512]{2,1,0:T(8,128)(2,1)S(1)}, bf16[2,128,512]{2,1,0:T(8,128)(2,1)}, u32[]{:S(2)}) copy-start(bf16[2,128,512]{2,1,0:T(8,128)(2,1)} %w_in.7) | copy-start | bytes 786436
  36.8 16.5 %copy-start.3 = (bf16[2,128,128]{2,1,0:T(8,128)(2,1)S(1)}, bf16[2,128,128]{2,1,0:T(8,128)(2,1)}, u32[]{:S(2)}) copy-start(bf16[2,128,128]{2,1,0:T(8,128)(2,1)} %w_gate.7) | copy-start | bytes 196612
  36.8 16.5 %copy-start.4 = (bf16[2,128,128]{2,1,0:T(8,128)(2,1)S(1)}, bf16[2,128,128]{2,1,0:T(8,128)(2,1)}, u32[]{:S(2)}) copy-start(bf16[2,128,128]{2,1,0:T(8,128)(2,1)} %w_out.5) | copy-start | bytes 196612
  53.3 0.7 copy-start.8
  78.6 16.5 %copy-start.6 = (bf16[16,16,128]{2,1,0:T(8,128)(2,1)S(1)}, bf16[16,16,128]{2,1,0:T(8,128)(2,1)}, u32[]{:S(2)}) copy-start(bf16[16,16,128]{2,1,0:T(8,128)(2,1)} %param.11) | copy-start | bytes 196612

commit v2 on v1

--- a/solution.py
+++ b/solution.py
@@ -124,10 +124,10 @@
     send_ref[...] = send[...].astype(BF16)
 
 
-def prepare_back(recv, z, normed, gain, w_in, w_gate, m, dpg, dp):
+def prepare_back(recv, w, z, normed, gain, w_in, w_gate, m, dpg, dp):
     p = dot(w_in, normed, 0, 0)
     for k in range(2):
-        cot = messages_to_channels(recv, 2 * k, 4) * m
+        cot = messages_to_channels(recv, 2 * k, w) * m
         s = jax.nn.sigmoid(p[256 * k : 256 * k + 128])
         v = p[256 * k + 128 : 256 * k + 256]
         dp[256 * k : 256 * k + 128, :] = (cot * v * s * (1.0 - s)).astype(BF16)
@@ -144,11 +144,24 @@
     return gx, dot(normed, dy, 1, 1)
 
 
-def start_kernel(pair, mask, chain, bias, in_gain, w_in, w_gate, z_ref, n_ref, g_ref, m_ref, send_ref, send):
+def start_kernel(*refs):
+    hbm, (z_ref, n_ref, g_ref, m_ref, gain_ref, send_ref), refs = refs[:8], refs[8:14], refs[14:]
+    vmem, send, sem = refs[:8], refs[8], refs[9]
+    copies = [
+        pltpu.make_async_copy(src.at[0] if k > 5 else src, dst, sem.at[k])
+        for k, (src, dst) in enumerate(zip(hbm, vmem))
+    ]
+    for copy in copies:
+        copy.start()
+    pair, mask, chain, bias, in_gain, out_gain, w_in, w_gate = vmem
     row = 2 * lax.axis_index("g") + lax.axis_index("h")
     col = lax.axis_index("q")
     res = lax.broadcasted_iota(jnp.int32, (256, POS), 0)
     pos = lax.broadcasted_iota(jnp.int32, (256, POS), 1)
+    in_row = (res == row * 16 + pos // 16).astype(F32)
+    in_col = (res == col * 16 + pos % 16).astype(F32)
+    for copy in copies:
+        copy.wait()
     both = jnp.concatenate(
         [
             jnp.broadcast_to(mask[...].astype(F32), (8, 256)),
@@ -156,30 +169,32 @@
         ],
         axis=0,
     )
-    of_row = dot(both, (res == row * 16 + pos // 16).astype(F32), 1, 0)
-    of_col = dot(both, (res == col * 16 + pos % 16).astype(F32), 1, 0)
+    of_row = dot(both, in_row, 1, 0)
+    of_col = dot(both, in_col, 1, 0)
     m8 = of_row[0:8] * of_col[0:8]
     m_ref[...] = m8
+    gain_ref[0:2, :] = in_gain[...]
+    gain_ref[2:4, :] = out_gain[...]
     same = (of_row[8:9] == of_col[8:9]).astype(F32)
     z = pair[...].astype(F32).T + same * column(bias[...])
     z_ref[...] = z
-    prepare(z, column(in_gain[0:1]), w_in[0], w_gate[0], m8[0:1], n_ref, g_ref, send, send_ref)
-
-
-def middle_kernel(x_in, z0, g0, m, in_gain, out_gain, w_in, w_gate, w_out, z_ref, y_ref, n_ref, g_ref, send_ref, xs, send):
+    prepare(z, column(in_gain[0:1]), w_in[...], w_gate[...], m8[0:1], n_ref, g_ref, send, send_ref)
+
+
+def middle_kernel(x_in, z0, g0, m, gains, w_in, w_gate, w_out, z_ref, y_ref, n_ref, g_ref, send_ref, xs, send):
     xs[...] = x_in[...].astype(F32)
     hat, _ = normalise(messages_to_channels(xs, 0, 2))
-    y = dot(w_out[0], hat * column(out_gain[0:1]), 0, 0)
+    y = dot(w_out[0], hat * column(gains[2:3]), 0, 0)
     y_ref[...] = y
     z = z0[...] + g0[...] * y
     z_ref[...] = z
-    prepare(z, column(in_gain[1:2]), w_in[1], w_gate[1], m[0:1], n_ref, g_ref, send, send_ref)
-
-
-def turn_kernel(x_in, z1, g1, n1, cot_in, out_gain, w_out, new_ref, cot_ref, dpg_ref, gw_ref, send_ref, xs, send):
+    prepare(z, column(gains[1:2]), w_in[1], w_gate[1], m[0:1], n_ref, g_ref, send, send_ref)
+
+
+def turn_kernel(x_in, z1, g1, n1, cot_in, gains, w_out, new_ref, cot_ref, dpg_ref, gw_ref, send_ref, xs, send):
     xs[...] = x_in[...].astype(F32)
     x = messages_to_channels(xs, 0, 2)
-    gain = column(out_gain[1:2])
+    gain = column(gains[3:4])
     hat, _ = normalise(x)
     y = dot(w_out[1], hat * gain, 0, 0)
     g = g1[...]
@@ -195,10 +210,10 @@
     send_ref[...] = send[...].astype(BF16)
 
 
-def back_kernel(gab, n1, z1, m, dpg1, cot, gw1, x_in, g0, y0, n0, in_gain, out_gain, w_in, w_gate, w_out, dz_ref, dpg_ref, send_ref, rs, dp, xs, send):
+def back_kernel(gab, n1, z1, m, dpg1, cot, gw1, x_in, g0, y0, n0, gains, w_in, w_gate, w_out, dz_ref, dpg_ref, send_ref, mine_ref, other_ref, rs, dp, xs, send):
     rs[...] = gab[...].astype(F32)
     dz = cot[...] + prepare_back(
-        rs, z1[...], n1[...], column(in_gain[1:2]), w_in[1], w_gate[1], m[0:1], dpg1[...], dp
+        rs, 4, z1[...], n1[...], column(gains[1:2]), w_in[1], w_gate[1], m[0:1], dpg1[...], dp
     )
     dz_ref[...] = dz
     w1 = [dot(n1[...], dp[128 * e : 128 * (e + 1), :], 1, 1) for e in range(4)]
@@ -207,27 +222,34 @@
     dpg_ref[...] = dpg
     xs[...] = x_in[...].astype(F32)
     gx, gwo = finish_back(
-        messages_to_channels(xs, 0, 2), dz * g, column(out_gain[0:1]), w_out[0]
+        messages_to_channels(xs, 0, 2), dz * g, column(gains[2:3]), w_out[0]
     )
     gwg = dot(n0[...], dpg, 1, 1)
-    channels_to_messages(gx, send, 0, 6)
-    parts = w1 + [gw1[0:128, :], gw1[128:256, :], gwg, gwo]
-    for k, part in enumerate(parts):
-        send[pl.ds((k % 2) * 128 * 6 + 2 + k // 2, 128, stride=6), :] = part
-    send_ref[...] = send[...].astype(BF16)
-
-
-def end_kernel(gab, n0, z0, m, dpg0, dz1, in_gain, w_in, w_gate, grad_ref, send_ref, rs, dp, send):
+    channels_to_messages(gx, send, 0, 2)
+    send_ref[...] = send[...].astype(BF16)
+    h = lax.axis_index("h")
+    late = [gw1[0:128, :], gw1[128:256, :], gwg, gwo]
+    for k in range(4):
+        block = slice(128 * k, 128 * (k + 1))
+        mine_ref[block, :] = jnp.where(h == 0, w1[k], late[k])
+        other_ref[block, :] = jnp.where(h == 0, late[k], w1[k]).astype(BF16)
+
+
+def end_kernel(gab, n0, z0, m, dpg0, dz1, gains, w_in, w_gate, grad_ref, send_ref, sum_ref, rs, dp, send):
     rs[...] = gab[...].astype(F32)
     dz = dz1[...] + prepare_back(
-        rs, z0[...], n0[...], column(in_gain[0:1]), w_in[0], w_gate[0], m[0:1], dpg0[...], dp
+        rs, 8, z0[...], n0[...], column(gains[0:1]), w_in[0], w_gate[0], m[0:1], dpg0[...], dp
     )
     grad_ref[...] = dz.T
     for e in range(4):
-        send[pl.ds((e % 2) * 256 + e // 2, 128, stride=2), :] = dot(
-            n0[...], dp[128 * e : 128 * (e + 1), :], 1, 1
-        )
-    send_ref[...] = send[...].astype(BF16)
+        part = dot(n0[...], dp[128 * e : 128 * (e + 1), :], 1, 1)
+        h, k = e // 2, e % 2
+        for g in range(8):
+            send[pl.ds((g * 32 + h * 16) * 2 + k, 16, stride=2), :] = part[g * 16 : (g + 1) * 16]
+    send_ref[...] = send[...].astype(BF16)
+    sum_ref[...] = jnp.zeros((8, 128), F32)
+    for k in range(4):
+        sum_ref[k : k + 1, :] = jnp.sum(rs[pl.ds(4 + k, CH, stride=8), :], axis=0, keepdims=True)
 
 
 def sum_kernel(recv, others, send_ref, rs, send):
@@ -237,21 +259,27 @@
             total = jnp.sum(rs[pl.ds(k, 256, stride=2), :], axis=0, keepdims=True)
         else:
             total = others[k - 2 : k - 1, :]
-        send[pl.ds(k, 256, stride=6), :] = jnp.broadcast_to(total, (256, 128))
-    send_ref[...] = send[...].astype(BF16)
-
-
-def place_kernel(recv, in_ref, gate_ref, out_ref, rs):
-    rs[...] = recv[...].astype(F32)
-    rows = [rs[pl.ds(k, 256, stride=6), :] for k in range(6)]
-    for u, base in ((0, 0), (1, 2)):
-        for e in range(4):
-            in_ref[u, :, 128 * e : 128 * (e + 1)] = rows[base + e // 2][
-                128 * (e % 2) : 128 * (e % 2) + 128
-            ]
-    for u, k in ((0, 5), (1, 4)):
-        gate_ref[u] = rows[k][0:128]
-        out_ref[u] = rows[k][128:256]
+        send[pl.ds(k, CH, stride=6), :] = jnp.broadcast_to(total, (CH, 128))
+    send_ref[...] = send[...].astype(BF16)
+
+
+def place_kernel(mine, other, in_ref, gate_ref, out_ref, rs):
+    h = lax.axis_index("h")
+    here, there = mine[...].astype(F32), other[...].astype(F32)
+    rs[0] = jnp.where(h == 0, here, there)
+    rs[1] = jnp.where(h == 0, there, here)
+
+    def block(core, k):
+        return rs[core, pl.ds(k, CH, stride=6), :]
+
+    for e in range(4):
+        lanes = slice(128 * e, 128 * (e + 1))
+        in_ref[0, :, lanes] = block(e // 2, e % 2)
+        in_ref[1, :, lanes] = block(0, 2 + e)
+    gate_ref[1] = block(1, 2)
+    out_ref[1] = block(1, 3)
+    gate_ref[0] = block(1, 4)
+    out_ref[0] = block(1, 5)
 
 
 def product_kernel(incoming, recv, a_ref, b_ref, send_ref, rs, mat, res, send):
@@ -271,48 +299,52 @@
     send_ref[...] = send[...].astype(BF16)
 
 
-def product_back_kernel(incoming, w, recv, a_in, b_in, *refs):
-    if w > 2:
-        send_ref, sum_ref, rs, mat, res, send = refs
+def product_back_kernel(incoming, recv, a_in, b_in, *refs):
+    if incoming:
+        w = 4
+        send_ref, rs, mat, res, send = refs
     else:
-        send_ref, rs, mat, res, send = refs
+        w = 8
+        mine, other, send_ref, rs, mat, res, send = refs
+        weights = mine[...] + other[...].astype(F32)
+        for k in range(4):
+            send[pl.ds(4 + k, CH, stride=w), :] = weights[128 * k : 128 * (k + 1)]
     rs[...] = recv[...].astype(F32)
-    messages_to_matrix(rs, 0, w, mat)
+    messages_to_matrix(rs, 0, 2, mat)
     gx = get(mat).astype(BF16)
     if incoming:
         put(mat, b_in[...].astype(F32))
         put(res, dot(my_rows(mat), gx, 1, 1))
     else:
         put(res, dot(my_rows(mat), b_in[...], 1, 0))
-    half_to_messages(res, send, 0, 4)
+    half_to_messages(res, send, 0, w)
     if incoming:
         put(mat, a_in[...].astype(F32))
         put(res, dot(my_rows(mat), gx, 1, 0))
     else:
         put(mat, dot(gx, a_in[...], 0, 0))
         put(res, my_rows(mat))
-    half_to_messages(res, send, 2, 4)
-    send_ref[...] = send[...].astype(BF16)
-    if w > 2:
-        sum_ref[...] = jnp.zeros((8, 128), F32)
-        for k in range(2, w):
-            sum_ref[k - 2 : k - 1, :] = jnp.sum(
-                rs[pl.ds(k, 256, stride=w), :], axis=0, keepdims=True
-            )
-
-
-def call(kernel, name, outs, scratch, *args):
+    half_to_messages(res, send, 2, w)
+    send_ref[...] = send[...].astype(BF16)
+
+
+def call(kernel, name, outs, scratch, *args, **kwargs):
     return pl.pallas_call(
         kernel,
         name=name,
         out_shape=[jax.ShapeDtypeStruct(s, d) for s, d in outs],
-        scratch_shapes=[pltpu.VMEM(s, d) for s, d in scratch],
+        scratch_shapes=[s if not isinstance(s, tuple) else pltpu.VMEM(*s) for s in scratch],
         compiler_params=pltpu.CompilerParams(vmem_limit_bytes=24 * 1024 * 1024),
+        **kwargs,
     )(*args)
 
 
 def exchange(value, axes):
     return lax.all_to_all(value, axes, 0, 0, tiled=True)
+
+
+def swap_cores(value):
+    return lax.ppermute(value, "h", [(0, 1), (1, 0)])
 
 
 def shards(pair, pair_cot, mask, chain_ids, chain_bias, w_in, w_gate, w_out, in_gain, out_gain):
@@ -326,9 +358,12 @@
     def rows(n, dtype=F32):
         return ((n, 128), dtype)
 
-    z0, n0, g0, m, send = call(
-        start_kernel, "start", [field, field16, field, ((8, POS), F32), rows(1024, BF16)], [rows(1024)],
-        pair, mask, chain, bias, in_gain, w_in, w_gate,
+    operands = (pair, mask, chain, bias, in_gain, out_gain, w_in, w_gate)
+    z0, n0, g0, m, gains, send = call(
+        start_kernel, "start", [field, field16, field, ((8, POS), F32), rows(4), rows(1024, BF16)],
+        [(v.shape[1:] if k > 5 else v.shape, v.dtype) for k, v in enumerate(operands)]
+        + [rows(1024), pltpu.SemaphoreType.DMA((8,))],
+        *operands, in_specs=[pl.BlockSpec(memory_space=pltpu.HBM)] * 8,
     )
     a0, b0, send = call(
         functools.partial(product_kernel, False), "outgoing", [matrix16, matrix16, rows(256, BF16)],
@@ -337,7 +372,7 @@
     x0 = exchange(send, CHIPS)
     z1, y0, n1, g1, send = call(
         middle_kernel, "middle", [field, field, field16, field, rows(1024, BF16)], [rows(256), rows(1024)],
-        x0, z0, g0, m, in_gain, out_gain, w_in, w_gate, w_out,
+        x0, z0, g0, m, gains, w_in, w_gate, w_out,
     )
     a1, b1, send = call(
         functools.partial(product_kernel, True), "incoming", [matrix16, matrix16, rows(256, BF16)],
@@ -345,32 +380,35 @@
     )
     new_pair, cot, dpg1, gw1, send = call(
         turn_kernel, "turn", [rows(POS, BF16), field, field16, rows(256), rows(512, BF16)],
-        [rows(256), rows(512)], exchange(send, CHIPS), z1, g1, n1, cot_in, out_gain, w_out,
+        [rows(256), rows(512)], exchange(send, CHIPS), z1, g1, n1, cot_in, gains, w_out,
     )
     (send,) = call(
-        functools.partial(product_back_kernel, True, 2), "incoming_back", [rows(512, BF16)],
+        functools.partial(product_back_kernel, True), "incoming_back", [rows(512, BF16)],
         [rows(512), matrix, part, rows(512)], exchange(send, ALL), a1, b1,
     )
-    dz1, dpg0, send = call(
-        back_kernel, "back", [field, field16, rows(1536, BF16)],
-        [rows(512), ((512, POS), BF16), rows(256), rows(1536)],
-        exchange(send, CHIPS), n1, z1, m, dpg1, cot, gw1, x0, g0, y0, n0, in_gain, out_gain, w_in, w_gate, w_out,
-    )
-    send, sums = call(
-        functools.partial(product_back_kernel, False, 6), "outgoing_back", [rows(512, BF16), rows(8)],
-        [rows(1536), matrix, part, rows(512)], exchange(send, ALL), a0, b0,
-    )
-    pair_grad, send = call(
-        end_kernel, "end", [rows(POS), rows(512, BF16)], [rows(512), ((512, POS), BF16), rows(512)],
-        exchange(send, CHIPS), n0, z0, m, dpg0, dz1, in_gain, w_in, w_gate,
-    )
+    dz1, dpg0, send, mine, other = call(
+        back_kernel, "back", [field, field16, rows(512, BF16), rows(512), rows(512, BF16)],
+        [rows(512), ((512, POS), BF16), rows(256), rows(512)],
+        exchange(send, CHIPS), n1, z1, m, dpg1, cot, gw1, x0, g0, y0, n0, gains, w_in, w_gate, w_out,
+    )
+    other = swap_cores(other)
     (send,) = call(
-        sum_kernel, "sum", [rows(1536, BF16)], [rows(512), rows(1536)], exchange(send, ALL), sums
-    )
+        functools.partial(product_back_kernel, False), "outgoing_back", [rows(1024, BF16)],
+        [rows(512), matrix, part, rows(1024)], exchange(send, ALL), a0, b0, mine, other,
+    )
+    pair_grad, send, sums = call(
+        end_kernel, "end", [rows(POS), rows(512, BF16), rows(8)],
+        [rows(1024), ((512, POS), BF16), rows(512)],
+        exchange(send, CHIPS), n0, z0, m, dpg0, dz1, gains, w_in, w_gate,
+    )
+    (send,) = call(
+        sum_kernel, "sum", [rows(768, BF16)], [rows(512), rows(768)], exchange(send, ALL), sums
+    )
+    mine = exchange(send, CHIPS)
     in_grad, gate_grad, out_grad = call(
         place_kernel, "place",
-        [((2, 128, 512), F32), ((2, 128, 128), F32), ((2, 128, 128), F32)], [rows(1536)],
-        exchange(send, ALL),
+        [((2, 128, 512), F32), ((2, 128, 128), F32), ((2, 128, 128), F32)], [((2, 768, 128), F32)],
+        mine, swap_cores(mine),
     )
     return (new_pair.reshape(block), pair_grad.reshape(block), in_grad, gate_grad, out_grad)
 

time: 231 us -> 221 us (0.957)
  blocking collectives: 215 us -> 181 us
  starting transfers between devices: 0 us -> 12.5 us
  waiting for transfers between devices: 0 us -> 11.8 us
    all_to_all x10 -> x9, blocking collectives: 215 us -> 181 us  [exchange(): return lax.all_to_all(value, axes, 0, 0, tiled=True)]
    all_to_all x0 -> x1, waiting for transfers between devices: none -> 9.78 us  [exchange(): return lax.all_to_all(value, axes, 0, 0, tiled=True)]
    all_to_all x0 -> x1, starting transfers between devices: none -> 7.14 us  [exchange(): return lax.all_to_all(value, axes, 0, 0, tiled=True)]
    ppermute x0 -> x2, starting transfers between devices: none -> 5.36 us  [swap_cores(): return lax.ppermute(value, 'h', [(0, 1), (1, 0)])]
  transfers between devices with their start and end apart: 0 -> 3, of which waited for: 0 -> 3; matrix products, arithmetic and copies ran while one was open for 0% -> 0% of each run, Pallas kernels for 0% -> 0%
where the time goes in v2:
time: 221 us
  blocking collectives  181 us (82%)
  starting transfers between devices  12.5 us (6%)
  waiting for transfers between devices  11.8 us (5%)
  Pallas kernels  10.8 us (5%)
  local copies, waits for them, and re-layouts  3.48 us (2%)
    all_to_all x9, blocking collectives, exchange(): return lax.all_to_all(value, axes, 0, 0, tiled=True)  181 us
    pallas_call x11, Pallas kernels, call(): pl.pallas_call(kernel, name=name, out_shape=[jax.ShapeDtypeStruct(s, d) f...  10.8 us
    all_to_all x1, waiting for transfers between devices, exchange(): return lax.all_to_all(value, axes, 0, 0, tiled=True)  9.78 us
    all_to_all x1, starting transfers between devices, exchange(): return lax.all_to_all(value, axes, 0, 0, tiled=True)  7.14 us
    ppermute x2, starting transfers between devices, swap_cores(): return lax.ppermute(value, 'h', [(0, 1), (1, 0)])  5.36 us
  transfers between devices with their start and end apart: 3, of which 3 were waited for; matrix products, arithmetic and copies ran while one was open for 0% of the time, Pallas kernels for 0%

profile of v2, /device:TPU:1, one launch (start us, length us, event | category | flops | bytes accessed | tf_op | source)
XLA Modules:
  0.0 220.7 jit_solution(260571875437001712)
XLA Ops:
  1.4 0.9 copy-done
  4.9 31.1 %all_to_all.110 = bf16[256,4,128]{2,1,0:T(4,128)(2,1)S(1)} all-to-all(bf16[256,4,128]{2,1,0:T(4,128)(2,1)S(1)} %bitcast.36), channel_id=1, replica_groups=mesh['g'=8,'h'=2,'q'=16] {'g','h','q'}, dimensions={0} | all-to-all | bytes 524288 | tf_op jit(solution)/shard_map/all_to_all | solution.py:343
  36.1 1.2 outgoing.1
  37.2 16.5 %all_to_all.111 = bf16[128,2,128]{2,1,0:T(2,128)(2,1)S(1)} all-to-all(bf16[128,2,128]{2,1,0:T(2,128)(2,1)S(1)} %bitcast.42), channel_id=1, replica_groups=mesh['g'=8,'h'=2,'q'=16] {'g','q'}, dimensions={0} | all-to-all | bytes 131072 | tf_op jit(solution)/shard_map/all_to_all | solution.py:343
  54.3 22.7 %all_to_all.112 = bf16[256,4,128]{2,1,0:T(4,128)(2,1)S(1)} all-to-all(bf16[256,4,128]{2,1,0:T(4,128)(2,1)S(1)} %bitcast.37), channel_id=1, replica_groups=mesh['g'=8,'h'=2,'q'=16] {'g','h','q'}, dimensions={0} | all-to-all | bytes 524288 | tf_op jit(solution)/shard_map/all_to_all | solution.py:343
  77.0 1.3 incoming.1
  78.3 16.5 %all_to_all.113 = bf16[128,2,128]{2,1,0:T(2,128)(2,1)S(1)} all-to-all(bf16[128,2,128]{2,1,0:T(2,128)(2,1)S(1)} %bitcast.43), channel_id=1, replica_groups=mesh['g'=8,'h'=2,'q'=16] {'g','q'}, dimensions={0} | all-to-all | bytes 131072 | tf_op jit(solution)/shard_map/all_to_all | solution.py:343
  94.8 1.0 turn.1
  95.8 20.1 %all_to_all.114 = bf16[256,2,128]{2,1,0:T(2,128)(2,1)S(1)} all-to-all(bf16[256,2,128]{2,1,0:T(2,128)(2,1)S(1)} %bitcast.40), channel_id=1, replica_groups=mesh['g'=8,'h'=2,'q'=16] {'g','h','q'}, dimensions={0} | all-to-all | bytes 262144 | tf_op jit(solution)/shard_map/all_to_all | solution.py:343
  115.8 1.0 incoming_back.1
  116.9 16.7 %all_to_all.115 = bf16[128,4,128]{2,1,0:T(4,128)(2,1)S(1)} all-to-all(bf16[128,4,128]{2,1,0:T(4,128)(2,1)S(1)} %bitcast.32), channel_id=1, replica_groups=mesh['g'=8,'h'=2,'q'=16] {'g','q'}, dimensions={0} | all-to-all | bytes 262144 | tf_op jit(solution)/shard_map/all_to_all | solution.py:343
  133.6 1.4 back.1
  135.0 7.1 %all-to-all-start.6 = ((bf16[256,2,128]{2,1,0:T(2,128)(2,1)}), bf16[256,2,128]{2,1,0:T(2,128)(2,1)S(1)}, u32[]{:S(2)}, u32[]{:S(2)}) async-start(bf16[256,2,128]{2,1,0:T(2,128)(2,1)} %bitcast.18), calls=%async_computation.6 | async-start | bytes 262144 | tf_op jit(solution)/shard_map/all_to_all | solution.py:343
  142.2 2.4 %collective-permute-start = (bf16[512,128]{1,0:T(8,128)(2,1)S(1)}, bf16[512,128]{1,0:T(8,128)(2,1)S(1)}, u32[]{:S(2)}, u32[]{:S(2)}) collective-permute-start(bf16[512,128]{1,0:T(8,128)(2,1)S(1)} %get-tuple-element.62), channel_id=1, source_target_pairs={{0,16},{16,0},{1,17},{17,1},{2,18},{18,2},{3,19},{19,3},{4,20},{20... | collective-permute-start | bytes 393224 | tf_op jit(solution)/shard_map/ppermute | solution.py:347
  144.6 1.0 collective-permute-done.refs_1_
  145.5 9.8 %all-to-all-done.6 = bf16[256,2,128]{2,1,0:T(2,128)(2,1)S(1)} async-done(((bf16[256,2,128]{2,1,0:T(2,128)(2,1)}), bf16[256,2,128]{2,1,0:T(2,128)(2,1)S(1)}, u32[]{:S(2)}, u32[]{:S(2)}) %all-to-all-start.6) | async-done | bytes 131104 | tf_op jit(solution)/shard_map/all_to_all | solution.py:343
  155.3 1.0 outgoing_back.1
  156.4 18.5 %all_to_all.116 = bf16[128,8,128]{2,1,0:T(8,128)(2,1)S(1)} all-to-all(bf16[128,8,128]{2,1,0:T(8,128)(2,1)S(1)} %bitcast.28), channel_id=1, replica_groups=mesh['g'=8,'h'=2,'q'=16] {'g','q'}, dimensions={0} | all-to-all | bytes 524288 | tf_op jit(solution)/shard_map/all_to_all | solution.py:343
  174.8 1.3 end.1
  176.1 20.8 %all_to_all.117 = bf16[256,2,128]{2,1,0:T(2,128)(2,1)S(1)} all-to-all(bf16[256,2,128]{2,1,0:T(2,128)(2,1)S(1)} %bitcast.39), channel_id=1, replica_groups=mesh['g'=8,'h'=2,'q'=16] {'g','h','q'}, dimensions={0} | all-to-all | bytes 262144 | tf_op jit(solution)/shard_map/all_to_all | solution.py:343
  197.1 18.5 %all_to_all.118 = bf16[128,6,128]{2,1,0:T(8,128)(2,1)S(1)} all-to-all(bf16[128,6,128]{2,1,0:T(8,128)(2,1)S(1)} %all_to_all.97), channel_id=1, replica_groups=mesh['g'=8,'h'=2,'q'=16] {'g','q'}, dimensions={0} | all-to-all | bytes 393216 | tf_op jit(solution)/shard_map/all_to_all | solution.py:343
  215.6 3.0 %collective-permute-start.1 = (bf16[768,128]{1,0:T(8,128)(2,1)S(1)}, bf16[768,128]{1,0:T(8,128)(2,1)S(1)}, u32[]{:S(2)}, u32[]{:S(2)}) collective-permute-start(bf16[768,128]{1,0:T(8,128)(2,1)S(1)} %all_to_all.99.mine), channel_id=1, source_target_pairs={{0,16},{16,0},{1,17},{17,1},{2,18},{18,2},{3,19},{19,3},{4,20},{20... | collective-permute-start | bytes 589832 | tf_op jit(solution)/shard_map/ppermute | solution.py:347
  218.6 1.1 collective-permute-done.1.other
  219.7 1.0 place.1
  (28 shorter events, 4.1 us)
Async XLA Ops:
  0.6 0.7 copy-start.10
  0.6 0.7 copy-start.8
  0.7 0.7 copy-start.9
  0.7 0.7 copy-start.7
  0.7 0.7 copy-start.11
  1.4 1.0 copy-start
  2.3 0.8 copy-start.2
  3.2 0.8 copy-start.5
  36.1 17.6 %copy-start.1 = (bf16[2,128,512]{2,1,0:T(8,128)(2,1)S(1)}, bf16[2,128,512]{2,1,0:T(8,128)(2,1)}, u32[]{:S(2)}) copy-start(bf16[2,128,512]{2,1,0:T(8,128)(2,1)} %w_in.5) | copy-start | bytes 786436
  37.2 16.5 %copy-start.3 = (bf16[2,128,128]{2,1,0:T(8,128)(2,1)S(1)}, bf16[2,128,128]{2,1,0:T(8,128)(2,1)}, u32[]{:S(2)}) copy-start(bf16[2,128,128]{2,1,0:T(8,128)(2,1)} %w_gate.5) | copy-start | bytes 196612
  37.2 16.5 %copy-start.4 = (bf16[2,128,128]{2,1,0:T(8,128)(2,1)S(1)}, bf16[2,128,128]{2,1,0:T(8,128)(2,1)}, u32[]{:S(2)}) copy-start(bf16[2,128,128]{2,1,0:T(8,128)(2,1)} %w_out.5) | copy-start | bytes 196612
  78.3 16.5 %copy-start.6 = (bf16[16,16,128]{2,1,0:T(8,128)(2,1)S(1)}, bf16[16,16,128]{2,1,0:T(8,128)(2,1)}, u32[]{:S(2)}) copy-start(bf16[16,16,128]{2,1,0:T(8,128)(2,1)} %param.11) | copy-start | bytes 196612
  135.0 20.3 %all-to-all-start.6 = ((bf16[256,2,128]{2,1,0:T(2,128)(2,1)}), bf16[256,2,128]{2,1,0:T(2,128)(2,1)S(1)}, u32[]{:S(2)}, u32[]{:S(2)}) async-start(bf16[256,2,128]{2,1,0:T(2,128)(2,1)} %bitcast.18), calls=%async_computation.6 | async-start | bytes 262144 | tf_op jit(solution)/shard_map/all_to_all | solution.py:343
  142.2 3.4 %collective-permute-start = (bf16[512,128]{1,0:T(8,128)(2,1)S(1)}, bf16[512,128]{1,0:T(8,128)(2,1)S(1)}, u32[]{:S(2)}, u32[]{:S(2)}) collective-permute-start(bf16[512,128]{1,0:T(8,128)(2,1)S(1)} %get-tuple-element.62), channel_id=1, source_target_pairs={{0,16},{16,0},{1,17},{17,1},{2,18},{18,2},{3,19},{19,3},{4,20},{20... | collective-permute-start | bytes 393224 | tf_op jit(solution)/shard_map/ppermute | solution.py:347
  215.6 4.1 %collective-permute-start.1 = (bf16[768,128]{1,0:T(8,128)(2,1)S(1)}, bf16[768,128]{1,0:T(8,128)(2,1)S(1)}, u32[]{:S(2)}, u32[]{:S(2)}) collective-permute-start(bf16[768,128]{1,0:T(8,128)(2,1)S(1)} %all_to_all.99.mine), channel_id=1, source_target_pairs={{0,16},{16,0},{1,17},{17,1},{2,18},{18,2},{3,19},{19,3},{4,20},{20... | collective-permute-start | bytes 589832 | tf_op jit(solution)/shard_map/ppermute | solution.py:347

commit v3 on v2

--- a/solution.py
+++ b/solution.py
@@ -12,8 +12,10 @@
 POS = 256
 CH = 128
 EPS = 1e-05
-CHIPS = ("g", "q")
-ALL = ("g", "h", "q")
+SIZES = {"y": 4, "zl": 2, "h": 2, "zh": 4, "x": 4}
+CHIPS = ("y", "zl", "zh", "x")
+PLANE = ("y", "h", "x")
+LINE = ("zl", "zh")
 
 
 def dot(a, b, ca, cb):
@@ -36,14 +38,19 @@
     return tiles
 
 
-def messages_to_matrix(src, off, w, dst):
+def messages_to_matrix(mine, other, off, w, dst):
+    first = lax.axis_index("h") == 0
     for half in range(2):
         for qh in range(2):
-            tiles = [
-                src[pl.ds((qh * 8 + t) * w + off + half, 16, stride=16 * w), :] for t in range(8)
-            ]
-            for t, tile in enumerate(swap_blocks(tiles)):
-                dst[qh, pl.ds(half * 8 + t, 16, stride=16), :] = tile
+            even, odd = [], []
+            for t in range(8):
+                rows = pl.ds((qh * 8 + t) * w + off + half, 8, stride=16 * w)
+                here, there = mine[rows, :], other[rows, :]
+                even.append(jnp.where(first, here, there))
+                odd.append(jnp.where(first, there, here))
+            for core, tiles in enumerate((even, odd)):
+                for t, tile in enumerate(swap_blocks(tiles)):
+                    dst[qh, pl.ds(core * 16 + half * 8 + t, 8, stride=32), :] = tile
 
 
 def half_to_messages(src, dst, off, w):
@@ -78,12 +85,8 @@
 
 
 def channels_to_messages(v, dst, off, w):
-    for g in range(8):
-        for h in range(2):
-            for half in range(2):
-                dst[pl.ds((g * 32 + h * 16) * w + off + half, 16, stride=w), :] = v[
-                    g * 16 : (g + 1) * 16, half * 128 : (half + 1) * 128
-                ]
+    for half in range(2):
+        dst[pl.ds(off + half, CH, stride=w), :] = v[:, half * 128 : (half + 1) * 128]
 
 
 def messages_to_channels(src, off, w):
@@ -124,10 +127,10 @@
     send_ref[...] = send[...].astype(BF16)
 
 
-def prepare_back(recv, w, z, normed, gain, w_in, w_gate, m, dpg, dp):
+def prepare_back(recv, z, normed, gain, w_in, w_gate, m, dpg, dp):
     p = dot(w_in, normed, 0, 0)
     for k in range(2):
-        cot = messages_to_channels(recv, 2 * k, w) * m
+        cot = messages_to_channels(recv, 2 * k, 4) * m
         s = jax.nn.sigmoid(p[256 * k : 256 * k + 128])
         v = p[256 * k + 128 : 256 * k + 256]
         dp[256 * k : 256 * k + 128, :] = (cot * v * s * (1.0 - s)).astype(BF16)
@@ -154,8 +157,8 @@
     for copy in copies:
         copy.start()
     pair, mask, chain, bias, in_gain, out_gain, w_in, w_gate = vmem
-    row = 2 * lax.axis_index("g") + lax.axis_index("h")
-    col = lax.axis_index("q")
+    row = (lax.axis_index("y") * 2 + lax.axis_index("zl")) * 2 + lax.axis_index("h")
+    col = lax.axis_index("zh") * 4 + lax.axis_index("x")
     res = lax.broadcasted_iota(jnp.int32, (256, POS), 0)
     pos = lax.broadcasted_iota(jnp.int32, (256, POS), 1)
     in_row = (res == row * 16 + pos // 16).astype(F32)
@@ -210,10 +213,10 @@
     send_ref[...] = send[...].astype(BF16)
 
 
-def back_kernel(gab, n1, z1, m, dpg1, cot, gw1, x_in, g0, y0, n0, gains, w_in, w_gate, w_out, dz_ref, dpg_ref, send_ref, mine_ref, other_ref, rs, dp, xs, send):
+def back_kernel(gab, n1, z1, m, dpg1, cot, gw1, x_in, g0, y0, n0, gains, w_in, w_gate, w_out, dz_ref, dpg_ref, send_ref, early_ref, rs, dp, xs, send):
     rs[...] = gab[...].astype(F32)
     dz = cot[...] + prepare_back(
-        rs, 4, z1[...], n1[...], column(gains[1:2]), w_in[1], w_gate[1], m[0:1], dpg1[...], dp
+        rs, z1[...], n1[...], column(gains[1:2]), w_in[1], w_gate[1], m[0:1], dpg1[...], dp
     )
     dz_ref[...] = dz
     w1 = [dot(n1[...], dp[128 * e : 128 * (e + 1), :], 1, 1) for e in range(4)]
@@ -227,67 +230,50 @@
     gwg = dot(n0[...], dpg, 1, 1)
     channels_to_messages(gx, send, 0, 2)
     send_ref[...] = send[...].astype(BF16)
-    h = lax.axis_index("h")
-    late = [gw1[0:128, :], gw1[128:256, :], gwg, gwo]
-    for k in range(4):
-        block = slice(128 * k, 128 * (k + 1))
-        mine_ref[block, :] = jnp.where(h == 0, w1[k], late[k])
-        other_ref[block, :] = jnp.where(h == 0, late[k], w1[k]).astype(BF16)
-
-
-def end_kernel(gab, n0, z0, m, dpg0, dz1, gains, w_in, w_gate, grad_ref, send_ref, sum_ref, rs, dp, send):
+    for k, part in enumerate(w1 + [gw1[0:128, :], gw1[128:256, :], gwg, gwo]):
+        early_ref[128 * k : 128 * (k + 1), :] = part.astype(BF16)
+
+
+def end_kernel(gab, n0, z0, m, dpg0, dz1, gains, w_in, w_gate, early, grad_ref, send_ref, rs, dp):
     rs[...] = gab[...].astype(F32)
     dz = dz1[...] + prepare_back(
-        rs, 8, z0[...], n0[...], column(gains[0:1]), w_in[0], w_gate[0], m[0:1], dpg0[...], dp
+        rs, z0[...], n0[...], column(gains[0:1]), w_in[0], w_gate[0], m[0:1], dpg0[...], dp
     )
     grad_ref[...] = dz.T
     for e in range(4):
         part = dot(n0[...], dp[128 * e : 128 * (e + 1), :], 1, 1)
-        h, k = e // 2, e % 2
-        for g in range(8):
-            send[pl.ds((g * 32 + h * 16) * 2 + k, 16, stride=2), :] = part[g * 16 : (g + 1) * 16]
-    send_ref[...] = send[...].astype(BF16)
-    sum_ref[...] = jnp.zeros((8, 128), F32)
-    for k in range(4):
-        sum_ref[k : k + 1, :] = jnp.sum(rs[pl.ds(4 + k, CH, stride=8), :], axis=0, keepdims=True)
-
-
-def sum_kernel(recv, others, send_ref, rs, send):
-    rs[...] = recv[...].astype(F32)
-    for k in range(6):
-        if k < 2:
-            total = jnp.sum(rs[pl.ds(k, 256, stride=2), :], axis=0, keepdims=True)
-        else:
-            total = others[k - 2 : k - 1, :]
-        send[pl.ds(k, CH, stride=6), :] = jnp.broadcast_to(total, (CH, 128))
-    send_ref[...] = send[...].astype(BF16)
-
-
-def place_kernel(mine, other, in_ref, gate_ref, out_ref, rs):
-    h = lax.axis_index("h")
-    here, there = mine[...].astype(F32), other[...].astype(F32)
-    rs[0] = jnp.where(h == 0, here, there)
-    rs[1] = jnp.where(h == 0, there, here)
-
-    def block(core, k):
-        return rs[core, pl.ds(k, CH, stride=6), :]
+        send_ref[128 * e : 128 * (e + 1), :] = part.astype(BF16)
+    send_ref[512:1536, :] = early[...]
+
+
+def sum_kernel(recv, send_ref):
+    total = recv[0:48, :].astype(F32)
+    for k in range(1, recv.shape[0] // 48):
+        total = total + recv[48 * k : 48 * (k + 1), :].astype(F32)
+    total = total.astype(BF16)
+    for k in range(send_ref.shape[0] // 48):
+        send_ref[48 * k : 48 * (k + 1), :] = total
+
+
+def place_kernel(recv, in_ref, gate_ref, out_ref):
+    def block(k):
+        return recv[128 * k : 128 * (k + 1), :].astype(F32)
 
     for e in range(4):
         lanes = slice(128 * e, 128 * (e + 1))
-        in_ref[0, :, lanes] = block(e // 2, e % 2)
-        in_ref[1, :, lanes] = block(0, 2 + e)
-    gate_ref[1] = block(1, 2)
-    out_ref[1] = block(1, 3)
-    gate_ref[0] = block(1, 4)
-    out_ref[0] = block(1, 5)
-
-
-def product_kernel(incoming, recv, a_ref, b_ref, send_ref, rs, mat, res, send):
-    rs[...] = recv[...].astype(F32)
-    messages_to_matrix(rs, 2, 4, mat)
+        in_ref[0, :, lanes] = block(e)
+        in_ref[1, :, lanes] = block(4 + e)
+    for k, (ref, u) in enumerate(((gate_ref, 1), (out_ref, 1), (gate_ref, 0), (out_ref, 0))):
+        ref[u] = block(8 + k)
+
+
+def product_kernel(incoming, mine, other, a_ref, b_ref, send_ref, ms, os, mat, res, send):
+    ms[...] = mine[...].astype(F32)
+    os[...] = other[...].astype(F32)
+    messages_to_matrix(ms, os, 2, 4, mat)
     b = get(mat).astype(BF16)
     b_ref[...] = b
-    messages_to_matrix(rs, 0, 4, mat)
+    messages_to_matrix(ms, os, 0, 4, mat)
     a = get(mat).astype(BF16)
     a_ref[...] = a
     if incoming:
@@ -299,32 +285,24 @@
     send_ref[...] = send[...].astype(BF16)
 
 
-def product_back_kernel(incoming, recv, a_in, b_in, *refs):
-    if incoming:
-        w = 4
-        send_ref, rs, mat, res, send = refs
-    else:
-        w = 8
-        mine, other, send_ref, rs, mat, res, send = refs
-        weights = mine[...] + other[...].astype(F32)
-        for k in range(4):
-            send[pl.ds(4 + k, CH, stride=w), :] = weights[128 * k : 128 * (k + 1)]
-    rs[...] = recv[...].astype(F32)
-    messages_to_matrix(rs, 0, 2, mat)
+def product_back_kernel(incoming, mine, other, a_in, b_in, send_ref, ms, os, mat, res, send):
+    ms[...] = mine[...].astype(F32)
+    os[...] = other[...].astype(F32)
+    messages_to_matrix(ms, os, 0, 2, mat)
     gx = get(mat).astype(BF16)
     if incoming:
         put(mat, b_in[...].astype(F32))
         put(res, dot(my_rows(mat), gx, 1, 1))
     else:
         put(res, dot(my_rows(mat), b_in[...], 1, 0))
-    half_to_messages(res, send, 0, w)
+    half_to_messages(res, send, 0, 4)
     if incoming:
         put(mat, a_in[...].astype(F32))
         put(res, dot(my_rows(mat), gx, 1, 0))
     else:
         put(mat, dot(gx, a_in[...], 0, 0))
         put(res, my_rows(mat))
-    half_to_messages(res, send, 2, w)
+    half_to_messages(res, send, 2, 4)
     send_ref[...] = send[...].astype(BF16)
 
 
@@ -339,12 +317,17 @@
     )(*args)
 
 
-def exchange(value, axes):
+def exchange(value, axes=CHIPS):
     return lax.all_to_all(value, axes, 0, 0, tiled=True)
 
 
 def swap_cores(value):
     return lax.ppermute(value, "h", [(0, 1), (1, 0)])
+
+
+def exchange_both(value):
+    mine = exchange(value)
+    return mine, swap_cores(mine)
 
 
 def shards(pair, pair_cot, mask, chain_ids, chain_bias, w_in, w_gate, w_out, in_gain, out_gain):
@@ -360,65 +343,60 @@
 
     operands = (pair, mask, chain, bias, in_gain, out_gain, w_in, w_gate)
     z0, n0, g0, m, gains, send = call(
-        start_kernel, "start", [field, field16, field, ((8, POS), F32), rows(4), rows(1024, BF16)],
+        start_kernel, "start", [field, field16, field, ((8, POS), F32), rows(4), rows(512, BF16)],
         [(v.shape[1:] if k > 5 else v.shape, v.dtype) for k, v in enumerate(operands)]
-        + [rows(1024), pltpu.SemaphoreType.DMA((8,))],
+        + [rows(512), pltpu.SemaphoreType.DMA((8,))],
         *operands, in_specs=[pl.BlockSpec(memory_space=pltpu.HBM)] * 8,
     )
     a0, b0, send = call(
         functools.partial(product_kernel, False), "outgoing", [matrix16, matrix16, rows(256, BF16)],
-        [rows(1024), matrix, part, rows(256)], exchange(send, ALL),
-    )
-    x0 = exchange(send, CHIPS)
+        [rows(512), rows(512), matrix, part, rows(256)], *exchange_both(send),
+    )
+    x0 = exchange(send)
     z1, y0, n1, g1, send = call(
-        middle_kernel, "middle", [field, field, field16, field, rows(1024, BF16)], [rows(256), rows(1024)],
+        middle_kernel, "middle", [field, field, field16, field, rows(512, BF16)], [rows(256), rows(512)],
         x0, z0, g0, m, gains, w_in, w_gate, w_out,
     )
     a1, b1, send = call(
         functools.partial(product_kernel, True), "incoming", [matrix16, matrix16, rows(256, BF16)],
-        [rows(1024), matrix, part, rows(256)], exchange(send, ALL),
+        [rows(512), rows(512), matrix, part, rows(256)], *exchange_both(send),
     )
     new_pair, cot, dpg1, gw1, send = call(
-        turn_kernel, "turn", [rows(POS, BF16), field, field16, rows(256), rows(512, BF16)],
-        [rows(256), rows(512)], exchange(send, CHIPS), z1, g1, n1, cot_in, gains, w_out,
+        turn_kernel, "turn", [rows(POS, BF16), field, field16, rows(256), rows(256, BF16)],
+        [rows(256), rows(256)], exchange(send), z1, g1, n1, cot_in, gains, w_out,
     )
     (send,) = call(
         functools.partial(product_back_kernel, True), "incoming_back", [rows(512, BF16)],
-        [rows(512), matrix, part, rows(512)], exchange(send, ALL), a1, b1,
-    )
-    dz1, dpg0, send, mine, other = call(
-        back_kernel, "back", [field, field16, rows(512, BF16), rows(512), rows(512, BF16)],
-        [rows(512), ((512, POS), BF16), rows(256), rows(512)],
-        exchange(send, CHIPS), n1, z1, m, dpg1, cot, gw1, x0, g0, y0, n0, gains, w_in, w_gate, w_out,
-    )
-    other = swap_cores(other)
+        [rows(256), rows(256), matrix, part, rows(512)], *exchange_both(send), a1, b1,
+    )
+    dz1, dpg0, send, early = call(
+        back_kernel, "back", [field, field16, rows(256, BF16), rows(1024, BF16)],
+        [rows(512), ((512, POS), BF16), rows(256), rows(256)],
+        exchange(send), n1, z1, m, dpg1, cot, gw1, x0, g0, y0, n0, gains, w_in, w_gate, w_out,
+    )
     (send,) = call(
-        functools.partial(product_back_kernel, False), "outgoing_back", [rows(1024, BF16)],
-        [rows(512), matrix, part, rows(1024)], exchange(send, ALL), a0, b0, mine, other,
-    )
-    pair_grad, send, sums = call(
-        end_kernel, "end", [rows(POS), rows(512, BF16), rows(8)],
-        [rows(1024), ((512, POS), BF16), rows(512)],
-        exchange(send, CHIPS), n0, z0, m, dpg0, dz1, gains, w_in, w_gate,
-    )
-    (send,) = call(
-        sum_kernel, "sum", [rows(768, BF16)], [rows(512), rows(768)], exchange(send, ALL), sums
-    )
-    mine = exchange(send, CHIPS)
+        functools.partial(product_back_kernel, False), "outgoing_back", [rows(512, BF16)],
+        [rows(256), rows(256), matrix, part, rows(512)], *exchange_both(send), a0, b0,
+    )
+    pair_grad, send = call(
+        end_kernel, "end", [rows(POS), rows(1536, BF16)], [rows(512), ((512, POS), BF16)],
+        exchange(send), n0, z0, m, dpg0, dz1, gains, w_in, w_gate, early,
+    )
+    (send,) = call(sum_kernel, "plane_sum", [rows(384, BF16)], [], exchange(send, PLANE))
+    (send,) = call(sum_kernel, "line_sum", [rows(1536, BF16)], [], exchange(send, LINE))
     in_grad, gate_grad, out_grad = call(
         place_kernel, "place",
-        [((2, 128, 512), F32), ((2, 128, 128), F32), ((2, 128, 128), F32)], [((2, 768, 128), F32)],
-        mine, swap_cores(mine),
+        [((2, 128, 512), F32), ((2, 128, 128), F32), ((2, 128, 128), F32)], [], exchange(send, PLANE),
     )
     return (new_pair.reshape(block), pair_grad.reshape(block), in_grad, gate_grad, out_grad)
 
 
 def solution(mesh):
-    devices = mesh.devices.reshape(8, 2, 16)
-    split = P(("g", "h"), "q", None)
+    devices = mesh.devices.reshape(tuple(SIZES.values()))
+    split = P(("y", "zl", "h"), ("zh", "x"), None)
     return jax.shard_map(
         shards,
-        mesh=Mesh(devices, ALL),
+        mesh=Mesh(devices, tuple(SIZES)),
         in_specs=(split, split) + (P(),) * 8,
         out_specs=(split, split, P(), P(), P()),
         check_vma=False,

time: 221 us -> 212 us (0.959)
  waiting for transfers between devices: 11.8 us -> 3.78 us
  starting transfers between devices: 12.5 us -> 10 us
    all_to_all x1 -> x0, waiting for transfers between devices: 9.78 us -> none  [exchange(): return lax.all_to_all(value, axes, 0, 0, tiled=True)]
    all_to_all x1 -> x0, starting transfers between devices: 7.14 us -> none  [exchange(): return lax.all_to_all(value, axes, 0, 0, tiled=True)]
    ppermute x2 -> x4, starting transfers between devices: 5.36 us -> 10 us  [swap_cores(): return lax.ppermute(value, 'h', [(0, 1), (1, 0)])]
    all_to_all x9 -> x11, blocking collectives: 181 us -> 183 us  [exchange(): return lax.all_to_all(value, axes, 0, 0, tiled=True)]
    pallas_call x11 -> x12, Pallas kernels: 10.8 us -> 10.6 us  [call(): pl.pallas_call(kernel, name=name, out_shape=[jax.ShapeDtypeStruct(s, d) f...]
  transfers between devices with their start and end apart: 3 -> 4, of which waited for: 3 -> 4; matrix products, arithmetic and copies ran while one was open for 0% -> 0% of each run, Pallas kernels for 0% -> 0%
where the time goes in v3:
time: 212 us
  blocking collectives  183 us (86%)
  Pallas kernels  10.6 us (5%)
  starting transfers between devices  10 us (5%)
  waiting for transfers between devices  3.78 us (2%)
  local copies, waits for them, and re-layouts  3.34 us (2%)
    all_to_all x11, blocking collectives, exchange(): return lax.all_to_all(value, axes, 0, 0, tiled=True)  183 us
    pallas_call x12, Pallas kernels, call(): pl.pallas_call(kernel, name=name, out_shape=[jax.ShapeDtypeStruct(s, d) f...  10.6 us
    ppermute x4, starting transfers between devices, swap_cores(): return lax.ppermute(value, 'h', [(0, 1), (1, 0)])  10 us
  transfers between devices with their start and end apart: 4, of which 4 were waited for; matrix products, arithmetic and copies ran while one was open for 0% of the time, Pallas kernels for 0%

profile of v3, /device:TPU:1, one launch (start us, length us, event | category | flops | bytes accessed | tf_op | source)
XLA Modules:
  0.0 211.8 jit_solution(8030254887679038970)
XLA Ops:
  1.4 0.9 copy-done
  4.9 27.3 %all_to_all.121 = bf16[128,4,128]{2,1,0:T(4,128)(2,1)S(1)} all-to-all(bf16[128,4,128]{2,1,0:T(4,128)(2,1)S(1)} %bitcast.50), channel_id=1, replica_groups=mesh['y'=4,'zl'=2,'h'=2,'zh'=4,'x'=4] {'y','zl','zh','x'}, dimensions={0} | all-to-all | bytes 262144 | tf_op jit(solution)/shard_map/all_to_all | solution.py:321
  32.2 2.1 collective-permute-start
  34.4 1.0 collective-permute-done.other
  35.3 1.3 outgoing.1
  36.7 16.4 %all_to_all.122 = bf16[128,2,128]{2,1,0:T(2,128)(2,1)S(1)} all-to-all(bf16[128,2,128]{2,1,0:T(2,128)(2,1)S(1)} %bitcast.55), channel_id=1, replica_groups=mesh['y'=4,'zl'=2,'h'=2,'zh'=4,'x'=4] {'y','zl','zh','x'}, dimensions={0} | all-to-all | bytes 131072 | tf_op jit(solution)/shard_map/all_to_all | solution.py:321
  53.7 16.7 %all_to_all.123 = bf16[128,4,128]{2,1,0:T(4,128)(2,1)S(1)} all-to-all(bf16[128,4,128]{2,1,0:T(4,128)(2,1)S(1)} %bitcast.51), channel_id=1, replica_groups=mesh['y'=4,'zl'=2,'h'=2,'zh'=4,'x'=4] {'y','zl','zh','x'}, dimensions={0} | all-to-all | bytes 262144 | tf_op jit(solution)/shard_map/all_to_all | solution.py:321
  70.4 2.7 %collective-permute-start.1 = (bf16[512,128]{1,0:T(8,128)(2,1)S(1)}, bf16[512,128]{1,0:T(8,128)(2,1)S(1)}, u32[]{:S(2)}, u32[]{:S(2)}) collective-permute-start(bf16[512,128]{1,0:T(8,128)(2,1)S(1)} %bitcast.37), channel_id=1, source_target_pairs={{0,16},{16,0},{1,17},{17,1},{2,18},{18,2},{3,19},{19,3},{4,20},{20... | collective-permute-start | bytes 393224 | tf_op jit(solution)/shard_map/ppermute | solution.py:325
  73.1 1.0 collective-permute-done.1.other
  74.1 1.5 incoming.1
  75.6 16.6 %all_to_all.124 = bf16[128,2,128]{2,1,0:T(2,128)(2,1)S(1)} all-to-all(bf16[128,2,128]{2,1,0:T(2,128)(2,1)S(1)} %bitcast.56), channel_id=1, replica_groups=mesh['y'=4,'zl'=2,'h'=2,'zh'=4,'x'=4] {'y','zl','zh','x'}, dimensions={0} | all-to-all | bytes 131072 | tf_op jit(solution)/shard_map/all_to_all | solution.py:321
  92.2 1.0 turn.1
  93.2 16.2 %all_to_all.125 = bf16[128,2,128]{2,1,0:T(2,128)(2,1)S(1)} all-to-all(bf16[128,2,128]{2,1,0:T(2,128)(2,1)S(1)} %bitcast.54), channel_id=1, replica_groups=mesh['y'=4,'zl'=2,'h'=2,'zh'=4,'x'=4] {'y','zl','zh','x'}, dimensions={0} | all-to-all | bytes 131072 | tf_op jit(solution)/shard_map/all_to_all | solution.py:321
  109.4 2.7 %collective-permute-start.2 = (bf16[256,128]{1,0:T(8,128)(2,1)S(1)}, bf16[256,128]{1,0:T(8,128)(2,1)S(1)}, u32[]{:S(2)}, u32[]{:S(2)}) collective-permute-start(bf16[256,128]{1,0:T(8,128)(2,1)S(1)} %bitcast.45), channel_id=1, source_target_pairs={{0,16},{16,0},{1,17},{17,1},{2,18},{18,2},{3,19},{19,3},{4,20},{20... | collective-permute-start | bytes 196616 | tf_op jit(solution)/shard_map/ppermute | solution.py:325
  113.0 1.1 incoming_back.1
  114.1 17.1 %all_to_all.126 = bf16[128,4,128]{2,1,0:T(4,128)(2,1)S(1)} all-to-all(bf16[128,4,128]{2,1,0:T(4,128)(2,1)S(1)} %bitcast.39), channel_id=1, replica_groups=mesh['y'=4,'zl'=2,'h'=2,'zh'=4,'x'=4] {'y','zl','zh','x'}, dimensions={0} | all-to-all | bytes 262144 | tf_op jit(solution)/shard_map/all_to_all | solution.py:321
  132.0 16.5 %all_to_all.127 = bf16[128,2,128]{2,1,0:T(2,128)(2,1)S(1)} all-to-all(bf16[128,2,128]{2,1,0:T(2,128)(2,1)S(1)} %bitcast.53), channel_id=1, replica_groups=mesh['y'=4,'zl'=2,'h'=2,'zh'=4,'x'=4] {'y','zl','zh','x'}, dimensions={0} | all-to-all | bytes 131072 | tf_op jit(solution)/shard_map/all_to_all | solution.py:321
  148.4 2.6 %collective-permute-start.3 = (bf16[256,128]{1,0:T(8,128)(2,1)S(1)}, bf16[256,128]{1,0:T(8,128)(2,1)S(1)}, u32[]{:S(2)}, u32[]{:S(2)}) collective-permute-start(bf16[256,128]{1,0:T(8,128)(2,1)S(1)} %bitcast.47), channel_id=1, source_target_pairs={{0,16},{16,0},{1,17},{17,1},{2,18},{18,2},{3,19},{19,3},{4,20},{20... | collective-permute-start | bytes 196616 | tf_op jit(solution)/shard_map/ppermute | solution.py:325
  152.0 1.1 outgoing_back.1
  153.1 17.1 %all_to_all.128 = bf16[128,4,128]{2,1,0:T(4,128)(2,1)S(1)} all-to-all(bf16[128,4,128]{2,1,0:T(4,128)(2,1)S(1)} %bitcast.40), channel_id=1, replica_groups=mesh['y'=4,'zl'=2,'h'=2,'zh'=4,'x'=4] {'y','zl','zh','x'}, dimensions={0} | all-to-all | bytes 262144 | tf_op jit(solution)/shard_map/all_to_all | solution.py:321
  170.2 1.3 end.1
  171.4 14.8 %all_to_all.129 = bf16[32,48,128]{2,1,0:T(8,128)(2,1)S(1)} all-to-all(bf16[32,48,128]{2,1,0:T(8,128)(2,1)S(1)} %bitcast.42), channel_id=1, replica_groups=mesh['y'=4,'zl'=2,'h'=2,'zh'=4,'x'=4] {'y','h','x'}, dimensions={0} | all-to-all | bytes 786432 | tf_op jit(solution)/shard_map/all_to_all | solution.py:321
  186.3 9.4 %all_to_all.130 = bf16[8,48,128]{2,1,0:T(8,128)(2,1)S(1)} all-to-all(bf16[8,48,128]{2,1,0:T(8,128)(2,1)S(1)} %bitcast.43), channel_id=1, replica_groups=mesh['y'=4,'zl'=2,'h'=2,'zh'=4,'x'=4] {'zl','zh'}, dimensions={0} | all-to-all | bytes 196608 | tf_op jit(solution)/shard_map/all_to_all | solution.py:321
  195.8 15.1 %all_to_all.131 = bf16[32,48,128]{2,1,0:T(8,128)(2,1)S(1)} all-to-all(bf16[32,48,128]{2,1,0:T(8,128)(2,1)S(1)} %bitcast.31), channel_id=1, replica_groups=mesh['y'=4,'zl'=2,'h'=2,'zh'=4,'x'=4] {'y','h','x'}, dimensions={0} | all-to-all | bytes 786432 | tf_op jit(solution)/shard_map/all_to_all | solution.py:321
  (31 shorter events, 7.4 us)
Async XLA Ops:
  0.6 0.7 copy-start.10
  0.6 0.7 copy-start.8
  0.7 0.7 copy-start.9
  0.7 0.7 copy-start.7
  0.7 0.7 copy-start.11
  1.4 1.0 copy-start
  2.3 0.8 copy-start.2
  3.2 0.8 copy-start.5
  32.2 20.9 %copy-start.1 = (bf16[2,128,512]{2,1,0:T(8,128)(2,1)S(1)}, bf16[2,128,512]{2,1,0:T(8,128)(2,1)}, u32[]{:S(2)}) copy-start(bf16[2,128,512]{2,1,0:T(8,128)(2,1)} %w_in.5) | copy-start | bytes 786436
  32.2 3.1 %collective-permute-start = (bf16[512,128]{1,0:T(8,128)(2,1)S(1)}, bf16[512,128]{1,0:T(8,128)(2,1)S(1)}, u32[]{:S(2)}, u32[]{:S(2)}) collective-permute-start(bf16[512,128]{1,0:T(8,128)(2,1)S(1)} %bitcast.35), channel_id=1, source_target_pairs={{0,16},{16,0},{1,17},{17,1},{2,18},{18,2},{3,19},{19,3},{4,20},{20... | collective-permute-start | bytes 393224 | tf_op jit(solution)/shard_map/ppermute | solution.py:325
  36.7 16.4 %copy-start.3 = (bf16[2,128,128]{2,1,0:T(8,128)(2,1)S(1)}, bf16[2,128,128]{2,1,0:T(8,128)(2,1)}, u32[]{:S(2)}) copy-start(bf16[2,128,128]{2,1,0:T(8,128)(2,1)} %w_gate.5) | copy-start | bytes 196612
  36.7 16.4 %copy-start.4 = (bf16[2,128,128]{2,1,0:T(8,128)(2,1)S(1)}, bf16[2,128,128]{2,1,0:T(8,128)(2,1)}, u32[]{:S(2)}) copy-start(bf16[2,128,128]{2,1,0:T(8,128)(2,1)} %w_out.5) | copy-start | bytes 196612
  70.4 3.6 %collective-permute-start.1 = (bf16[512,128]{1,0:T(8,128)(2,1)S(1)}, bf16[512,128]{1,0:T(8,128)(2,1)S(1)}, u32[]{:S(2)}, u32[]{:S(2)}) collective-permute-start(bf16[512,128]{1,0:T(8,128)(2,1)S(1)} %bitcast.37), channel_id=1, source_target_pairs={{0,16},{16,0},{1,17},{17,1},{2,18},{18,2},{3,19},{19,3},{4,20},{20... | collective-permute-start | bytes 393224 | tf_op jit(solution)/shard_map/ppermute | solution.py:325
  75.6 16.6 %copy-start.6 = (bf16[16,16,128]{2,1,0:T(8,128)(2,1)S(1)}, bf16[16,16,128]{2,1,0:T(8,128)(2,1)}, u32[]{:S(2)}) copy-start(bf16[16,16,128]{2,1,0:T(8,128)(2,1)} %param.11) | copy-start | bytes 196612
  109.4 3.6 %collective-permute-start.2 = (bf16[256,128]{1,0:T(8,128)(2,1)S(1)}, bf16[256,128]{1,0:T(8,128)(2,1)S(1)}, u32[]{:S(2)}, u32[]{:S(2)}) collective-permute-start(bf16[256,128]{1,0:T(8,128)(2,1)S(1)} %bitcast.45), channel_id=1, source_target_pairs={{0,16},{16,0},{1,17},{17,1},{2,18},{18,2},{3,19},{19,3},{4,20},{20... | collective-permute-start | bytes 196616 | tf_op jit(solution)/shard_map/ppermute | solution.py:325
  148.4 3.5 %collective-permute-start.3 = (bf16[256,128]{1,0:T(8,128)(2,1)S(1)}, bf16[256,128]{1,0:T(8,128)(2,1)S(1)}, u32[]{:S(2)}, u32[]{:S(2)}) collective-permute-start(bf16[256,128]{1,0:T(8,128)(2,1)S(1)} %bitcast.47), channel_id=1, source_target_pairs={{0,16},{16,0},{1,17},{17,1},{2,18},{18,2},{3,19},{19,3},{4,20},{20... | collective-permute-start | bytes 196616 | tf_op jit(solution)/shard_map/ppermute | solution.py:325

commit v4 on v3

v4 whole, which is shorter than its diff:
```python
import functools

import jax
import jax.numpy as jnp
from jax import lax
from jax.experimental import pallas as pl
from jax.experimental.pallas import tpu as pltpu
from jax.sharding import Mesh, PartitionSpec as P

F32 = jnp.float32
BF16 = jnp.bfloat16
POS = 256
CH = 128
EPS = 1e-05
SIZES = {"y": 4, "zl": 2, "h": 2, "zh": 4, "x": 4}
CHIPS = ("zh", "x", "y", "zl")
PLANE = ("h", "x", "y")
LINE = ("zl", "zh")


def dot(a, b, ca, cb):
    return lax.dot_general(
        a.astype(BF16), b.astype(BF16), (((ca,), (cb,)), ((), ())), preferred_element_type=F32
    )


def swap_blocks(tiles):
    block = lax.broadcasted_iota(jnp.int32, tiles[0].shape, 1) // 16
    for d in (1, 2, 4):
        high = (block & d) != 0
        out = list(tiles)
        for t in range(8):
            if t & d == 0:
                lo, hi = tiles[t], tiles[t | d]
                out[t] = jnp.where(high, pltpu.roll(hi, 16 * d, 1), lo)
                out[t | d] = jnp.where(high, hi, pltpu.roll(lo, 128 - 16 * d, 1))
        tiles = out
    return tiles


def messages_to_half(src, off, w, dst):
    for half in range(2):
        for p in range(2):
            tiles = [
                src[pl.ds((2 * t + p) * 8 * w + off + half, 8, stride=w), :] for t in range(8)
            ]
            for t, tile in enumerate(swap_blocks(tiles)):
                dst[p, pl.ds(half * 8 + t, 8, stride=16), :] = tile
    return jnp.concatenate([dst[0], dst[1]], axis=1).astype(BF16)


def half_to_messages(value, src, dst, off, w):
    for p in range(2):
        src[p] = value[p]
    for half in range(2):
        for p in range(2):
            tiles = [src[p, pl.ds(half * 8 + t, 8, stride=16), :] for t in range(8)]
            for t, tile in enumerate(swap_blocks(tiles)):
                dst[pl.ds((2 * t + p) * 8 * w + off + half, 8, stride=w), :] = tile


def halves(value):
    return value[:, 0:128], value[:, 128:256]


def by_parity(mine, other):
    first = lax.axis_index("h") == 0
    return jnp.where(first, mine, other), jnp.where(first, other, mine)


def own_columns(value):
    return by_parity(*halves(value))[0]


def other_columns(value):
    return by_parity(*halves(value))[1]


def channels_to_messages(v, dst, off, w):
    for half in range(2):
        dst[pl.ds(off + half, CH, stride=w), :] = v[:, half * 128 : (half + 1) * 128]


def messages_to_channels(src, off, w):
    return jnp.concatenate(
        [src[pl.ds(off + half, CH, stride=w), :] for half in range(2)], axis=1
    )


def column(row):
    square = jnp.broadcast_to(row, (CH, CH)).T
    return jnp.concatenate([square, square], axis=1)


def normalise(z):
    centered = z - jnp.mean(z, axis=0, keepdims=True)
    rstd = lax.rsqrt(jnp.mean(centered * centered, axis=0, keepdims=True) + EPS)
    return centered * rstd, rstd


def normalise_back(cot, hat, rstd):
    return rstd * (
        cot
        - jnp.mean(cot, axis=0, keepdims=True)
        - hat * jnp.mean(cot * hat, axis=0, keepdims=True)
    )


def prepare(z, gain, w_in, w_gate, m, n_ref, g_ref, send, send_ref, copies=()):
    hat, _ = normalise(z)
    normed = (hat * gain).astype(BF16)
    n_ref[...] = normed
    for copy in copies:
        copy.wait()
    p = dot(w_in[...], normed, 0, 0)
    a = m * jax.nn.sigmoid(p[0:128]) * p[128:256]
    b = m * jax.nn.sigmoid(p[256:384]) * p[384:512]
    g_ref[...] = jax.nn.sigmoid(dot(w_gate[...], normed, 0, 0))
    channels_to_messages(a, send, 0, 4)
    channels_to_messages(b, send, 2, 4)
    send_ref[...] = send[...].astype(BF16)


def prepare_back(recv, z, normed, gain, w_in, w_gate, m, dpg, dp):
    p = dot(w_in, normed, 0, 0)
    for k in range(2):
        cot = messages_to_channels(recv, 2 * k, 4) * m
        s = jax.nn.sigmoid(p[256 * k : 256 * k + 128])
        v = p[256 * k + 128 : 256 * k + 256]
        dp[256 * k : 256 * k + 128, :] = (cot * v * s * (1.0 - s)).astype(BF16)
        dp[256 * k + 128 : 256 * k + 256, :] = (cot * s).astype(BF16)
    dn = dot(w_in, dp[...], 1, 0) + dot(w_gate, dpg, 1, 0)
    hat, rstd = normalise(z)
    return normalise_back(dn * gain, hat, rstd)


def start_kernel(*refs):
    hbm, (z_ref, n_ref, g_ref, m_ref, gain_ref, send_ref), refs = refs[:8], refs[8:14], refs[14:]
    vmem, send, sem = refs[:8], refs[8], refs[9]
    copies = [
        pltpu.make_async_copy(src.at[0] if k > 5 else src, dst, sem.at[k])
        for k, (src, dst) in enumerate(zip(hbm, vmem))
    ]
    for copy in copies:
        copy.start()
    pair, mask, chain, bias, in_gain, out_gain, w_in, w_gate = vmem
    row = (lax.axis_index("y") * 2 + lax.axis_index("zl")) * 2 + lax.axis_index("h")
    col = lax.axis_index("zh") * 4 + lax.axis_index("x")
    res = lax.broadcasted_iota(jnp.int32, (256, POS), 0)
    pos = lax.broadcasted_iota(jnp.int32, (256, POS), 1)
    in_row = (res == row * 16 + pos // 16).astype(F32)
    in_col = (res == col * 16 + pos % 16).astype(F32)
    for copy in copies[:6]:
        copy.wait()
    both = jnp.concatenate(
        [
            jnp.broadcast_to(mask[...].astype(F32), (8, 256)),
            jnp.broadcast_to(chain[...].astype(F32), (8, 256)),
        ],
        axis=0,
    )
    of_row = dot(both, in_row, 1, 0)
    of_col = dot(both, in_col, 1, 0)
    m8 = of_row[0:8] * of_col[0:8]
    m_ref[...] = m8
    gain_ref[0:2, :] = in_gain[...]
    gain_ref[2:4, :] = out_gain[...]
    same = (of_row[8:9] == of_col[8:9]).astype(F32)
    z = pair[...].astype(F32).T + same * column(bias[...])
    z_ref[...] = z
    gain = column(in_gain[0:1])
    prepare(z, gain, w_in, w_gate, m8[0:1], n_ref, g_ref, send, send_ref, copies[6:])


def middle_kernel(x_in, z0, g0, m, gains, w_in, w_gate, w_out, z_ref, y_ref, n_ref, g_ref, send_ref, xs, send):
    xs[...] = x_in[...].astype(F32)
    hat, _ = normalise(messages_to_channels(xs, 0, 2))
    y = dot(w_out[0], hat * column(gains[2:3]), 0, 0)
    y_ref[...] = y
    z = z0[...] + g0[...] * y
    z_ref[...] = z
    prepare(z, column(gains[1:2]), w_in.at[1], w_gate.at[1], m[0:1], n_ref, g_ref, send, send_ref)


def turn_kernel(x_in, g1, cot_in, gains, w_out, cot_ref, y_ref, xn_ref, dy_ref, dpg_ref, send_ref, xs, send):
    xs[...] = x_in[...].astype(F32)
    gain = column(gains[3:4])
    hat, rstd = normalise(messages_to_channels(xs, 0, 2))
    xn = (hat * gain).astype(BF16)
    xn_ref[...] = xn
    y = dot(w_out[1], xn, 0, 0)
    y_ref[...] = y
    g = g1[...]
    cot = cot_in[...].astype(F32).T
    cot_ref[...] = cot
    dy = (cot * g).astype(BF16)
    dy_ref[...] = dy
    dpg_ref[...] = (cot * y * g * (1.0 - g)).astype(BF16)
    gx = normalise_back(dot(w_out[1], dy, 1, 0) * gain, hat, rstd)
    channels_to_messages(gx, send, 0, 2)
    send_ref[...] = send[...].astype(BF16)


def turn_rest_kernel(z1, y1, g1, n1, xn, dy, dpg, new_ref, gw_ref):
    new_ref[...] = (z1[...] + g1[...] * y1[...]).T.astype(BF16)
    gw_ref[0:128, :] = dot(n1[...], dpg[...], 1, 1).astype(BF16)
    gw_ref[128:256, :] = dot(xn[...], dy[...], 1, 1).astype(BF16)


def back_kernel(gab, n1, z1, m, dpg1, cot, x_in, g0, y0, gains, w_in, w_gate, w_out, dz_ref, dp_ref, dpg_ref, xn_ref, dy_ref, send_ref, rs, xs, send):
    rs[...] = gab[...].astype(F32)
    dz = cot[...] + prepare_back(
        rs, z1[...], n1[...], column(gains[1:2]), w_in[1], w_gate[1], m[0:1], dpg1[...], dp_ref
    )
    dz_ref[...] = dz
    g = g0[...]
    dpg_ref[...] = (dz * y0[...] * g * (1.0 - g)).astype(BF16)
    dy = (dz * g).astype(BF16)
    dy_ref[...] = dy
    xs[...] = x_in[...].astype(F32)
    gain = column(gains[2:3])
    hat, rstd = normalise(messages_to_channels(xs, 0, 2))
    xn_ref[...] = (hat * gain).astype(BF16)
    gx = normalise_back(dot(w_out[0], dy, 1, 0) * gain, hat, rstd)
    channels_to_messages(gx, send, 0, 2)
    send_ref[...] = send[...].astype(BF16)


def back_rest_kernel(n1, dp1, gw1, n0, dpg0, xn, dy, early_ref):
    for e in range(4):
        block = slice(128 * e, 128 * (e + 1))
        early_ref[block, :] = dot(n1[...], dp1[block, :], 1, 1).astype(BF16)
    early_ref[512:768, :] = gw1[...]
    early_ref[768:896, :] = dot(n0[...], dpg0[...], 1, 1).astype(BF16)
    early_ref[896:1024, :] = dot(xn[...], dy[...], 1, 1).astype(BF16)


def end_kernel(gab, n0, z0, m, dpg0, dz1, gains, w_in, w_gate, early, grad_ref, send_ref, rs, dp):
    rs[...] = gab[...].astype(F32)
    dz = dz1[...] + prepare_back(
        rs, z0[...], n0[...], column(gains[0:1]), w_in[0], w_gate[0], m[0:1], dpg0[...], dp
    )
    grad_ref[...] = dz.T
    for e in range(4):
        part = dot(n0[...], dp[128 * e : 128 * (e + 1), :], 1, 1)
        send_ref[128 * e : 128 * (e + 1), :] = part.astype(BF16)
    send_ref[512:1536, :] = early[...]


def sum_kernel(recv, send_ref):
    total = recv[0:48, :].astype(F32)
    for k in range(1, recv.shape[0] // 48):
        total = total + recv[48 * k : 48 * (k + 1), :].astype(F32)
    total = total.astype(BF16)
    for k in range(send_ref.shape[0] // 48):
        send_ref[48 * k : 48 * (k + 1), :] = total


def place_kernel(recv, grad, in_out, gate_out, out_out, grad_out, in_ref, gate_ref, out_ref, sem):
    copies = []

    def write(src, dst):
        copies.append(pltpu.make_async_copy(src, dst, sem.at[len(copies)]))
        copies[-1].start()

    def block(k):
        return recv[128 * k : 128 * (k + 1), :].astype(F32)

    write(grad, grad_out)
    for u in range(2):
        for e in range(4):
            in_ref[u, :, 128 * e : 128 * (e + 1)] = block(4 * u + e)
        write(in_ref.at[u], in_out.at[u])
    for k, u in ((8, 1), (10, 0)):
        gate_ref[u] = block(k)
        out_ref[u] = block(k + 1)
    write(gate_ref, gate_out)
    write(out_ref, out_out)
    for copy in copies:
        copy.wait()


def outgoing_mine_kernel(mine, a_ref, b_ref, x_ref, ms, mat):
    ms[...] = mine[...].astype(F32)
    a, b = messages_to_half(ms, 0, 4, mat), messages_to_half(ms, 2, 4, mat)
    a_ref[...] = a
    b_ref[...] = b
    x_ref[...] = dot(a, b, 1, 1)


def outgoing_kernel(other, a, x_mine, b_ref, send_ref, os, mat, send):
    os[...] = other[...].astype(F32)
    b = messages_to_half(os, 2, 4, mat)
    b_ref[...] = b
    half_to_messages(by_parity(x_mine[...], dot(a[...], b, 1, 1)), mat, send, 0, 2)
    send_ref[...] = send[...].astype(BF16)


def incoming_mine_kernel(mine, a_ref, b_ref, x_ref, ms, mat):
    ms[...] = mine[...].astype(F32)
    a, b = messages_to_half(ms, 0, 4, mat), messages_to_half(ms, 2, 4, mat)
    a_ref[...] = a
    b_ref[...] = b
    x_ref[...] = dot(own_columns(a), b, 0, 0)


def incoming_kernel(other, x_mine, send_ref, os, mat, send):
    os[...] = other[...].astype(F32)
    a, b = messages_to_half(os, 0, 4, mat), messages_to_half(os, 2, 4, mat)
    half_to_messages(halves(x_mine[...] + dot(own_columns(a), b, 0, 0)), mat, send, 0, 2)
    send_ref[...] = send[...].astype(BF16)


def incoming_back_mine_kernel(mine, a, b, ga_ref, gb_ref, ms, mat):
    ms[...] = mine[...].astype(F32)
    gx = messages_to_half(ms, 0, 2, mat)
    ga_ref[...] = dot(b[...], gx, 1, 1)
    gb_ref[...] = dot(own_columns(a[...]), gx, 1, 0)


def incoming_back_kernel(other, a, b, ga_mine, gb_mine, send_ref, os, mat, send):
    os[...] = other[...].astype(F32)
    gx = messages_to_half(os, 0, 2, mat)
    half_to_messages(by_parity(ga_mine[...], dot(b[...], gx, 1, 1)), mat, send, 0, 4)
    gb = gb_mine[...] + dot(other_columns(a[...]), gx, 1, 0)
    half_to_messages(halves(gb), mat, send, 2, 4)
    send_ref[...] = send[...].astype(BF16)


def other_rows_kernel(other_ab, a_ref, os, mat):
    os[...] = other_ab[...].astype(F32)
    a_ref[...] = messages_to_half(os, 0, 4, mat)


def outgoing_back_mine_kernel(mine, a, b, b_other, ga_ref, gb_ref, ms, mat, send):
    ms[...] = mine[...].astype(F32)
    gx = messages_to_half(ms, 0, 2, mat)
    even, odd = by_parity(b[...], b_other[...])
    ga = dot(gx, jnp.concatenate([even, odd], axis=0), 1, 0)
    half_to_messages(halves(ga), mat, send, 0, 2)
    ga_ref[...] = send[...]
    gb_ref[...] = dot(own_columns(gx), a[...], 0, 0)


def outgoing_back_kernel(other, ga, gb_mine, a_other, send_ref, os, mat, send):
    os[...] = other[...].astype(F32)
    gx = messages_to_half(os, 0, 2, mat)
    gb = gb_mine[...] + dot(own_columns(gx), a_other[...], 0, 0)
    half_to_messages(halves(gb), mat, send, 2, 4)
    for half in range(2):
        send[pl.ds(half, CH, stride=4), :] = ga[pl.ds(half, CH, stride=2), :]
    send_ref[...] = send[...].astype(BF16)


def call(kernel, name, outs, scratch, *args, **kwargs):
    return pl.pallas_call(
        kernel,
        name=name,
        out_shape=[jax.ShapeDtypeStruct(s, d) for s, d in outs],
        scratch_shapes=[s if not isinstance(s, tuple) else pltpu.VMEM(*s) for s in scratch],
        compiler_params=pltpu.CompilerParams(vmem_limit_bytes=24 * 1024 * 1024),
        cost_estimate=pl.CostEstimate(flops=2**24, bytes_accessed=2**20, transcendentals=0),
        **kwargs,
    )(*args)


def exchange(value, axes=CHIPS):
    return lax.all_to_all(value, axes, 0, 0, tiled=True)


def swap_cores(value):
    return lax.ppermute(value, "h", [(0, 1), (1, 0)])


def after(done, *values):
    return lax.optimization_barrier((done,) + values)[1:]


def shards(pair, pair_cot, mask, chain_ids, chain_bias, w_in, w_gate, w_out, in_gain, out_gain):
    block = pair.shape
    pair = pair.reshape(POS, CH)
    cot_in = pair_cot.reshape(POS, CH)
    mask, chain, bias = mask[None, :], chain_ids[None, :], chain_bias[None, :]
    field, field16 = ((CH, POS), F32), ((CH, POS), BF16)
    square, work = ((128, 128), F32), ((2, 128, 128), F32)

    def rows(n, dtype=F32):
        return ((n, 128), dtype)

    operands = [
        pltpu.with_memory_space_constraint(v, pltpu.HBM)
        for v in (pair, mask, chain, bias, in_gain, out_gain, w_in, w_gate)
    ]
    z0, n0, g0, m, gains, send = call(
        start_kernel, "start", [field, field16, field, ((8, POS), F32), rows(4), rows(512, BF16)],
        [(v.shape[1:] if k > 5 else v.shape, v.dtype) for k, v in enumerate(operands)]
        + [rows(512), pltpu.SemaphoreType.DMA((8,))],
        *operands, in_specs=[pl.BlockSpec(memory_space=pltpu.HBM)] * 8,
    )
    mine = exchange(send)
    other_ab = swap_cores(mine)
    a0, b0, x_mine = call(
        outgoing_mine_kernel, "outgoing_mine", [field16, field16, square], [rows(512), work], mine
    )
    b0_other, send = call(
        outgoing_kernel, "outgoing", [field16, rows(256, BF16)], [rows(512), work, rows(256)],
        other_ab, a0, x_mine,
    )
    x0 = exchange(send)
    z1, y0, n1, g1, send = call(
        middle_kernel, "middle", [field, field, field16, field, rows(512, BF16)], [rows(256), rows(512)],
        x0, z0, g0, m, gains, w_in, w_gate, w_out,
    )
    mine = exchange(send)
    other = swap_cores(mine)
    a1, b1, x_mine = call(
        incoming_mine_kernel, "incoming_mine", [field16, field16, field], [rows(512), work], mine
    )
    (a0_other,) = call(
        other_rows_kernel, "other_rows", [field16], [rows(512), work], *after(mine, other_ab)
    )
    (send,) = call(
        incoming_kernel, "incoming", [rows(256, BF16)], [rows(512), work, rows(256)],
        other, *after(a0_other, x_mine),
    )
    cot, y1, xn, dy, dpg1, send = call(
        turn_kernel, "turn", [field, field, field16, field16, field16, rows(256, BF16)],
        [rows(256), rows(256)], exchange(send), g1, cot_in, gains, w_out,
    )
    mine = exchange(send)
    other = swap_cores(mine)
    ga, gb = call(
        incoming_back_mine_kernel, "incoming_back_mine", [square, field], [rows(256), work], mine, a1, b1
    )
    new_pair, gw1 = call(
        turn_rest_kernel, "turn_rest", [rows(POS, BF16), rows(256, BF16)], [],
        *after(mine, z1, y1, g1, n1, xn, dy, dpg1),
    )
    (send,) = call(
        incoming_back_kernel, "incoming_back", [rows(512, BF16)], [rows(256), work, rows(512)],
        other, a1, b1, *after(gw1, ga, gb),
    )
    dz1, dp1, dpg0, xn, dy, send = call(
        back_kernel, "back", [field, ((512, POS), BF16), field16, field16, field16, rows(256, BF16)],
        [rows(512), rows(256), rows(256)],
        exchange(send), n1, z1, m, dpg1, cot, x0, g0, y0, gains, w_in, w_gate, w_out,
    )
    mine = exchange(send)
    other = swap_cores(mine)
    ga, gb = call(
        outgoing_back_mine_kernel, "outgoing_back_mine", [rows(256), field],
        [rows(256), work, rows(256)], mine, a0, b0, b0_other,
    )
    (early,) = call(
        back_rest_kernel, "back_rest", [rows(1024, BF16)], [], *after(mine, n1, dp1, gw1, n0, dpg0, xn, dy)
    )
    (send,) = call(
        outgoing_back_kernel, "outgoing_back", [rows(512, BF16)], [rows(256), work, rows(512)],
        other, *after(early, ga, gb), a0_other,
    )
    pair_grad, send = call(
        end_kernel, "end", [rows(POS), rows(1536, BF16)],
        [rows(512), ((512, POS), BF16)],
        exchange(send), n0, z0, m, dpg0, dz1, gains, w_in, w_gate, early,
    )
    (send,) = call(sum_kernel, "plane_sum", [rows(384, BF16)], [], exchange(send, PLANE))
    (send,) = call(sum_kernel, "line_sum", [rows(1536, BF16)], [], exchange(send, LINE))
    weights = [((2, 128, 512), F32), ((2, 128, 128), F32), ((2, 128, 128), F32)]
    in_grad, gate_grad, out_grad, pair_grad = call(
        place_kernel, "place", weights + [rows(POS)], weights + [pltpu.SemaphoreType.DMA((5,))],
        exchange(send, PLANE), pair_grad, out_specs=[pl.BlockSpec(memory_space=pltpu.HBM)] * 4,
    )
    return (new_pair.reshape(block), pair_grad.reshape(block), in_grad, gate_grad, out_grad)


def solution(mesh):
    devices = mesh.devices.reshape(tuple(SIZES.values()))
    split = P(("y", "zl", "h"), ("zh", "x"), None)
    return jax.shard_map(
        shards,
        mesh=Mesh(devices, tuple(SIZES)),
        in_specs=(split, split) + (P(),) * 8,
        out_specs=(split, split, P(), P(), P()),
        check_vma=False,
    )
```

time: 212 us -> 205 us (0.967)
  local copies, waits for them, and re-layouts: 3.34 us -> 0.02 us
  waiting for transfers between devices: 3.78 us -> 0.78 us
    unnamed x24 -> x8, local copies, waits for them, and re-layouts: 3.34 us -> 0.02 us
    ppermute x4, waiting for transfers between devices: 3.78 us -> 0.78 us  [swap_cores(): return lax.ppermute(value, 'h', [(0, 1), (1, 0)])]
    pallas_call x12 -> x19, Pallas kernels: 10.6 us -> 11 us  [call(): pl.pallas_call(kernel, name=name, out_shape=[jax.ShapeDtypeStruct(s, d) f...]
  transfers between devices with their start and end apart: 4 -> 4, of which waited for: 4 -> 2; matrix products, arithmetic and copies ran while one was open for 0% -> 0% of each run, Pallas kernels for 0% -> 2%
where the time goes in v4:
time: 205 us
  blocking collectives  182 us (89%)
  Pallas kernels  11 us (5%)
  starting transfers between devices  9.86 us (5%)
    all_to_all x11, blocking collectives, exchange(): return lax.all_to_all(value, axes, 0, 0, tiled=True)  182 us
    pallas_call x19, Pallas kernels, call(): pl.pallas_call(kernel, name=name, out_shape=[jax.ShapeDtypeStruct(s, d) f...  11 us
    ppermute x4, starting transfers between devices, swap_cores(): return lax.ppermute(value, 'h', [(0, 1), (1, 0)])  9.86 us
  transfers between devices with their start and end apart: 4, of which 2 were waited for; matrix products, arithmetic and copies ran while one was open for 0% of the time, Pallas kernels for 2%

profile of v4, /device:TPU:1, one launch (start us, length us, event | category | flops | bytes accessed | tf_op | source)
XLA Modules:
  0.0 204.8 jit_solution(8508308945087946125)
XLA Ops:
  0.6 1.5 start.1
  2.1 27.3 %all_to_all.121 = bf16[128,4,128]{2,1,0:T(4,128)(2,1)S(1)} all-to-all(bf16[128,4,128]{2,1,0:T(4,128)(2,1)S(1)} %bitcast.51), channel_id=1, replica_groups=mesh['y'=4,'zl'=2,'h'=2,'zh'=4,'x'=4] {'zh','x','y','zl'}, dimensions={0} | all-to-all | bytes 262144 | tf_op jit(solution)/shard_map/all_to_all | solution.py:368
  29.4 2.0 collective-permute-start
  32.4 0.7 outgoing.1
  33.1 16.2 %all_to_all.122 = bf16[128,2,128]{2,1,0:T(2,128)(2,1)S(1)} all-to-all(bf16[128,2,128]{2,1,0:T(2,128)(2,1)S(1)} %bitcast.56), channel_id=1, replica_groups=mesh['y'=4,'zl'=2,'h'=2,'zh'=4,'x'=4] {'zh','x','y','zl'}, dimensions={0} | all-to-all | bytes 131072 | tf_op jit(solution)/shard_map/all_to_all | solution.py:368
  50.0 16.6 %all_to_all.123 = bf16[128,4,128]{2,1,0:T(4,128)(2,1)S(1)} all-to-all(bf16[128,4,128]{2,1,0:T(4,128)(2,1)S(1)} %bitcast.52), channel_id=1, replica_groups=mesh['y'=4,'zl'=2,'h'=2,'zh'=4,'x'=4] {'zh','x','y','zl'}, dimensions={0} | all-to-all | bytes 262144 | tf_op jit(solution)/shard_map/all_to_all | solution.py:368
  66.5 2.8 %collective-permute-start.1 = (bf16[512,128]{1,0:T(8,128)(2,1)S(1)}, bf16[512,128]{1,0:T(8,128)(2,1)S(1)}, u32[]{:S(2)}, u32[]{:S(2)}) collective-permute-start(bf16[512,128]{1,0:T(8,128)(2,1)S(1)} %bitcast.36), channel_id=1, source_target_pairs={{0,16},{16,0},{1,17},{17,1},{2,18},{18,2},{3,19},{19,3},{4,20},{20... | collective-permute-start | bytes 393224 | tf_op jit(solution)/shard_map/ppermute | solution.py:372
  70.3 0.8 incoming.1
  71.0 16.2 %all_to_all.124 = bf16[128,2,128]{2,1,0:T(2,128)(2,1)S(1)} all-to-all(bf16[128,2,128]{2,1,0:T(2,128)(2,1)S(1)} %bitcast.48), channel_id=1, replica_groups=mesh['y'=4,'zl'=2,'h'=2,'zh'=4,'x'=4] {'zh','x','y','zl'}, dimensions={0} | all-to-all | bytes 131072 | tf_op jit(solution)/shard_map/all_to_all | solution.py:368
  87.6 16.3 %all_to_all.125 = bf16[128,2,128]{2,1,0:T(2,128)(2,1)S(1)} all-to-all(bf16[128,2,128]{2,1,0:T(2,128)(2,1)S(1)} %bitcast.55), channel_id=1, replica_groups=mesh['y'=4,'zl'=2,'h'=2,'zh'=4,'x'=4] {'zh','x','y','zl'}, dimensions={0} | all-to-all | bytes 131072 | tf_op jit(solution)/shard_map/all_to_all | solution.py:368
  103.9 2.7 %collective-permute-start.2 = (bf16[256,128]{1,0:T(8,128)(2,1)S(1)}, bf16[256,128]{1,0:T(8,128)(2,1)S(1)}, u32[]{:S(2)}, u32[]{:S(2)}) collective-permute-start(bf16[256,128]{1,0:T(8,128)(2,1)S(1)} %bitcast.45), channel_id=1, source_target_pairs={{0,16},{16,0},{1,17},{17,1},{2,18},{18,2},{3,19},{19,3},{4,20},{20... | collective-permute-start | bytes 196616 | tf_op jit(solution)/shard_map/ppermute | solution.py:372
  107.0 0.8 turn_rest.1
  107.8 0.8 incoming_back.1
  108.6 17.5 %all_to_all.126 = bf16[128,4,128]{2,1,0:T(4,128)(2,1)S(1)} all-to-all(bf16[128,4,128]{2,1,0:T(4,128)(2,1)S(1)} %bitcast.40), channel_id=1, replica_groups=mesh['y'=4,'zl'=2,'h'=2,'zh'=4,'x'=4] {'zh','x','y','zl'}, dimensions={0} | all-to-all | bytes 262144 | tf_op jit(solution)/shard_map/all_to_all | solution.py:368
  126.1 0.7 back.1
  126.8 16.1 %all_to_all.127 = bf16[128,2,128]{2,1,0:T(2,128)(2,1)S(1)} all-to-all(bf16[128,2,128]{2,1,0:T(2,128)(2,1)S(1)} %bitcast.54), channel_id=1, replica_groups=mesh['y'=4,'zl'=2,'h'=2,'zh'=4,'x'=4] {'zh','x','y','zl'}, dimensions={0} | all-to-all | bytes 131072 | tf_op jit(solution)/shard_map/all_to_all | solution.py:368
  142.9 2.3 %collective-permute-start.3 = (bf16[256,128]{1,0:T(8,128)(2,1)S(1)}, bf16[256,128]{1,0:T(8,128)(2,1)S(1)}, u32[]{:S(2)}, u32[]{:S(2)}) collective-permute-start(bf16[256,128]{1,0:T(8,128)(2,1)S(1)} %bitcast.49), channel_id=1, source_target_pairs={{0,16},{16,0},{1,17},{17,1},{2,18},{18,2},{3,19},{19,3},{4,20},{20... | collective-permute-start | bytes 196616 | tf_op jit(solution)/shard_map/ppermute | solution.py:372
  145.3 0.7 outgoing_back_mine.1
  146.3 0.7 outgoing_back.1
  147.0 17.1 %all_to_all.128 = bf16[128,4,128]{2,1,0:T(4,128)(2,1)S(1)} all-to-all(bf16[128,4,128]{2,1,0:T(4,128)(2,1)S(1)} %bitcast.41), channel_id=1, replica_groups=mesh['y'=4,'zl'=2,'h'=2,'zh'=4,'x'=4] {'zh','x','y','zl'}, dimensions={0} | all-to-all | bytes 262144 | tf_op jit(solution)/shard_map/all_to_all | solution.py:368
  164.8 14.8 %all_to_all.129 = bf16[32,48,128]{2,1,0:T(8,128)(2,1)S(1)} all-to-all(bf16[32,48,128]{2,1,0:T(8,128)(2,1)S(1)} %bitcast.42), channel_id=1, replica_groups=mesh['y'=4,'zl'=2,'h'=2,'zh'=4,'x'=4] {'h','x','y'}, dimensions={0} | all-to-all | bytes 786432 | tf_op jit(solution)/shard_map/all_to_all | solution.py:368
  179.6 9.3 %all_to_all.130 = bf16[8,48,128]{2,1,0:T(8,128)(2,1)S(1)} all-to-all(bf16[8,48,128]{2,1,0:T(8,128)(2,1)S(1)} %bitcast.43), channel_id=1, replica_groups=mesh['y'=4,'zl'=2,'h'=2,'zh'=4,'x'=4] {'zl','zh'}, dimensions={0} | all-to-all | bytes 196608 | tf_op jit(solution)/shard_map/all_to_all | solution.py:368
  188.9 14.8 %all_to_all.131 = bf16[32,48,128]{2,1,0:T(8,128)(2,1)S(1)} all-to-all(bf16[32,48,128]{2,1,0:T(8,128)(2,1)S(1)} %bitcast.31), channel_id=1, replica_groups=mesh['y'=4,'zl'=2,'h'=2,'zh'=4,'x'=4] {'h','x','y'}, dimensions={0} | all-to-all | bytes 786432 | tf_op jit(solution)/shard_map/all_to_all | solution.py:368
  203.7 1.0 place.1
  (22 shorter events, 4.3 us)
Async XLA Ops:
  29.4 20.0 %copy-start = (bf16[2,128,512]{2,1,0:T(8,128)(2,1)S(1)}, bf16[2,128,512]{2,1,0:T(8,128)(2,1)}, u32[]{:S(2)}) copy-start(bf16[2,128,512]{2,1,0:T(8,128)(2,1)} %w_in.5) | copy-start | bytes 786436
  29.4 3.0 %collective-permute-start = (bf16[512,128]{1,0:T(8,128)(2,1)S(1)}, bf16[512,128]{1,0:T(8,128)(2,1)S(1)}, u32[]{:S(2)}, u32[]{:S(2)}) collective-permute-start(bf16[512,128]{1,0:T(8,128)(2,1)S(1)} %bitcast.38), channel_id=1, source_target_pairs={{0,16},{16,0},{1,17},{17,1},{2,18},{18,2},{3,19},{19,3},{4,20},{20... | collective-permute-start | bytes 393224 | tf_op jit(solution)/shard_map/ppermute | solution.py:372
  33.1 16.3 %copy-start.1 = (bf16[2,128,128]{2,1,0:T(8,128)(2,1)S(1)}, bf16[2,128,128]{2,1,0:T(8,128)(2,1)}, u32[]{:S(2)}) copy-start(bf16[2,128,128]{2,1,0:T(8,128)(2,1)} %w_gate.5) | copy-start | bytes 196612
  33.1 16.3 %copy-start.2 = (bf16[2,128,128]{2,1,0:T(8,128)(2,1)S(1)}, bf16[2,128,128]{2,1,0:T(8,128)(2,1)}, u32[]{:S(2)}) copy-start(bf16[2,128,128]{2,1,0:T(8,128)(2,1)} %w_out.5) | copy-start | bytes 196612
  66.5 3.8 %collective-permute-start.1 = (bf16[512,128]{1,0:T(8,128)(2,1)S(1)}, bf16[512,128]{1,0:T(8,128)(2,1)S(1)}, u32[]{:S(2)}, u32[]{:S(2)}) collective-permute-start(bf16[512,128]{1,0:T(8,128)(2,1)S(1)} %bitcast.36), channel_id=1, source_target_pairs={{0,16},{16,0},{1,17},{17,1},{2,18},{18,2},{3,19},{19,3},{4,20},{20... | collective-permute-start | bytes 393224 | tf_op jit(solution)/shard_map/ppermute | solution.py:372
  71.0 16.3 %copy-start.3 = (bf16[16,16,128]{2,1,0:T(8,128)(2,1)S(1)}, bf16[16,16,128]{2,1,0:T(8,128)(2,1)}, u32[]{:S(2)}) copy-start(bf16[16,16,128]{2,1,0:T(8,128)(2,1)} %param.11) | copy-start | bytes 196612
  103.9 3.9 %collective-permute-start.2 = (bf16[256,128]{1,0:T(8,128)(2,1)S(1)}, bf16[256,128]{1,0:T(8,128)(2,1)S(1)}, u32[]{:S(2)}, u32[]{:S(2)}) collective-permute-start(bf16[256,128]{1,0:T(8,128)(2,1)S(1)} %bitcast.45), channel_id=1, source_target_pairs={{0,16},{16,0},{1,17},{17,1},{2,18},{18,2},{3,19},{19,3},{4,20},{20... | collective-permute-start | bytes 196616 | tf_op jit(solution)/shard_map/ppermute | solution.py:372
  142.9 3.3 %collective-permute-start.3 = (bf16[256,128]{1,0:T(8,128)(2,1)S(1)}, bf16[256,128]{1,0:T(8,128)(2,1)S(1)}, u32[]{:S(2)}, u32[]{:S(2)}) collective-permute-start(bf16[256,128]{1,0:T(8,128)(2,1)S(1)} %bitcast.49), channel_id=1, source_target_pairs={{0,16},{16,0},{1,17},{17,1},{2,18},{18,2},{3,19},{19,3},{4,20},{20... | collective-permute-start | bytes 196616 | tf_op jit(solution)/shard_map/ppermute | solution.py:372

commit v5 on v4

--- a/solution.py
+++ b/solution.py
@@ -14,7 +14,7 @@
 EPS = 1e-05
 SIZES = {"y": 4, "zl": 2, "h": 2, "zh": 4, "x": 4}
 CHIPS = ("zh", "x", "y", "zl")
-PLANE = ("h", "x", "y")
+PLANE = ("x", "y")
 LINE = ("zl", "zh")
 
 
@@ -106,7 +106,7 @@
     )
 
 
-def prepare(z, gain, w_in, w_gate, m, n_ref, g_ref, send, send_ref, copies=()):
+def prepare(z, gain, w_in, m, n_ref, send, send_ref, copies=()):
     hat, _ = normalise(z)
     normed = (hat * gain).astype(BF16)
     n_ref[...] = normed
@@ -115,13 +115,12 @@
     p = dot(w_in[...], normed, 0, 0)
     a = m * jax.nn.sigmoid(p[0:128]) * p[128:256]
     b = m * jax.nn.sigmoid(p[256:384]) * p[384:512]
-    g_ref[...] = jax.nn.sigmoid(dot(w_gate[...], normed, 0, 0))
     channels_to_messages(a, send, 0, 4)
     channels_to_messages(b, send, 2, 4)
     send_ref[...] = send[...].astype(BF16)
 
 
-def prepare_back(recv, z, normed, gain, w_in, w_gate, m, dpg, dp):
+def project_back(recv, normed, w_in, m, dp):
     p = dot(w_in, normed, 0, 0)
     for k in range(2):
         cot = messages_to_channels(recv, 2 * k, 4) * m
@@ -129,21 +128,24 @@
         v = p[256 * k + 128 : 256 * k + 256]
         dp[256 * k : 256 * k + 128, :] = (cot * v * s * (1.0 - s)).astype(BF16)
         dp[256 * k + 128 : 256 * k + 256, :] = (cot * s).astype(BF16)
+
+
+def normed_back(dp, z, gain, w_in, w_gate, dpg):
     dn = dot(w_in, dp[...], 1, 0) + dot(w_gate, dpg, 1, 0)
     hat, rstd = normalise(z)
     return normalise_back(dn * gain, hat, rstd)
 
 
 def start_kernel(*refs):
-    hbm, (z_ref, n_ref, g_ref, m_ref, gain_ref, send_ref), refs = refs[:8], refs[8:14], refs[14:]
-    vmem, send, sem = refs[:8], refs[8], refs[9]
+    hbm, (z_ref, n_ref, m_ref, gain_ref, send_ref), refs = refs[:7], refs[7:12], refs[12:]
+    vmem, send, sem = refs[:7], refs[7], refs[8]
     copies = [
         pltpu.make_async_copy(src.at[0] if k > 5 else src, dst, sem.at[k])
         for k, (src, dst) in enumerate(zip(hbm, vmem))
     ]
     for copy in copies:
         copy.start()
-    pair, mask, chain, bias, in_gain, out_gain, w_in, w_gate = vmem
+    pair, mask, chain, bias, in_gain, out_gain, w_in = vmem
     row = (lax.axis_index("y") * 2 + lax.axis_index("zl")) * 2 + lax.axis_index("h")
     col = lax.axis_index("zh") * 4 + lax.axis_index("x")
     res = lax.broadcasted_iota(jnp.int32, (256, POS), 0)
@@ -169,17 +171,21 @@
     z = pair[...].astype(F32).T + same * column(bias[...])
     z_ref[...] = z
     gain = column(in_gain[0:1])
-    prepare(z, gain, w_in, w_gate, m8[0:1], n_ref, g_ref, send, send_ref, copies[6:])
-
-
-def middle_kernel(x_in, z0, g0, m, gains, w_in, w_gate, w_out, z_ref, y_ref, n_ref, g_ref, send_ref, xs, send):
+    prepare(z, gain, w_in, m8[0:1], n_ref, send, send_ref, copies[6:])
+
+
+def gate_kernel(u, normed, w_gate, g_ref):
+    g_ref[...] = jax.nn.sigmoid(dot(w_gate[u], normed[...], 0, 0))
+
+
+def middle_kernel(x_in, z0, g0, m, gains, w_in, w_out, z_ref, y_ref, n_ref, send_ref, xs, send):
     xs[...] = x_in[...].astype(F32)
     hat, _ = normalise(messages_to_channels(xs, 0, 2))
     y = dot(w_out[0], hat * column(gains[2:3]), 0, 0)
     y_ref[...] = y
     z = z0[...] + g0[...] * y
     z_ref[...] = z
-    prepare(z, column(gains[1:2]), w_in.at[1], w_gate.at[1], m[0:1], n_ref, g_ref, send, send_ref)
+    prepare(z, column(gains[1:2]), w_in.at[1], m[0:1], n_ref, send, send_ref)
 
 
 def turn_kernel(x_in, g1, cot_in, gains, w_out, cot_ref, y_ref, xn_ref, dy_ref, dpg_ref, send_ref, xs, send):
@@ -209,8 +215,9 @@
 
 def back_kernel(gab, n1, z1, m, dpg1, cot, x_in, g0, y0, gains, w_in, w_gate, w_out, dz_ref, dp_ref, dpg_ref, xn_ref, dy_ref, send_ref, rs, xs, send):
     rs[...] = gab[...].astype(F32)
-    dz = cot[...] + prepare_back(
-        rs, z1[...], n1[...], column(gains[1:2]), w_in[1], w_gate[1], m[0:1], dpg1[...], dp_ref
+    project_back(rs, n1[...], w_in[1], m[0:1], dp_ref)
+    dz = cot[...] + normed_back(
+        dp_ref, z1[...], column(gains[1:2]), w_in[1], w_gate[1], dpg1[...]
     )
     dz_ref[...] = dz
     g = g0[...]
@@ -235,16 +242,25 @@
     early_ref[896:1024, :] = dot(xn[...], dy[...], 1, 1).astype(BF16)
 
 
-def end_kernel(gab, n0, z0, m, dpg0, dz1, gains, w_in, w_gate, early, grad_ref, send_ref, rs, dp):
+def end_kernel(gab, n0, m, w_in, early, dp_ref, mine_ref, send_ref, rs):
     rs[...] = gab[...].astype(F32)
-    dz = dz1[...] + prepare_back(
-        rs, z0[...], n0[...], column(gains[0:1]), w_in[0], w_gate[0], m[0:1], dpg0[...], dp
-    )
+    project_back(rs, n0[...], w_in[0], m[0:1], dp_ref)
+    first = lax.axis_index("h") == 0
+    parts = [dot(n0[...], dp_ref[128 * e : 128 * (e + 1), :], 1, 1) for e in range(4)]
+    parts += [early[128 * k : 128 * (k + 1), :].astype(F32) for k in range(8)]
+    for k, (low, high) in enumerate([(0, 2), (1, 3), (4, 8), (5, 9), (6, 10), (7, 11)]):
+        block = slice(128 * k, 128 * (k + 1))
+        mine_ref[block, :] = jnp.where(first, parts[low], parts[high])
+        send_ref[block, :] = jnp.where(first, parts[high], parts[low]).astype(BF16)
+
+
+def end_rest_kernel(dp, z0, dpg0, dz1, gains, w_in, w_gate, grad_ref):
+    dz = dz1[...] + normed_back(dp, z0[...], column(gains[0:1]), w_in[0], w_gate[0], dpg0[...])
     grad_ref[...] = dz.T
-    for e in range(4):
-        part = dot(n0[...], dp[128 * e : 128 * (e + 1), :], 1, 1)
-        send_ref[128 * e : 128 * (e + 1), :] = part.astype(BF16)
-    send_ref[512:1536, :] = early[...]
+
+
+def core_sum_kernel(mine, other, send_ref):
+    send_ref[...] = (mine[...] + other[...].astype(F32)).astype(BF16)
 
 
 def sum_kernel(recv, send_ref):
@@ -256,28 +272,41 @@
         send_ref[48 * k : 48 * (k + 1), :] = total
 
 
-def place_kernel(recv, grad, in_out, gate_out, out_out, grad_out, in_ref, gate_ref, out_ref, sem):
-    copies = []
-
-    def write(src, dst):
-        copies.append(pltpu.make_async_copy(src, dst, sem.at[len(copies)]))
-        copies[-1].start()
+def place_kernel(core_of, rows, *refs):
+    in_out, gate_out, out_out, in_ref, gate_ref, out_ref, sem = refs[-7:]
 
     def block(k):
-        return recv[128 * k : 128 * (k + 1), :].astype(F32)
-
-    write(grad, grad_out)
-    for u in range(2):
+        return rows[128 * k : 128 * (k + 1), :].astype(F32)
+
+    def write(src, dst, k):
+        copy = pltpu.make_async_copy(src, dst, sem.at[k])
+        copy.start()
+        return copy
+
+    def low():
+        for e in range(2):
+            in_ref[0, :, 128 * e : 128 * (e + 1)] = block(e)
+        copies = [write(in_ref.at[0, :, 0:256], in_out.at[0, :, 0:256], 0)]
         for e in range(4):
-            in_ref[u, :, 128 * e : 128 * (e + 1)] = block(4 * u + e)
-        write(in_ref.at[u], in_out.at[u])
-    for k, u in ((8, 1), (10, 0)):
-        gate_ref[u] = block(k)
-        out_ref[u] = block(k + 1)
-    write(gate_ref, gate_out)
-    write(out_ref, out_out)
-    for copy in copies:
-        copy.wait()
+            in_ref[1, :, 128 * e : 128 * (e + 1)] = block(2 + e)
+        copies.append(write(in_ref.at[1], in_out.at[1], 1))
+        for copy in copies:
+            copy.wait()
+
+    def high():
+        for e in range(2):
+            in_ref[0, :, 128 * (2 + e) : 128 * (3 + e)] = block(e)
+        copies = [write(in_ref.at[0, :, 256:512], in_out.at[0, :, 256:512], 0)]
+        for k, u in ((2, 1), (4, 0)):
+            gate_ref[u] = block(k)
+            out_ref[u] = block(k + 1)
+        copies += [write(gate_ref, gate_out, 1), write(out_ref, out_out, 2)]
+        for copy in copies:
+            copy.wait()
+
+    is_low = lax.axis_index("h") == core_of
+    pl.when(is_low)(low)
+    pl.when(jnp.logical_not(is_low))(high)
 
 
 def outgoing_mine_kernel(mine, a_ref, b_ref, x_ref, ms, mat):
@@ -389,27 +418,30 @@
 
     operands = [
         pltpu.with_memory_space_constraint(v, pltpu.HBM)
-        for v in (pair, mask, chain, bias, in_gain, out_gain, w_in, w_gate)
+        for v in (pair, mask, chain, bias, in_gain, out_gain, w_in)
     ]
-    z0, n0, g0, m, gains, send = call(
-        start_kernel, "start", [field, field16, field, ((8, POS), F32), rows(4), rows(512, BF16)],
+    z0, n0, m, gains, send = call(
+        start_kernel, "start", [field, field16, ((8, POS), F32), rows(4), rows(512, BF16)],
         [(v.shape[1:] if k > 5 else v.shape, v.dtype) for k, v in enumerate(operands)]
-        + [rows(512), pltpu.SemaphoreType.DMA((8,))],
-        *operands, in_specs=[pl.BlockSpec(memory_space=pltpu.HBM)] * 8,
+        + [rows(512), pltpu.SemaphoreType.DMA((7,))],
+        *operands, in_specs=[pl.BlockSpec(memory_space=pltpu.HBM)] * 7,
     )
     mine = exchange(send)
     other_ab = swap_cores(mine)
     a0, b0, x_mine = call(
         outgoing_mine_kernel, "outgoing_mine", [field16, field16, square], [rows(512), work], mine
     )
+    (g0,) = call(
+        functools.partial(gate_kernel, 0), "gate0", [field], [], *after(mine, n0), w_gate
+    )
     b0_other, send = call(
         outgoing_kernel, "outgoing", [field16, rows(256, BF16)], [rows(512), work, rows(256)],
-        other_ab, a0, x_mine,
+        other_ab, a0, *after(g0, x_mine),
     )
     x0 = exchange(send)
-    z1, y0, n1, g1, send = call(
-        middle_kernel, "middle", [field, field, field16, field, rows(512, BF16)], [rows(256), rows(512)],
-        x0, z0, g0, m, gains, w_in, w_gate, w_out,
+    z1, y0, n1, send = call(
+        middle_kernel, "middle", [field, field, field16, rows(512, BF16)], [rows(256), rows(512)],
+        x0, z0, g0, m, gains, w_in, w_out,
     )
     mine = exchange(send)
     other = swap_cores(mine)
@@ -419,9 +451,12 @@
     (a0_other,) = call(
         other_rows_kernel, "other_rows", [field16], [rows(512), work], *after(mine, other_ab)
     )
+    (g1,) = call(
+        functools.partial(gate_kernel, 1), "gate1", [field], [], *after(mine, n1), w_gate
+    )
     (send,) = call(
         incoming_kernel, "incoming", [rows(256, BF16)], [rows(512), work, rows(256)],
-        other, *after(a0_other, x_mine),
+        other, *after((a0_other, g1), x_mine),
     )
     cot, y1, xn, dy, dpg1, send = call(
         turn_kernel, "turn", [field, field, field16, field16, field16, rows(256, BF16)],
@@ -458,17 +493,31 @@
         outgoing_back_kernel, "outgoing_back", [rows(512, BF16)], [rows(256), work, rows(512)],
         other, *after(early, ga, gb), a0_other,
     )
-    pair_grad, send = call(
-        end_kernel, "end", [rows(POS), rows(1536, BF16)],
-        [rows(512), ((512, POS), BF16)],
-        exchange(send), n0, z0, m, dpg0, dz1, gains, w_in, w_gate, early,
+    dp0, mine, send = call(
+        end_kernel, "end", [((512, POS), BF16), rows(768), rows(768, BF16)], [rows(512)],
+        exchange(send), n0, m, w_in, early,
+    )
+    other = swap_cores(send)
+    (pair_grad,) = call(
+        end_rest_kernel, "end_rest", [rows(POS)], [], dp0, z0, dpg0, dz1, gains, w_in, w_gate
+    )
+    (send,) = call(
+        core_sum_kernel, "core_sum", [rows(768, BF16)], [], *after(pair_grad, mine), other
     )
     (send,) = call(sum_kernel, "plane_sum", [rows(384, BF16)], [], exchange(send, PLANE))
-    (send,) = call(sum_kernel, "line_sum", [rows(1536, BF16)], [], exchange(send, LINE))
+    (send,) = call(sum_kernel, "line_sum", [rows(768, BF16)], [], exchange(send, LINE))
+    mine = exchange(send, PLANE)
     weights = [((2, 128, 512), F32), ((2, 128, 128), F32), ((2, 128, 128), F32)]
-    in_grad, gate_grad, out_grad, pair_grad = call(
-        place_kernel, "place", weights + [rows(POS)], weights + [pltpu.SemaphoreType.DMA((5,))],
-        exchange(send, PLANE), pair_grad, out_specs=[pl.BlockSpec(memory_space=pltpu.HBM)] * 4,
+    hbm = [pl.BlockSpec(memory_space=pltpu.HBM)] * 3
+    scratch = weights + [pltpu.SemaphoreType.DMA((3,))]
+    other = swap_cores(mine)
+    grads = call(
+        functools.partial(place_kernel, 0), "place_mine", weights, scratch, mine, out_specs=hbm
+    )
+    in_grad, gate_grad, out_grad = call(
+        functools.partial(place_kernel, 1), "place_other", weights, scratch, other, *grads,
+        in_specs=[pl.BlockSpec(memory_space=pltpu.VMEM)] + hbm, out_specs=hbm,
+        input_output_aliases={1: 0, 2: 1, 3: 2},
     )
     return (new_pair.reshape(block), pair_grad.reshape(block), in_grad, gate_grad, out_grad)
 

time: 205 us -> 204 us (level)
  blocking collectives: 182 us -> 173 us
  starting transfers between devices: 9.86 us -> 15.1 us
    all_to_all x11, blocking collectives: 182 us -> 173 us  [exchange(): return lax.all_to_all(value, axes, 0, 0, tiled=True)]
    ppermute x4 -> x6, starting transfers between devices: 9.86 us -> 15.1 us  [swap_cores(): return lax.ppermute(value, 'h', [(0, 1), (1, 0)])]
    pallas_call x19 -> x24, Pallas kernels: 11 us -> 12.9 us  [call(): pl.pallas_call(kernel, name=name, out_shape=[jax.ShapeDtypeStruct(s, d) f...]
  transfers between devices with their start and end apart: 4 -> 6, of which waited for: 2 -> 2; matrix products, arithmetic and copies ran while one was open for 0% -> 0% of each run, Pallas kernels for 2% -> 3%
where the time goes in v5:
time: 204 us; the launch traced here: 203 us
  blocking collectives  173 us (85%)
  starting transfers between devices  15.1 us (7%)
  Pallas kernels  12.9 us (6%)
    all_to_all x11, blocking collectives, exchange(): return lax.all_to_all(value, axes, 0, 0, tiled=True)  173 us
    ppermute x6, starting transfers between devices, swap_cores(): return lax.ppermute(value, 'h', [(0, 1), (1, 0)])  15.1 us
    pallas_call x24, Pallas kernels, call(): pl.pallas_call(kernel, name=name, out_shape=[jax.ShapeDtypeStruct(s, d) f...  12.9 us
  transfers between devices with their start and end apart: 6, of which 2 were waited for; matrix products, arithmetic and copies ran while one was open for 0% of the time, Pallas kernels for 3%

profile of v5, /device:TPU:1, one launch (start us, length us, event | category | flops | bytes accessed | tf_op | source)
XLA Modules:
  0.0 203.0 jit_solution(14007275689675242980)
XLA Ops:
  0.6 1.4 start.1
  2.1 27.3 %all_to_all.121 = bf16[128,4,128]{2,1,0:T(4,128)(2,1)S(1)} all-to-all(bf16[128,4,128]{2,1,0:T(4,128)(2,1)S(1)} %bitcast.52), channel_id=1, replica_groups=mesh['y'=4,'zl'=2,'h'=2,'zh'=4,'x'=4] {'zh','x','y','zl'}, dimensions={0} | all-to-all | bytes 262144 | tf_op jit(solution)/shard_map/all_to_all | solution.py:397
  29.3 2.0 %collective-permute-start = (bf16[512,128]{1,0:T(8,128)(2,1)S(1)}, bf16[512,128]{1,0:T(8,128)(2,1)S(1)}, u32[]{:S(2)}, u32[]{:S(2)}) collective-permute-start(bf16[512,128]{1,0:T(8,128)(2,1)S(1)} %bitcast.39), channel_id=1, source_target_pairs={{0,16},{16,0},{1,17},{17,1},{2,18},{18,2},{3,19},{19,3},{4,20},{20... | collective-permute-start | bytes 393224 | tf_op jit(solution)/shard_map/ppermute | solution.py:401
  33.1 16.3 %all_to_all.122 = bf16[128,2,128]{2,1,0:T(2,128)(2,1)S(1)} all-to-all(bf16[128,2,128]{2,1,0:T(2,128)(2,1)S(1)} %bitcast.57), channel_id=1, replica_groups=mesh['y'=4,'zl'=2,'h'=2,'zh'=4,'x'=4] {'zh','x','y','zl'}, dimensions={0} | all-to-all | bytes 131072 | tf_op jit(solution)/shard_map/all_to_all | solution.py:397
  50.0 16.6 %all_to_all.123 = bf16[128,4,128]{2,1,0:T(4,128)(2,1)S(1)} all-to-all(bf16[128,4,128]{2,1,0:T(4,128)(2,1)S(1)} %bitcast.53), channel_id=1, replica_groups=mesh['y'=4,'zl'=2,'h'=2,'zh'=4,'x'=4] {'zh','x','y','zl'}, dimensions={0} | all-to-all | bytes 262144 | tf_op jit(solution)/shard_map/all_to_all | solution.py:397
  66.6 2.6 %collective-permute-start.1 = (bf16[512,128]{1,0:T(8,128)(2,1)S(1)}, bf16[512,128]{1,0:T(8,128)(2,1)S(1)}, u32[]{:S(2)}, u32[]{:S(2)}) collective-permute-start(bf16[512,128]{1,0:T(8,128)(2,1)S(1)} %bitcast.37), channel_id=1, source_target_pairs={{0,16},{16,0},{1,17},{17,1},{2,18},{18,2},{3,19},{19,3},{4,20},{20... | collective-permute-start | bytes 393224 | tf_op jit(solution)/shard_map/ppermute | solution.py:401
  70.2 0.8 incoming.1
  71.0 16.2 %all_to_all.124 = bf16[128,2,128]{2,1,0:T(2,128)(2,1)S(1)} all-to-all(bf16[128,2,128]{2,1,0:T(2,128)(2,1)S(1)} %bitcast.49), channel_id=1, replica_groups=mesh['y'=4,'zl'=2,'h'=2,'zh'=4,'x'=4] {'zh','x','y','zl'}, dimensions={0} | all-to-all | bytes 131072 | tf_op jit(solution)/shard_map/all_to_all | solution.py:397
  87.5 16.3 %all_to_all.125 = bf16[128,2,128]{2,1,0:T(2,128)(2,1)S(1)} all-to-all(bf16[128,2,128]{2,1,0:T(2,128)(2,1)S(1)} %bitcast.56), channel_id=1, replica_groups=mesh['y'=4,'zl'=2,'h'=2,'zh'=4,'x'=4] {'zh','x','y','zl'}, dimensions={0} | all-to-all | bytes 131072 | tf_op jit(solution)/shard_map/all_to_all | solution.py:397
  103.8 2.7 %collective-permute-start.2 = (bf16[256,128]{1,0:T(8,128)(2,1)S(1)}, bf16[256,128]{1,0:T(8,128)(2,1)S(1)}, u32[]{:S(2)}, u32[]{:S(2)}) collective-permute-start(bf16[256,128]{1,0:T(8,128)(2,1)S(1)} %bitcast.46), channel_id=1, source_target_pairs={{0,16},{16,0},{1,17},{17,1},{2,18},{18,2},{3,19},{19,3},{4,20},{20... | collective-permute-start | bytes 196616 | tf_op jit(solution)/shard_map/ppermute | solution.py:401
  107.0 0.8 turn_rest.1
  107.7 0.8 incoming_back.1
  108.5 17.4 %all_to_all.126 = bf16[128,4,128]{2,1,0:T(4,128)(2,1)S(1)} all-to-all(bf16[128,4,128]{2,1,0:T(4,128)(2,1)S(1)} %bitcast.42), channel_id=1, replica_groups=mesh['y'=4,'zl'=2,'h'=2,'zh'=4,'x'=4] {'zh','x','y','zl'}, dimensions={0} | all-to-all | bytes 262144 | tf_op jit(solution)/shard_map/all_to_all | solution.py:397
  126.7 16.2 %all_to_all.127 = bf16[128,2,128]{2,1,0:T(2,128)(2,1)S(1)} all-to-all(bf16[128,2,128]{2,1,0:T(2,128)(2,1)S(1)} %bitcast.55), channel_id=1, replica_groups=mesh['y'=4,'zl'=2,'h'=2,'zh'=4,'x'=4] {'zh','x','y','zl'}, dimensions={0} | all-to-all | bytes 131072 | tf_op jit(solution)/shard_map/all_to_all | solution.py:397
  142.9 2.3 %collective-permute-start.3 = (bf16[256,128]{1,0:T(8,128)(2,1)S(1)}, bf16[256,128]{1,0:T(8,128)(2,1)S(1)}, u32[]{:S(2)}, u32[]{:S(2)}) collective-permute-start(bf16[256,128]{1,0:T(8,128)(2,1)S(1)} %bitcast.50), channel_id=1, source_target_pairs={{0,16},{16,0},{1,17},{17,1},{2,18},{18,2},{3,19},{19,3},{4,20},{20... | collective-permute-start | bytes 196616 | tf_op jit(solution)/shard_map/ppermute | solution.py:401
  146.9 17.1 %all_to_all.128 = bf16[128,4,128]{2,1,0:T(4,128)(2,1)S(1)} all-to-all(bf16[128,4,128]{2,1,0:T(4,128)(2,1)S(1)} %bitcast.43), channel_id=1, replica_groups=mesh['y'=4,'zl'=2,'h'=2,'zh'=4,'x'=4] {'zh','x','y','zl'}, dimensions={0} | all-to-all | bytes 262144 | tf_op jit(solution)/shard_map/all_to_all | solution.py:397
  164.6 1.6 collective-permute-start.4
  166.2 1.0 end_rest.1
  167.3 10.0 %all_to_all.129 = bf16[16,48,128]{2,1,0:T(8,128)(2,1)S(1)} all-to-all(bf16[16,48,128]{2,1,0:T(8,128)(2,1)S(1)} %bitcast.33), channel_id=1, replica_groups=mesh['y'=4,'zl'=2,'h'=2,'zh'=4,'x'=4] {'x','y'}, dimensions={0} | all-to-all | bytes 393216 | tf_op jit(solution)/shard_map/all_to_all | solution.py:397
  177.4 9.3 %all_to_all.130 = bf16[8,48,128]{2,1,0:T(8,128)(2,1)S(1)} all-to-all(bf16[8,48,128]{2,1,0:T(8,128)(2,1)S(1)} %bitcast.44), channel_id=1, replica_groups=mesh['y'=4,'zl'=2,'h'=2,'zh'=4,'x'=4] {'zl','zh'}, dimensions={0} | all-to-all | bytes 196608 | tf_op jit(solution)/shard_map/all_to_all | solution.py:397
  186.7 10.4 %all_to_all.131 = bf16[16,48,128]{2,1,0:T(8,128)(2,1)S(1)} all-to-all(bf16[16,48,128]{2,1,0:T(8,128)(2,1)S(1)} %bitcast.32), channel_id=1, replica_groups=mesh['y'=4,'zl'=2,'h'=2,'zh'=4,'x'=4] {'x','y'}, dimensions={0} | all-to-all | bytes 393216 | tf_op jit(solution)/shard_map/all_to_all | solution.py:397
  197.1 3.8 %collective-permute-start.5 = (bf16[768,128]{1,0:T(8,128)(2,1)S(1)}, bf16[768,128]{1,0:T(8,128)(2,1)S(1)}, u32[]{:S(2)}, u32[]{:S(2)}) collective-permute-start(bf16[768,128]{1,0:T(8,128)(2,1)S(1)} %bitcast.29), channel_id=1, source_target_pairs={{0,16},{16,0},{1,17},{17,1},{2,18},{18,2},{3,19},{19,3},{4,20},{20... | collective-permute-start | bytes 589832 | tf_op jit(solution)/shard_map/ppermute | solution.py:401
  200.9 0.8 place_mine.1
  202.0 0.8 place_other.1
  (31 shorter events, 7.5 us)
Async XLA Ops:
  29.3 3.1 %collective-permute-start = (bf16[512,128]{1,0:T(8,128)(2,1)S(1)}, bf16[512,128]{1,0:T(8,128)(2,1)S(1)}, u32[]{:S(2)}, u32[]{:S(2)}) collective-permute-start(bf16[512,128]{1,0:T(8,128)(2,1)S(1)} %bitcast.39), channel_id=1, source_target_pairs={{0,16},{16,0},{1,17},{17,1},{2,18},{18,2},{3,19},{19,3},{4,20},{20... | collective-permute-start | bytes 393224 | tf_op jit(solution)/shard_map/ppermute | solution.py:401
  31.4 0.8 copy-start.1
  32.4 17.0 %copy-start = (bf16[2,128,512]{2,1,0:T(8,128)(2,1)S(1)}, bf16[2,128,512]{2,1,0:T(8,128)(2,1)}, u32[]{:S(2)}) copy-start(bf16[2,128,512]{2,1,0:T(8,128)(2,1)} %w_in.7) | copy-start | bytes 786436
  33.1 16.3 %copy-start.2 = (bf16[2,128,128]{2,1,0:T(8,128)(2,1)S(1)}, bf16[2,128,128]{2,1,0:T(8,128)(2,1)}, u32[]{:S(2)}) copy-start(bf16[2,128,128]{2,1,0:T(8,128)(2,1)} %w_out.5) | copy-start | bytes 196612
  66.6 3.6 %collective-permute-start.1 = (bf16[512,128]{1,0:T(8,128)(2,1)S(1)}, bf16[512,128]{1,0:T(8,128)(2,1)S(1)}, u32[]{:S(2)}, u32[]{:S(2)}) collective-permute-start(bf16[512,128]{1,0:T(8,128)(2,1)S(1)} %bitcast.37), channel_id=1, source_target_pairs={{0,16},{16,0},{1,17},{17,1},{2,18},{18,2},{3,19},{19,3},{4,20},{20... | collective-permute-start | bytes 393224 | tf_op jit(solution)/shard_map/ppermute | solution.py:401
  70.9 16.3 %copy-start.3 = (bf16[16,16,128]{2,1,0:T(8,128)(2,1)S(1)}, bf16[16,16,128]{2,1,0:T(8,128)(2,1)}, u32[]{:S(2)}) copy-start(bf16[16,16,128]{2,1,0:T(8,128)(2,1)} %param.11) | copy-start | bytes 196612
  103.8 3.9 %collective-permute-start.2 = (bf16[256,128]{1,0:T(8,128)(2,1)S(1)}, bf16[256,128]{1,0:T(8,128)(2,1)S(1)}, u32[]{:S(2)}, u32[]{:S(2)}) collective-permute-start(bf16[256,128]{1,0:T(8,128)(2,1)S(1)} %bitcast.46), channel_id=1, source_target_pairs={{0,16},{16,0},{1,17},{17,1},{2,18},{18,2},{3,19},{19,3},{4,20},{20... | collective-permute-start | bytes 196616 | tf_op jit(solution)/shard_map/ppermute | solution.py:401
  142.9 3.3 %collective-permute-start.3 = (bf16[256,128]{1,0:T(8,128)(2,1)S(1)}, bf16[256,128]{1,0:T(8,128)(2,1)S(1)}, u32[]{:S(2)}, u32[]{:S(2)}) collective-permute-start(bf16[256,128]{1,0:T(8,128)(2,1)S(1)} %bitcast.50), channel_id=1, source_target_pairs={{0,16},{16,0},{1,17},{17,1},{2,18},{18,2},{3,19},{19,3},{4,20},{20... | collective-permute-start | bytes 196616 | tf_op jit(solution)/shard_map/ppermute | solution.py:401
  164.6 2.7 %collective-permute-start.4 = (bf16[768,128]{1,0:T(8,128)(2,1)S(1)}, bf16[768,128]{1,0:T(8,128)(2,1)S(1)}, u32[]{:S(2)}, u32[]{:S(2)}) collective-permute-start(bf16[768,128]{1,0:T(8,128)(2,1)S(1)} %get-tuple-element.134), channel_id=1, source_target_pairs={{0,16},{16,0},{1,17},{17,1},{2,18},{18,2},{3,19},{19,3},{4,20},{20... | collective-permute-start | bytes 589832 | tf_op jit(solution)/shard_map/ppermute | solution.py:401
  197.1 4.9 %collective-permute-start.5 = (bf16[768,128]{1,0:T(8,128)(2,1)S(1)}, bf16[768,128]{1,0:T(8,128)(2,1)S(1)}, u32[]{:S(2)}, u32[]{:S(2)}) collective-permute-start(bf16[768,128]{1,0:T(8,128)(2,1)S(1)} %bitcast.29), channel_id=1, source_target_pairs={{0,16},{16,0},{1,17},{17,1},{2,18},{18,2},{3,19},{19,3},{4,20},{20... | collective-permute-start | bytes 589832 | tf_op jit(solution)/shard_map/ppermute | solution.py:401

commit v6 on v5

--- a/solution.py
+++ b/solution.py
@@ -26,26 +26,33 @@
 
 def swap_blocks(tiles):
     block = lax.broadcasted_iota(jnp.int32, tiles[0].shape, 1) // 16
-    for d in (1, 2, 4):
-        high = (block & d) != 0
-        out = list(tiles)
-        for t in range(8):
-            if t & d == 0:
-                lo, hi = tiles[t], tiles[t | d]
-                out[t] = jnp.where(high, pltpu.roll(hi, 16 * d, 1), lo)
-                out[t | d] = jnp.where(high, hi, pltpu.roll(lo, 128 - 16 * d, 1))
-        tiles = out
-    return tiles
+    high = block >= 4
+    out = list(tiles)
+    for t in range(4):
+        lo, hi = tiles[t], tiles[t + 4]
+        crossed = pltpu.roll(jnp.where(high, lo, hi), 64, 1)
+        out[t] = jnp.where(high, crossed, lo)
+        out[t + 4] = jnp.where(high, hi, crossed)
+    tiles, out = out, []
+    for i in range(8):
+        value = tiles[i]
+        for t in range(4):
+            if t != i % 4:
+                moved = pltpu.roll(tiles[i - i % 4 + t], 16 * (t - i % 4) % 128, 1)
+                value = jnp.where(block % 4 == t, moved, value)
+        out.append(value)
+    return out
 
 
 def messages_to_half(src, off, w, dst):
     for half in range(2):
-        for p in range(2):
-            tiles = [
-                src[pl.ds((2 * t + p) * 8 * w + off + half, 8, stride=w), :] for t in range(8)
-            ]
-            for t, tile in enumerate(swap_blocks(tiles)):
-                dst[p, pl.ds(half * 8 + t, 8, stride=16), :] = tile
+        tiles = [
+            src[pl.ds(16 * t * w + off + half, 16, stride=w), :].astype(BF16) for t in range(8)
+        ]
+        for t, tile in enumerate(swap_blocks(tiles)):
+            tile = tile.astype(F32)
+            for p in range(2):
+                dst[p, pl.ds(half * 8 + t, 8, stride=16), :] = tile[8 * p : 8 * (p + 1)]
     return jnp.concatenate([dst[0], dst[1]], axis=1).astype(BF16)
 
 
@@ -53,10 +60,12 @@
     for p in range(2):
         src[p] = value[p]
     for half in range(2):
-        for p in range(2):
-            tiles = [src[p, pl.ds(half * 8 + t, 8, stride=16), :] for t in range(8)]
-            for t, tile in enumerate(swap_blocks(tiles)):
-                dst[pl.ds((2 * t + p) * 8 * w + off + half, 8, stride=w), :] = tile
+        tiles = []
+        for t in range(8):
+            both = [src[p, pl.ds(half * 8 + t, 8, stride=16), :] for p in range(2)]
+            tiles.append(jnp.concatenate(both, axis=0).astype(BF16))
+        for t, tile in enumerate(swap_blocks(tiles)):
+            dst[pl.ds(16 * t * w + off + half, 16, stride=w), :] = tile.astype(F32)
 
 
 def halves(value):
@@ -120,14 +129,12 @@
     send_ref[...] = send[...].astype(BF16)
 
 
-def project_back(recv, normed, w_in, m, dp):
-    p = dot(w_in, normed, 0, 0)
+def project_back(recv, factors, dp):
     for k in range(2):
-        cot = messages_to_channels(recv, 2 * k, 4) * m
-        s = jax.nn.sigmoid(p[256 * k : 256 * k + 128])
-        v = p[256 * k + 128 : 256 * k + 256]
-        dp[256 * k : 256 * k + 128, :] = (cot * v * s * (1.0 - s)).astype(BF16)
-        dp[256 * k + 128 : 256 * k + 256, :] = (cot * s).astype(BF16)
+        cot = messages_to_channels(recv, 2 * k, 4)
+        for e in range(2 * k, 2 * k + 2):
+            block = slice(128 * e, 128 * (e + 1))
+            dp[block, :] = (cot * factors[block, :]).astype(BF16)
 
 
 def normed_back(dp, z, gain, w_in, w_gate, dpg):
@@ -137,15 +144,15 @@
 
 
 def start_kernel(*refs):
-    hbm, (z_ref, n_ref, m_ref, gain_ref, send_ref), refs = refs[:7], refs[7:12], refs[12:]
-    vmem, send, sem = refs[:7], refs[7], refs[8]
+    hbm, (z_ref, n_ref, m_ref, gain_ref, w_in, w_gate, send_ref), refs = refs[:8], refs[8:15], refs[15:]
+    vmem, send, sem = refs[:6] + (w_in, w_gate), refs[6], refs[7]
     copies = [
         pltpu.make_async_copy(src.at[0] if k > 5 else src, dst, sem.at[k])
         for k, (src, dst) in enumerate(zip(hbm, vmem))
     ]
     for copy in copies:
         copy.start()
-    pair, mask, chain, bias, in_gain, out_gain, w_in = vmem
+    pair, mask, chain, bias, in_gain, out_gain = vmem[:6]
     row = (lax.axis_index("y") * 2 + lax.axis_index("zl")) * 2 + lax.axis_index("h")
     col = lax.axis_index("zh") * 4 + lax.axis_index("x")
     res = lax.broadcasted_iota(jnp.int32, (256, POS), 0)
@@ -171,14 +178,23 @@
     z = pair[...].astype(F32).T + same * column(bias[...])
     z_ref[...] = z
     gain = column(in_gain[0:1])
-    prepare(z, gain, w_in, m8[0:1], n_ref, send, send_ref, copies[6:])
-
-
-def gate_kernel(u, normed, w_gate, g_ref):
-    g_ref[...] = jax.nn.sigmoid(dot(w_gate[u], normed[...], 0, 0))
-
-
-def middle_kernel(x_in, z0, g0, m, gains, w_in, w_out, z_ref, y_ref, n_ref, send_ref, xs, send):
+    prepare(z, gain, w_in, m8[0:1], n_ref, send, send_ref, copies[6:7])
+    copies[7].wait()
+
+
+def side_kernel(normed, m, w_in, w_gate, g_ref, factor_ref):
+    p = dot(w_in[...], normed[...], 0, 0)
+    for k in range(2):
+        s = jax.nn.sigmoid(p[256 * k : 256 * k + 128])
+        ms = m[0:1] * s
+        factor_ref[256 * k : 256 * k + 128, :] = ms * (1.0 - s) * p[256 * k + 128 : 256 * k + 256]
+        factor_ref[256 * k + 128 : 256 * k + 256, :] = ms
+    g_ref[...] = jax.nn.sigmoid(dot(w_gate[...], normed[...], 0, 0))
+
+
+def middle_kernel(x_in, z0, g0, m, gains, w_in, w_gate, w_out, z_ref, y_ref, n_ref, w_in_ref, w_gate_ref, send_ref, xs, send):
+    w_in_ref[...] = w_in[1]
+    w_gate_ref[...] = w_gate[1]
     xs[...] = x_in[...].astype(F32)
     hat, _ = normalise(messages_to_channels(xs, 0, 2))
     y = dot(w_out[0], hat * column(gains[2:3]), 0, 0)
@@ -213,9 +229,9 @@
     gw_ref[128:256, :] = dot(xn[...], dy[...], 1, 1).astype(BF16)
 
 
-def back_kernel(gab, n1, z1, m, dpg1, cot, x_in, g0, y0, gains, w_in, w_gate, w_out, dz_ref, dp_ref, dpg_ref, xn_ref, dy_ref, send_ref, rs, xs, send):
+def back_kernel(gab, factors, z1, dpg1, cot, x_in, g0, y0, gains, w_in, w_gate, w_out, dz_ref, dp_ref, dpg_ref, xn_ref, dy_ref, send_ref, rs, xs, send):
     rs[...] = gab[...].astype(F32)
-    project_back(rs, n1[...], w_in[1], m[0:1], dp_ref)
+    project_back(rs, factors, dp_ref)
     dz = cot[...] + normed_back(
         dp_ref, z1[...], column(gains[1:2]), w_in[1], w_gate[1], dpg1[...]
     )
@@ -242,9 +258,9 @@
     early_ref[896:1024, :] = dot(xn[...], dy[...], 1, 1).astype(BF16)
 
 
-def end_kernel(gab, n0, m, w_in, early, dp_ref, mine_ref, send_ref, rs):
+def end_kernel(gab, factors, n0, early, dp_ref, mine_ref, send_ref, rs):
     rs[...] = gab[...].astype(F32)
-    project_back(rs, n0[...], w_in[0], m[0:1], dp_ref)
+    project_back(rs, factors, dp_ref)
     first = lax.axis_index("h") == 0
     parts = [dot(n0[...], dp_ref[128 * e : 128 * (e + 1), :], 1, 1) for e in range(4)]
     parts += [early[128 * k : 128 * (k + 1), :].astype(F32) for k in range(8)]
@@ -418,30 +434,31 @@
 
     operands = [
         pltpu.with_memory_space_constraint(v, pltpu.HBM)
-        for v in (pair, mask, chain, bias, in_gain, out_gain, w_in)
+        for v in (pair, mask, chain, bias, in_gain, out_gain, w_in, w_gate)
     ]
-    z0, n0, m, gains, send = call(
-        start_kernel, "start", [field, field16, ((8, POS), F32), rows(4), rows(512, BF16)],
-        [(v.shape[1:] if k > 5 else v.shape, v.dtype) for k, v in enumerate(operands)]
-        + [rows(512), pltpu.SemaphoreType.DMA((7,))],
-        *operands, in_specs=[pl.BlockSpec(memory_space=pltpu.HBM)] * 7,
+    z0, n0, m, gains, w_in0, w_gate0, send = call(
+        start_kernel, "start",
+        [field, field16, ((8, POS), F32), rows(4), ((128, 512), BF16), rows(128, BF16), rows(512, BF16)],
+        [(v.shape, v.dtype) for v in operands[:6]] + [rows(512), pltpu.SemaphoreType.DMA((8,))],
+        *operands, in_specs=[pl.BlockSpec(memory_space=pltpu.HBM)] * 8,
     )
     mine = exchange(send)
     other_ab = swap_cores(mine)
     a0, b0, x_mine = call(
         outgoing_mine_kernel, "outgoing_mine", [field16, field16, square], [rows(512), work], mine
     )
-    (g0,) = call(
-        functools.partial(gate_kernel, 0), "gate0", [field], [], *after(mine, n0), w_gate
+    factors = ((512, POS), F32)
+    g0, factors0 = call(
+        side_kernel, "side0", [field, factors], [], *after(mine, n0), m, w_in0, w_gate0
     )
     b0_other, send = call(
         outgoing_kernel, "outgoing", [field16, rows(256, BF16)], [rows(512), work, rows(256)],
         other_ab, a0, *after(g0, x_mine),
     )
     x0 = exchange(send)
-    z1, y0, n1, send = call(
-        middle_kernel, "middle", [field, field, field16, rows(512, BF16)], [rows(256), rows(512)],
-        x0, z0, g0, m, gains, w_in, w_out,
+    z1, y0, n1, w_in1, w_gate1, send = call(
+        middle_kernel, "middle", [field, field, field16, ((128, 512), BF16), rows(128, BF16), rows(512, BF16)],
+        [rows(256), rows(512)], x0, z0, g0, m, gains, w_in, w_gate, w_out,
     )
     mine = exchange(send)
     other = swap_cores(mine)
@@ -451,8 +468,8 @@
     (a0_other,) = call(
         other_rows_kernel, "other_rows", [field16], [rows(512), work], *after(mine, other_ab)
     )
-    (g1,) = call(
-        functools.partial(gate_kernel, 1), "gate1", [field], [], *after(mine, n1), w_gate
+    g1, factors1 = call(
+        side_kernel, "side1", [field, factors], [], *after(mine, n1), m, w_in1, w_gate1
     )
     (send,) = call(
         incoming_kernel, "incoming", [rows(256, BF16)], [rows(512), work, rows(256)],
@@ -478,7 +495,7 @@
     dz1, dp1, dpg0, xn, dy, send = call(
         back_kernel, "back", [field, ((512, POS), BF16), field16, field16, field16, rows(256, BF16)],
         [rows(512), rows(256), rows(256)],
-        exchange(send), n1, z1, m, dpg1, cot, x0, g0, y0, gains, w_in, w_gate, w_out,
+        exchange(send), factors1, z1, dpg1, cot, x0, g0, y0, gains, w_in, w_gate, w_out,
     )
     mine = exchange(send)
     other = swap_cores(mine)
@@ -495,7 +512,7 @@
     )
     dp0, mine, send = call(
         end_kernel, "end", [((512, POS), BF16), rows(768), rows(768, BF16)], [rows(512)],
-        exchange(send), n0, m, w_in, early,
+        exchange(send), factors0, n0, early,
     )
     other = swap_cores(send)
     (pair_grad,) = call(

time: 204 us -> 203 us (level)
  transfers between devices with their start and end apart: 6 -> 6, of which waited for: 2 -> 3; matrix products, arithmetic and copies ran while one was open for 0% -> 0% of each run, Pallas kernels for 3% -> 3%
where the time goes in v6:
time: 203 us; the launch traced here: 202 us
  blocking collectives  173 us (85%)
  starting transfers between devices  15.4 us (8%)
  Pallas kernels  12.1 us (6%)
    all_to_all x11, blocking collectives, exchange(): return lax.all_to_all(value, axes, 0, 0, tiled=True)  173 us
    ppermute x6, starting transfers between devices, swap_cores(): return lax.ppermute(value, 'h', [(0, 1), (1, 0)])  15.4 us
    pallas_call x24, Pallas kernels, call(): pl.pallas_call(kernel, name=name, out_shape=[jax.ShapeDtypeStruct(s, d) f...  12.1 us
  transfers between devices with their start and end apart: 6, of which 3 were waited for; matrix products, arithmetic and copies ran while one was open for 0% of the time, Pallas kernels for 3%

profile of v6, /device:TPU:1, one launch (start us, length us, event | category | flops | bytes accessed | tf_op | source)
XLA Modules:
  0.0 202.1 jit_solution(11131684324352662005)
XLA Ops:
  0.6 1.4 start.1
  2.1 27.2 %all_to_all.121 = bf16[128,4,128]{2,1,0:T(4,128)(2,1)S(1)} all-to-all(bf16[128,4,128]{2,1,0:T(4,128)(2,1)S(1)} %bitcast.52), channel_id=1, replica_groups=mesh['y'=4,'zl'=2,'h'=2,'zh'=4,'x'=4] {'zh','x','y','zl'}, dimensions={0} | all-to-all | bytes 262144 | tf_op jit(solution)/shard_map/all_to_all | solution.py:413
  29.3 2.0 %collective-permute-start = (bf16[512,128]{1,0:T(8,128)(2,1)S(1)}, bf16[512,128]{1,0:T(8,128)(2,1)S(1)}, u32[]{:S(2)}, u32[]{:S(2)}) collective-permute-start(bf16[512,128]{1,0:T(8,128)(2,1)S(1)} %bitcast.39), channel_id=1, source_target_pairs={{0,16},{16,0},{1,17},{17,1},{2,18},{18,2},{3,19},{19,3},{4,20},{20... | collective-permute-start | bytes 393224 | tf_op jit(solution)/shard_map/ppermute | solution.py:417
  33.0 16.2 %all_to_all.122 = bf16[128,2,128]{2,1,0:T(2,128)(2,1)S(1)} all-to-all(bf16[128,2,128]{2,1,0:T(2,128)(2,1)S(1)} %bitcast.57), channel_id=1, replica_groups=mesh['y'=4,'zl'=2,'h'=2,'zh'=4,'x'=4] {'zh','x','y','zl'}, dimensions={0} | all-to-all | bytes 131072 | tf_op jit(solution)/shard_map/all_to_all | solution.py:413
  49.8 16.6 %all_to_all.123 = bf16[128,4,128]{2,1,0:T(4,128)(2,1)S(1)} all-to-all(bf16[128,4,128]{2,1,0:T(4,128)(2,1)S(1)} %bitcast.53), channel_id=1, replica_groups=mesh['y'=4,'zl'=2,'h'=2,'zh'=4,'x'=4] {'zh','x','y','zl'}, dimensions={0} | all-to-all | bytes 262144 | tf_op jit(solution)/shard_map/all_to_all | solution.py:413
  66.4 2.8 %collective-permute-start.1 = (bf16[512,128]{1,0:T(8,128)(2,1)S(1)}, bf16[512,128]{1,0:T(8,128)(2,1)S(1)}, u32[]{:S(2)}, u32[]{:S(2)}) collective-permute-start(bf16[512,128]{1,0:T(8,128)(2,1)S(1)} %bitcast.37), channel_id=1, source_target_pairs={{0,16},{16,0},{1,17},{17,1},{2,18},{18,2},{3,19},{19,3},{4,20},{20... | collective-permute-start | bytes 393224 | tf_op jit(solution)/shard_map/ppermute | solution.py:417
  70.2 0.7 incoming.1
  70.9 16.3 %all_to_all.124 = bf16[128,2,128]{2,1,0:T(2,128)(2,1)S(1)} all-to-all(bf16[128,2,128]{2,1,0:T(2,128)(2,1)S(1)} %bitcast.49), channel_id=1, replica_groups=mesh['y'=4,'zl'=2,'h'=2,'zh'=4,'x'=4] {'zh','x','y','zl'}, dimensions={0} | all-to-all | bytes 131072 | tf_op jit(solution)/shard_map/all_to_all | solution.py:413
  87.4 16.3 %all_to_all.125 = bf16[128,2,128]{2,1,0:T(2,128)(2,1)S(1)} all-to-all(bf16[128,2,128]{2,1,0:T(2,128)(2,1)S(1)} %bitcast.56), channel_id=1, replica_groups=mesh['y'=4,'zl'=2,'h'=2,'zh'=4,'x'=4] {'zh','x','y','zl'}, dimensions={0} | all-to-all | bytes 131072 | tf_op jit(solution)/shard_map/all_to_all | solution.py:413
  103.7 2.7 %collective-permute-start.2 = (bf16[256,128]{1,0:T(8,128)(2,1)S(1)}, bf16[256,128]{1,0:T(8,128)(2,1)S(1)}, u32[]{:S(2)}, u32[]{:S(2)}) collective-permute-start(bf16[256,128]{1,0:T(8,128)(2,1)S(1)} %bitcast.46), channel_id=1, source_target_pairs={{0,16},{16,0},{1,17},{17,1},{2,18},{18,2},{3,19},{19,3},{4,20},{20... | collective-permute-start | bytes 196616 | tf_op jit(solution)/shard_map/ppermute | solution.py:417
  106.9 0.8 turn_rest.1
  107.7 0.7 incoming_back.1
  108.3 17.5 %all_to_all.126 = bf16[128,4,128]{2,1,0:T(4,128)(2,1)S(1)} all-to-all(bf16[128,4,128]{2,1,0:T(4,128)(2,1)S(1)} %bitcast.41), channel_id=1, replica_groups=mesh['y'=4,'zl'=2,'h'=2,'zh'=4,'x'=4] {'zh','x','y','zl'}, dimensions={0} | all-to-all | bytes 262144 | tf_op jit(solution)/shard_map/all_to_all | solution.py:413
  126.4 16.1 %all_to_all.127 = bf16[128,2,128]{2,1,0:T(2,128)(2,1)S(1)} all-to-all(bf16[128,2,128]{2,1,0:T(2,128)(2,1)S(1)} %bitcast.55), channel_id=1, replica_groups=mesh['y'=4,'zl'=2,'h'=2,'zh'=4,'x'=4] {'zh','x','y','zl'}, dimensions={0} | all-to-all | bytes 131072 | tf_op jit(solution)/shard_map/all_to_all | solution.py:413
  142.5 2.3 %collective-permute-start.3 = (bf16[256,128]{1,0:T(8,128)(2,1)S(1)}, bf16[256,128]{1,0:T(8,128)(2,1)S(1)}, u32[]{:S(2)}, u32[]{:S(2)}) collective-permute-start(bf16[256,128]{1,0:T(8,128)(2,1)S(1)} %bitcast.50), channel_id=1, source_target_pairs={{0,16},{16,0},{1,17},{17,1},{2,18},{18,2},{3,19},{19,3},{4,20},{20... | collective-permute-start | bytes 196616 | tf_op jit(solution)/shard_map/ppermute | solution.py:417
  146.4 17.1 %all_to_all.128 = bf16[128,4,128]{2,1,0:T(4,128)(2,1)S(1)} all-to-all(bf16[128,4,128]{2,1,0:T(4,128)(2,1)S(1)} %bitcast.42), channel_id=1, replica_groups=mesh['y'=4,'zl'=2,'h'=2,'zh'=4,'x'=4] {'zh','x','y','zl'}, dimensions={0} | all-to-all | bytes 262144 | tf_op jit(solution)/shard_map/all_to_all | solution.py:413
  163.8 1.6 collective-permute-start.4
  165.4 1.0 end_rest.1
  166.5 10.0 %all_to_all.129 = bf16[16,48,128]{2,1,0:T(8,128)(2,1)S(1)} all-to-all(bf16[16,48,128]{2,1,0:T(8,128)(2,1)S(1)} %bitcast.33), channel_id=1, replica_groups=mesh['y'=4,'zl'=2,'h'=2,'zh'=4,'x'=4] {'x','y'}, dimensions={0} | all-to-all | bytes 393216 | tf_op jit(solution)/shard_map/all_to_all | solution.py:413
  176.5 9.3 %all_to_all.130 = bf16[8,48,128]{2,1,0:T(8,128)(2,1)S(1)} all-to-all(bf16[8,48,128]{2,1,0:T(8,128)(2,1)S(1)} %bitcast.44), channel_id=1, replica_groups=mesh['y'=4,'zl'=2,'h'=2,'zh'=4,'x'=4] {'zl','zh'}, dimensions={0} | all-to-all | bytes 196608 | tf_op jit(solution)/shard_map/all_to_all | solution.py:413
  185.9 10.4 %all_to_all.131 = bf16[16,48,128]{2,1,0:T(8,128)(2,1)S(1)} all-to-all(bf16[16,48,128]{2,1,0:T(8,128)(2,1)S(1)} %bitcast.32), channel_id=1, replica_groups=mesh['y'=4,'zl'=2,'h'=2,'zh'=4,'x'=4] {'x','y'}, dimensions={0} | all-to-all | bytes 393216 | tf_op jit(solution)/shard_map/all_to_all | solution.py:413
  196.3 3.8 %collective-permute-start.5 = (bf16[768,128]{1,0:T(8,128)(2,1)S(1)}, bf16[768,128]{1,0:T(8,128)(2,1)S(1)}, u32[]{:S(2)}, u32[]{:S(2)}) collective-permute-start(bf16[768,128]{1,0:T(8,128)(2,1)S(1)} %bitcast.29), channel_id=1, source_target_pairs={{0,16},{16,0},{1,17},{17,1},{2,18},{18,2},{3,19},{19,3},{4,20},{20... | collective-permute-start | bytes 589832 | tf_op jit(solution)/shard_map/ppermute | solution.py:417
  200.1 0.8 place_mine.1
  201.2 0.8 place_other.1
  (31 shorter events, 6.6 us)
Async XLA Ops:
  29.3 3.0 %collective-permute-start = (bf16[512,128]{1,0:T(8,128)(2,1)S(1)}, bf16[512,128]{1,0:T(8,128)(2,1)S(1)}, u32[]{:S(2)}, u32[]{:S(2)}) collective-permute-start(bf16[512,128]{1,0:T(8,128)(2,1)S(1)} %bitcast.39), channel_id=1, source_target_pairs={{0,16},{16,0},{1,17},{17,1},{2,18},{18,2},{3,19},{19,3},{4,20},{20... | collective-permute-start | bytes 393224 | tf_op jit(solution)/shard_map/ppermute | solution.py:417
  32.1 17.1 %copy-start = (bf16[2,128,512]{2,1,0:T(8,128)(2,1)S(1)}, bf16[2,128,512]{2,1,0:T(8,128)(2,1)}, u32[]{:S(2)}) copy-start(bf16[2,128,512]{2,1,0:T(8,128)(2,1)} %w_in.5) | copy-start | bytes 786436
  33.0 16.3 %copy-start.1 = (bf16[2,128,128]{2,1,0:T(8,128)(2,1)S(1)}, bf16[2,128,128]{2,1,0:T(8,128)(2,1)}, u32[]{:S(2)}) copy-start(bf16[2,128,128]{2,1,0:T(8,128)(2,1)} %w_gate.5) | copy-start | bytes 196612
  33.0 16.3 %copy-start.2 = (bf16[2,128,128]{2,1,0:T(8,128)(2,1)S(1)}, bf16[2,128,128]{2,1,0:T(8,128)(2,1)}, u32[]{:S(2)}) copy-start(bf16[2,128,128]{2,1,0:T(8,128)(2,1)} %w_out.5) | copy-start | bytes 196612
  66.4 3.8 %collective-permute-start.1 = (bf16[512,128]{1,0:T(8,128)(2,1)S(1)}, bf16[512,128]{1,0:T(8,128)(2,1)S(1)}, u32[]{:S(2)}, u32[]{:S(2)}) collective-permute-start(bf16[512,128]{1,0:T(8,128)(2,1)S(1)} %bitcast.37), channel_id=1, source_target_pairs={{0,16},{16,0},{1,17},{17,1},{2,18},{18,2},{3,19},{19,3},{4,20},{20... | collective-permute-start | bytes 393224 | tf_op jit(solution)/shard_map/ppermute | solution.py:417
  70.8 16.3 %copy-start.3 = (bf16[16,16,128]{2,1,0:T(8,128)(2,1)S(1)}, bf16[16,16,128]{2,1,0:T(8,128)(2,1)}, u32[]{:S(2)}) copy-start(bf16[16,16,128]{2,1,0:T(8,128)(2,1)} %param.11) | copy-start | bytes 196612
  103.7 3.9 %collective-permute-start.2 = (bf16[256,128]{1,0:T(8,128)(2,1)S(1)}, bf16[256,128]{1,0:T(8,128)(2,1)S(1)}, u32[]{:S(2)}, u32[]{:S(2)}) collective-permute-start(bf16[256,128]{1,0:T(8,128)(2,1)S(1)} %bitcast.46), channel_id=1, source_target_pairs={{0,16},{16,0},{1,17},{17,1},{2,18},{18,2},{3,19},{19,3},{4,20},{20... | collective-permute-start | bytes 196616 | tf_op jit(solution)/shard_map/ppermute | solution.py:417
  142.5 3.3 %collective-permute-start.3 = (bf16[256,128]{1,0:T(8,128)(2,1)S(1)}, bf16[256,128]{1,0:T(8,128)(2,1)S(1)}, u32[]{:S(2)}, u32[]{:S(2)}) collective-permute-start(bf16[256,128]{1,0:T(8,128)(2,1)S(1)} %bitcast.50), channel_id=1, source_target_pairs={{0,16},{16,0},{1,17},{17,1},{2,18},{18,2},{3,19},{19,3},{4,20},{20... | collective-permute-start | bytes 196616 | tf_op jit(solution)/shard_map/ppermute | solution.py:417
  163.8 2.7 %collective-permute-start.4 = (bf16[768,128]{1,0:T(8,128)(2,1)S(1)}, bf16[768,128]{1,0:T(8,128)(2,1)S(1)}, u32[]{:S(2)}, u32[]{:S(2)}) collective-permute-start(bf16[768,128]{1,0:T(8,128)(2,1)S(1)} %get-tuple-element.150), channel_id=1, source_target_pairs={{0,16},{16,0},{1,17},{17,1},{2,18},{18,2},{3,19},{19,3},{4,20},{20... | collective-permute-start | bytes 589832 | tf_op jit(solution)/shard_map/ppermute | solution.py:417
  196.3 4.9 %collective-permute-start.5 = (bf16[768,128]{1,0:T(8,128)(2,1)S(1)}, bf16[768,128]{1,0:T(8,128)(2,1)S(1)}, u32[]{:S(2)}, u32[]{:S(2)}) collective-permute-start(bf16[768,128]{1,0:T(8,128)(2,1)S(1)} %bitcast.29), channel_id=1, source_target_pairs={{0,16},{16,0},{1,17},{17,1},{2,18},{18,2},{3,19},{19,3},{4,20},{20... | collective-permute-start | bytes 589832 | tf_op jit(solution)/shard_map/ppermute | solution.py:417

commit v7 on v6

--- a/solution.py
+++ b/solution.py
@@ -116,7 +116,7 @@
 
 
 def prepare(z, gain, w_in, m, n_ref, send, send_ref, copies=()):
-    hat, _ = normalise(z)
+    hat, rstd = normalise(z)
     normed = (hat * gain).astype(BF16)
     n_ref[...] = normed
     for copy in copies:
@@ -127,6 +127,7 @@
     channels_to_messages(a, send, 0, 4)
     channels_to_messages(b, send, 2, 4)
     send_ref[...] = send[...].astype(BF16)
+    return hat, rstd
 
 
 def project_back(recv, factors, dp):
@@ -137,9 +138,8 @@
             dp[block, :] = (cot * factors[block, :]).astype(BF16)
 
 
-def normed_back(dp, z, gain, w_in, w_gate, dpg):
+def normed_back(dp, hat, rstd, gain, w_in, w_gate, dpg):
     dn = dot(w_in, dp[...], 1, 0) + dot(w_gate, dpg, 1, 0)
-    hat, rstd = normalise(z)
     return normalise_back(dn * gain, hat, rstd)
 
 
@@ -192,21 +192,32 @@
     g_ref[...] = jax.nn.sigmoid(dot(w_gate[...], normed[...], 0, 0))
 
 
-def middle_kernel(x_in, z0, g0, m, gains, w_in, w_gate, w_out, z_ref, y_ref, n_ref, w_in_ref, w_gate_ref, send_ref, xs, send):
+def columns_kernel(gains, col_ref):
+    for k in range(4):
+        col_ref[k] = column(gains[k : k + 1])
+
+
+def middle_kernel(x_in, z0, g0, m, gains, w_in, w_gate, w_out, z_ref, y_ref, n_ref, w_in_ref, w_gate_ref, hats_ref, rstd_ref, xn_ref, send_ref, xs, send):
     w_in_ref[...] = w_in[1]
     w_gate_ref[...] = w_gate[1]
     xs[...] = x_in[...].astype(F32)
-    hat, _ = normalise(messages_to_channels(xs, 0, 2))
-    y = dot(w_out[0], hat * column(gains[2:3]), 0, 0)
+    hat, rstd = normalise(messages_to_channels(xs, 0, 2))
+    xn = (hat * gains[2]).astype(BF16)
+    y = dot(w_out[0], xn, 0, 0)
     y_ref[...] = y
     z = z0[...] + g0[...] * y
     z_ref[...] = z
-    prepare(z, column(gains[1:2]), w_in.at[1], m[0:1], n_ref, send, send_ref)
+    hats_ref[0] = hat
+    xn_ref[...] = xn
+    rstd_ref[0:8, :] = jnp.broadcast_to(rstd, (8, POS))
+    hat, rstd = prepare(z, gains[1], w_in.at[1], m[0:1], n_ref, send, send_ref)
+    hats_ref[1] = hat
+    rstd_ref[8:16, :] = jnp.broadcast_to(rstd, (8, POS))
 
 
 def turn_kernel(x_in, g1, cot_in, gains, w_out, cot_ref, y_ref, xn_ref, dy_ref, dpg_ref, send_ref, xs, send):
     xs[...] = x_in[...].astype(F32)
-    gain = column(gains[3:4])
+    gain = gains[3]
     hat, rstd = normalise(messages_to_channels(xs, 0, 2))
     xn = (hat * gain).astype(BF16)
     xn_ref[...] = xn
@@ -229,22 +240,18 @@
     gw_ref[128:256, :] = dot(xn[...], dy[...], 1, 1).astype(BF16)
 
 
-def back_kernel(gab, factors, z1, dpg1, cot, x_in, g0, y0, gains, w_in, w_gate, w_out, dz_ref, dp_ref, dpg_ref, xn_ref, dy_ref, send_ref, rs, xs, send):
+def back_kernel(gab, factors, hats, rstds, dpg1, cot, g0, y0, gains, w_in, w_gate, w_out, dz_ref, dp_ref, dpg_ref, dy_ref, send_ref, rs, send):
     rs[...] = gab[...].astype(F32)
     project_back(rs, factors, dp_ref)
     dz = cot[...] + normed_back(
-        dp_ref, z1[...], column(gains[1:2]), w_in[1], w_gate[1], dpg1[...]
+        dp_ref, hats[1], rstds[8:9], gains[1], w_in[1], w_gate[1], dpg1[...]
     )
     dz_ref[...] = dz
     g = g0[...]
     dpg_ref[...] = (dz * y0[...] * g * (1.0 - g)).astype(BF16)
     dy = (dz * g).astype(BF16)
     dy_ref[...] = dy
-    xs[...] = x_in[...].astype(F32)
-    gain = column(gains[2:3])
-    hat, rstd = normalise(messages_to_channels(xs, 0, 2))
-    xn_ref[...] = (hat * gain).astype(BF16)
-    gx = normalise_back(dot(w_out[0], dy, 1, 0) * gain, hat, rstd)
+    gx = normalise_back(dot(w_out[0], dy, 1, 0) * gains[2], hats[0], rstds[0:1])
     channels_to_messages(gx, send, 0, 2)
     send_ref[...] = send[...].astype(BF16)
 
@@ -271,7 +278,9 @@
 
 
 def end_rest_kernel(dp, z0, dpg0, dz1, gains, w_in, w_gate, grad_ref):
-    dz = dz1[...] + normed_back(dp, z0[...], column(gains[0:1]), w_in[0], w_gate[0], dpg0[...])
+    dz = dz1[...] + normed_back(
+        dp, *normalise(z0[...]), gains[0], w_in[0], w_gate[0], dpg0[...]
+    )
     grad_ref[...] = dz.T
 
 
@@ -451,13 +460,15 @@
     g0, factors0 = call(
         side_kernel, "side0", [field, factors], [], *after(mine, n0), m, w_in0, w_gate0
     )
+    (gains,) = call(columns_kernel, "columns", [((4, CH, POS), F32)], [], *after(mine, gains))
     b0_other, send = call(
         outgoing_kernel, "outgoing", [field16, rows(256, BF16)], [rows(512), work, rows(256)],
-        other_ab, a0, *after(g0, x_mine),
+        other_ab, a0, *after((g0, gains), x_mine),
     )
     x0 = exchange(send)
-    z1, y0, n1, w_in1, w_gate1, send = call(
-        middle_kernel, "middle", [field, field, field16, ((128, 512), BF16), rows(128, BF16), rows(512, BF16)],
+    z1, y0, n1, w_in1, w_gate1, hats, rstds, xn0, send = call(
+        middle_kernel, "middle", [field, field, field16, ((128, 512), BF16), rows(128, BF16), ((2, CH, POS), F32), ((16, POS), F32),
+         field16, rows(512, BF16)],
         [rows(256), rows(512)], x0, z0, g0, m, gains, w_in, w_gate, w_out,
     )
     mine = exchange(send)
@@ -492,10 +503,10 @@
         incoming_back_kernel, "incoming_back", [rows(512, BF16)], [rows(256), work, rows(512)],
         other, a1, b1, *after(gw1, ga, gb),
     )
-    dz1, dp1, dpg0, xn, dy, send = call(
-        back_kernel, "back", [field, ((512, POS), BF16), field16, field16, field16, rows(256, BF16)],
-        [rows(512), rows(256), rows(256)],
-        exchange(send), factors1, z1, dpg1, cot, x0, g0, y0, gains, w_in, w_gate, w_out,
+    dz1, dp1, dpg0, dy, send = call(
+        back_kernel, "back", [field, ((512, POS), BF16), field16, field16, rows(256, BF16)],
+        [rows(512), rows(256)],
+        exchange(send), factors1, hats, rstds, dpg1, cot, g0, y0, gains, w_in, w_gate, w_out,
     )
     mine = exchange(send)
     other = swap_cores(mine)
@@ -504,7 +515,7 @@
         [rows(256), work, rows(256)], mine, a0, b0, b0_other,
     )
     (early,) = call(
-        back_rest_kernel, "back_rest", [rows(1024, BF16)], [], *after(mine, n1, dp1, gw1, n0, dpg0, xn, dy)
+        back_rest_kernel, "back_rest", [rows(1024, BF16)], [], *after(mine, n1, dp1, gw1, n0, dpg0, xn0, dy)
     )
     (send,) = call(
         outgoing_back_kernel, "outgoing_back", [rows(512, BF16)], [rows(256), work, rows(512)],

time: 203 us -> 203 us (level)
    pallas_call x24 -> x25, Pallas kernels: 12.1 us -> 12.2 us  [call(): pl.pallas_call(kernel, name=name, out_shape=[jax.ShapeDtypeStruct(s, d) f...]
where the time goes in v7:
time: 203 us; the launch traced here: 202 us
  blocking collectives  173 us (85%)
  starting transfers between devices  15.4 us (8%)
  Pallas kernels  12.2 us (6%)
    all_to_all x11, blocking collectives, exchange(): return lax.all_to_all(value, axes, 0, 0, tiled=True)  173 us
    ppermute x6, starting transfers between devices, swap_cores(): return lax.ppermute(value, 'h', [(0, 1), (1, 0)])  15.4 us
    pallas_call x25, Pallas kernels, call(): pl.pallas_call(kernel, name=name, out_shape=[jax.ShapeDtypeStruct(s, d) f...  12.2 us
  transfers between devices with their start and end apart: 6, of which 3 were waited for; matrix products, arithmetic and copies ran while one was open for 0% of the time, Pallas kernels for 3%

profile of v7, /device:TPU:1, one launch (start us, length us, event | category | flops | bytes accessed | tf_op | source)
XLA Modules:
  0.0 202.1 jit_solution(17488079796194253871)
XLA Ops:
  0.6 1.4 start.1
  2.1 27.2 %all_to_all.121 = bf16[128,4,128]{2,1,0:T(4,128)(2,1)S(1)} all-to-all(bf16[128,4,128]{2,1,0:T(4,128)(2,1)S(1)} %bitcast.52), channel_id=1, replica_groups=mesh['y'=4,'zl'=2,'h'=2,'zh'=4,'x'=4] {'zh','x','y','zl'}, dimensions={0} | all-to-all | bytes 262144 | tf_op jit(solution)/shard_map/all_to_all | solution.py:422
  29.3 2.0 %collective-permute-start = (bf16[512,128]{1,0:T(8,128)(2,1)S(1)}, bf16[512,128]{1,0:T(8,128)(2,1)S(1)}, u32[]{:S(2)}, u32[]{:S(2)}) collective-permute-start(bf16[512,128]{1,0:T(8,128)(2,1)S(1)} %bitcast.38), channel_id=1, source_target_pairs={{0,16},{16,0},{1,17},{17,1},{2,18},{18,2},{3,19},{19,3},{4,20},{20... | collective-permute-start | bytes 393224 | tf_op jit(solution)/shard_map/ppermute | solution.py:426
  33.0 16.2 %all_to_all.122 = bf16[128,2,128]{2,1,0:T(2,128)(2,1)S(1)} all-to-all(bf16[128,2,128]{2,1,0:T(2,128)(2,1)S(1)} %bitcast.55), channel_id=1, replica_groups=mesh['y'=4,'zl'=2,'h'=2,'zh'=4,'x'=4] {'zh','x','y','zl'}, dimensions={0} | all-to-all | bytes 131072 | tf_op jit(solution)/shard_map/all_to_all | solution.py:422
  49.8 16.6 %all_to_all.123 = bf16[128,4,128]{2,1,0:T(4,128)(2,1)S(1)} all-to-all(bf16[128,4,128]{2,1,0:T(4,128)(2,1)S(1)} %bitcast.51), channel_id=1, replica_groups=mesh['y'=4,'zl'=2,'h'=2,'zh'=4,'x'=4] {'zh','x','y','zl'}, dimensions={0} | all-to-all | bytes 262144 | tf_op jit(solution)/shard_map/all_to_all | solution.py:422
  66.4 2.8 %collective-permute-start.1 = (bf16[512,128]{1,0:T(8,128)(2,1)S(1)}, bf16[512,128]{1,0:T(8,128)(2,1)S(1)}, u32[]{:S(2)}, u32[]{:S(2)}) collective-permute-start(bf16[512,128]{1,0:T(8,128)(2,1)S(1)} %bitcast.36), channel_id=1, source_target_pairs={{0,16},{16,0},{1,17},{17,1},{2,18},{18,2},{3,19},{19,3},{4,20},{20... | collective-permute-start | bytes 393224 | tf_op jit(solution)/shard_map/ppermute | solution.py:426
  70.1 0.7 incoming.1
  70.8 16.3 %all_to_all.124 = bf16[128,2,128]{2,1,0:T(2,128)(2,1)S(1)} all-to-all(bf16[128,2,128]{2,1,0:T(2,128)(2,1)S(1)} %bitcast.47), channel_id=1, replica_groups=mesh['y'=4,'zl'=2,'h'=2,'zh'=4,'x'=4] {'zh','x','y','zl'}, dimensions={0} | all-to-all | bytes 131072 | tf_op jit(solution)/shard_map/all_to_all | solution.py:422
  87.4 16.3 %all_to_all.125 = bf16[128,2,128]{2,1,0:T(2,128)(2,1)S(1)} all-to-all(bf16[128,2,128]{2,1,0:T(2,128)(2,1)S(1)} %bitcast.54), channel_id=1, replica_groups=mesh['y'=4,'zl'=2,'h'=2,'zh'=4,'x'=4] {'zh','x','y','zl'}, dimensions={0} | all-to-all | bytes 131072 | tf_op jit(solution)/shard_map/all_to_all | solution.py:422
  103.7 2.7 %collective-permute-start.2 = (bf16[256,128]{1,0:T(8,128)(2,1)S(1)}, bf16[256,128]{1,0:T(8,128)(2,1)S(1)}, u32[]{:S(2)}, u32[]{:S(2)}) collective-permute-start(bf16[256,128]{1,0:T(8,128)(2,1)S(1)} %bitcast.44), channel_id=1, source_target_pairs={{0,16},{16,0},{1,17},{17,1},{2,18},{18,2},{3,19},{19,3},{4,20},{20... | collective-permute-start | bytes 196616 | tf_op jit(solution)/shard_map/ppermute | solution.py:426
  106.8 0.8 turn_rest.1
  107.6 0.7 incoming_back.1
  108.3 17.5 %all_to_all.126 = bf16[128,4,128]{2,1,0:T(4,128)(2,1)S(1)} all-to-all(bf16[128,4,128]{2,1,0:T(4,128)(2,1)S(1)} %bitcast.40), channel_id=1, replica_groups=mesh['y'=4,'zl'=2,'h'=2,'zh'=4,'x'=4] {'zh','x','y','zl'}, dimensions={0} | all-to-all | bytes 262144 | tf_op jit(solution)/shard_map/all_to_all | solution.py:422
  126.3 16.1 %all_to_all.127 = bf16[128,2,128]{2,1,0:T(2,128)(2,1)S(1)} all-to-all(bf16[128,2,128]{2,1,0:T(2,128)(2,1)S(1)} %bitcast.53), channel_id=1, replica_groups=mesh['y'=4,'zl'=2,'h'=2,'zh'=4,'x'=4] {'zh','x','y','zl'}, dimensions={0} | all-to-all | bytes 131072 | tf_op jit(solution)/shard_map/all_to_all | solution.py:422
  142.4 2.4 %collective-permute-start.3 = (bf16[256,128]{1,0:T(8,128)(2,1)S(1)}, bf16[256,128]{1,0:T(8,128)(2,1)S(1)}, u32[]{:S(2)}, u32[]{:S(2)}) collective-permute-start(bf16[256,128]{1,0:T(8,128)(2,1)S(1)} %bitcast.48), channel_id=1, source_target_pairs={{0,16},{16,0},{1,17},{17,1},{2,18},{18,2},{3,19},{19,3},{4,20},{20... | collective-permute-start | bytes 196616 | tf_op jit(solution)/shard_map/ppermute | solution.py:426
  146.3 17.1 %all_to_all.128 = bf16[128,4,128]{2,1,0:T(4,128)(2,1)S(1)} all-to-all(bf16[128,4,128]{2,1,0:T(4,128)(2,1)S(1)} %bitcast.41), channel_id=1, replica_groups=mesh['y'=4,'zl'=2,'h'=2,'zh'=4,'x'=4] {'zh','x','y','zl'}, dimensions={0} | all-to-all | bytes 262144 | tf_op jit(solution)/shard_map/all_to_all | solution.py:422
  163.7 1.6 collective-permute-start.4
  165.3 1.0 end_rest.1
  166.4 10.0 %all_to_all.129 = bf16[16,48,128]{2,1,0:T(8,128)(2,1)S(1)} all-to-all(bf16[16,48,128]{2,1,0:T(8,128)(2,1)S(1)} %bitcast.33), channel_id=1, replica_groups=mesh['y'=4,'zl'=2,'h'=2,'zh'=4,'x'=4] {'x','y'}, dimensions={0} | all-to-all | bytes 393216 | tf_op jit(solution)/shard_map/all_to_all | solution.py:422
  176.5 9.3 %all_to_all.130 = bf16[8,48,128]{2,1,0:T(8,128)(2,1)S(1)} all-to-all(bf16[8,48,128]{2,1,0:T(8,128)(2,1)S(1)} %bitcast.42), channel_id=1, replica_groups=mesh['y'=4,'zl'=2,'h'=2,'zh'=4,'x'=4] {'zl','zh'}, dimensions={0} | all-to-all | bytes 196608 | tf_op jit(solution)/shard_map/all_to_all | solution.py:422
  185.8 10.4 %all_to_all.131 = bf16[16,48,128]{2,1,0:T(8,128)(2,1)S(1)} all-to-all(bf16[16,48,128]{2,1,0:T(8,128)(2,1)S(1)} %bitcast.32), channel_id=1, replica_groups=mesh['y'=4,'zl'=2,'h'=2,'zh'=4,'x'=4] {'x','y'}, dimensions={0} | all-to-all | bytes 393216 | tf_op jit(solution)/shard_map/all_to_all | solution.py:422
  196.2 3.8 %collective-permute-start.5 = (bf16[768,128]{1,0:T(8,128)(2,1)S(1)}, bf16[768,128]{1,0:T(8,128)(2,1)S(1)}, u32[]{:S(2)}, u32[]{:S(2)}) collective-permute-start(bf16[768,128]{1,0:T(8,128)(2,1)S(1)} %bitcast.29), channel_id=1, source_target_pairs={{0,16},{16,0},{1,17},{17,1},{2,18},{18,2},{3,19},{19,3},{4,20},{20... | collective-permute-start | bytes 589832 | tf_op jit(solution)/shard_map/ppermute | solution.py:426
  200.1 0.8 place_mine.1
  201.1 0.8 place_other.1
  (32 shorter events, 6.6 us)
Async XLA Ops:
  29.3 3.0 %collective-permute-start = (bf16[512,128]{1,0:T(8,128)(2,1)S(1)}, bf16[512,128]{1,0:T(8,128)(2,1)S(1)}, u32[]{:S(2)}, u32[]{:S(2)}) collective-permute-start(bf16[512,128]{1,0:T(8,128)(2,1)S(1)} %bitcast.38), channel_id=1, source_target_pairs={{0,16},{16,0},{1,17},{17,1},{2,18},{18,2},{3,19},{19,3},{4,20},{20... | collective-permute-start | bytes 393224 | tf_op jit(solution)/shard_map/ppermute | solution.py:426
  32.3 17.0 %copy-start = (bf16[2,128,512]{2,1,0:T(8,128)(2,1)S(1)}, bf16[2,128,512]{2,1,0:T(8,128)(2,1)}, u32[]{:S(2)}) copy-start(bf16[2,128,512]{2,1,0:T(8,128)(2,1)} %w_in.5) | copy-start | bytes 786436
  33.0 16.3 %copy-start.1 = (bf16[2,128,128]{2,1,0:T(8,128)(2,1)S(1)}, bf16[2,128,128]{2,1,0:T(8,128)(2,1)}, u32[]{:S(2)}) copy-start(bf16[2,128,128]{2,1,0:T(8,128)(2,1)} %w_gate.5) | copy-start | bytes 196612
  33.0 16.3 %copy-start.2 = (bf16[2,128,128]{2,1,0:T(8,128)(2,1)S(1)}, bf16[2,128,128]{2,1,0:T(8,128)(2,1)}, u32[]{:S(2)}) copy-start(bf16[2,128,128]{2,1,0:T(8,128)(2,1)} %w_out.5) | copy-start | bytes 196612
  66.4 3.8 %collective-permute-start.1 = (bf16[512,128]{1,0:T(8,128)(2,1)S(1)}, bf16[512,128]{1,0:T(8,128)(2,1)S(1)}, u32[]{:S(2)}, u32[]{:S(2)}) collective-permute-start(bf16[512,128]{1,0:T(8,128)(2,1)S(1)} %bitcast.36), channel_id=1, source_target_pairs={{0,16},{16,0},{1,17},{17,1},{2,18},{18,2},{3,19},{19,3},{4,20},{20... | collective-permute-start | bytes 393224 | tf_op jit(solution)/shard_map/ppermute | solution.py:426
  70.8 16.3 %copy-start.3 = (bf16[16,16,128]{2,1,0:T(8,128)(2,1)S(1)}, bf16[16,16,128]{2,1,0:T(8,128)(2,1)}, u32[]{:S(2)}) copy-start(bf16[16,16,128]{2,1,0:T(8,128)(2,1)} %param.11) | copy-start | bytes 196612
  103.7 3.9 %collective-permute-start.2 = (bf16[256,128]{1,0:T(8,128)(2,1)S(1)}, bf16[256,128]{1,0:T(8,128)(2,1)S(1)}, u32[]{:S(2)}, u32[]{:S(2)}) collective-permute-start(bf16[256,128]{1,0:T(8,128)(2,1)S(1)} %bitcast.44), channel_id=1, source_target_pairs={{0,16},{16,0},{1,17},{17,1},{2,18},{18,2},{3,19},{19,3},{4,20},{20... | collective-permute-start | bytes 196616 | tf_op jit(solution)/shard_map/ppermute | solution.py:426
  142.4 3.3 %collective-permute-start.3 = (bf16[256,128]{1,0:T(8,128)(2,1)S(1)}, bf16[256,128]{1,0:T(8,128)(2,1)S(1)}, u32[]{:S(2)}, u32[]{:S(2)}) collective-permute-start(bf16[256,128]{1,0:T(8,128)(2,1)S(1)} %bitcast.48), channel_id=1, source_target_pairs={{0,16},{16,0},{1,17},{17,1},{2,18},{18,2},{3,19},{19,3},{4,20},{20... | collective-permute-start | bytes 196616 | tf_op jit(solution)/shard_map/ppermute | solution.py:426
  163.7 2.7 %collective-permute-start.4 = (bf16[768,128]{1,0:T(8,128)(2,1)S(1)}, bf16[768,128]{1,0:T(8,128)(2,1)S(1)}, u32[]{:S(2)}, u32[]{:S(2)}) collective-permute-start(bf16[768,128]{1,0:T(8,128)(2,1)S(1)} %get-tuple-element.156), channel_id=1, source_target_pairs={{0,16},{16,0},{1,17},{17,1},{2,18},{18,2},{3,19},{19,3},{4,20},{20... | collective-permute-start | bytes 589832 | tf_op jit(solution)/shard_map/ppermute | solution.py:426
  196.2 4.9 %collective-permute-start.5 = (bf16[768,128]{1,0:T(8,128)(2,1)S(1)}, bf16[768,128]{1,0:T(8,128)(2,1)S(1)}, u32[]{:S(2)}, u32[]{:S(2)}) collective-permute-start(bf16[768,128]{1,0:T(8,128)(2,1)S(1)} %bitcast.29), channel_id=1, source_target_pairs={{0,16},{16,0},{1,17},{17,1},{2,18},{18,2},{3,19},{19,3},{4,20},{20... | collective-permute-start | bytes 589832 | tf_op jit(solution)/shard_map/ppermute | solution.py:426

commit v8 on v7

--- a/solution.py
+++ b/solution.py
@@ -297,41 +297,27 @@
         send_ref[48 * k : 48 * (k + 1), :] = total
 
 
-def place_kernel(core_of, rows, *refs):
-    in_out, gate_out, out_out, in_ref, gate_ref, out_ref, sem = refs[-7:]
+def place_kernel(rows, in_out, gate_out, out_out, in_ref, gate_ref, out_ref, sem):
+    copies = []
+
+    def write(src, dst):
+        copies.append(pltpu.make_async_copy(src, dst, sem.at[len(copies)]))
+        copies[-1].start()
 
     def block(k):
         return rows[128 * k : 128 * (k + 1), :].astype(F32)
 
-    def write(src, dst, k):
-        copy = pltpu.make_async_copy(src, dst, sem.at[k])
-        copy.start()
-        return copy
-
-    def low():
-        for e in range(2):
-            in_ref[0, :, 128 * e : 128 * (e + 1)] = block(e)
-        copies = [write(in_ref.at[0, :, 0:256], in_out.at[0, :, 0:256], 0)]
-        for e in range(4):
-            in_ref[1, :, 128 * e : 128 * (e + 1)] = block(2 + e)
-        copies.append(write(in_ref.at[1], in_out.at[1], 1))
-        for copy in copies:
-            copy.wait()
-
-    def high():
-        for e in range(2):
-            in_ref[0, :, 128 * (2 + e) : 128 * (3 + e)] = block(e)
-        copies = [write(in_ref.at[0, :, 256:512], in_out.at[0, :, 256:512], 0)]
-        for k, u in ((2, 1), (4, 0)):
-            gate_ref[u] = block(k)
-            out_ref[u] = block(k + 1)
-        copies += [write(gate_ref, gate_out, 1), write(out_ref, out_out, 2)]
-        for copy in copies:
-            copy.wait()
-
-    is_low = lax.axis_index("h") == core_of
-    pl.when(is_low)(low)
-    pl.when(jnp.logical_not(is_low))(high)
+    for u, blocks in enumerate(((0, 1, 6, 7), (2, 3, 4, 5))):
+        for e, k in enumerate(blocks):
+            in_ref[u, :, 128 * e : 128 * (e + 1)] = block(k)
+        write(in_ref.at[u], in_out.at[u])
+    for k, u in ((8, 1), (10, 0)):
+        gate_ref[u] = block(k)
+        out_ref[u] = block(k + 1)
+    write(gate_ref, gate_out)
+    write(out_ref, out_out)
+    for copy in copies:
+        copy.wait()
 
 
 def outgoing_mine_kernel(mine, a_ref, b_ref, x_ref, ms, mat):
@@ -533,19 +519,11 @@
         core_sum_kernel, "core_sum", [rows(768, BF16)], [], *after(pair_grad, mine), other
     )
     (send,) = call(sum_kernel, "plane_sum", [rows(384, BF16)], [], exchange(send, PLANE))
-    (send,) = call(sum_kernel, "line_sum", [rows(768, BF16)], [], exchange(send, LINE))
-    mine = exchange(send, PLANE)
+    (send,) = call(sum_kernel, "line_sum", [rows(1536, BF16)], [], exchange(send, LINE))
     weights = [((2, 128, 512), F32), ((2, 128, 128), F32), ((2, 128, 128), F32)]
-    hbm = [pl.BlockSpec(memory_space=pltpu.HBM)] * 3
-    scratch = weights + [pltpu.SemaphoreType.DMA((3,))]
-    other = swap_cores(mine)
-    grads = call(
-        functools.partial(place_kernel, 0), "place_mine", weights, scratch, mine, out_specs=hbm
-    )
     in_grad, gate_grad, out_grad = call(
-        functools.partial(place_kernel, 1), "place_other", weights, scratch, other, *grads,
-        in_specs=[pl.BlockSpec(memory_space=pltpu.VMEM)] + hbm, out_specs=hbm,
-        input_output_aliases={1: 0, 2: 1, 3: 2},
+        place_kernel, "place", weights, weights + [pltpu.SemaphoreType.DMA((4,))],
+        exchange(send, ("h",) + PLANE), out_specs=[pl.BlockSpec(memory_space=pltpu.HBM)] * 3,
     )
     return (new_pair.reshape(block), pair_grad.reshape(block), in_grad, gate_grad, out_grad)
 

time: 203 us -> 204 us (level)
  blocking collectives: 173 us -> 179 us
  starting transfers between devices: 15.4 us -> 11.5 us
    all_to_all x11, blocking collectives: 173 us -> 179 us  [exchange(): return lax.all_to_all(value, axes, 0, 0, tiled=True)]
    ppermute x6 -> x5, starting transfers between devices: 15.4 us -> 11.5 us  [swap_cores(): return lax.ppermute(value, 'h', [(0, 1), (1, 0)])]
    pallas_call x25 -> x24, Pallas kernels: 12.2 us -> 11.5 us  [call(): pl.pallas_call(kernel, name=name, out_shape=[jax.ShapeDtypeStruct(s, d) f...]
  transfers between devices with their start and end apart: 6 -> 5, of which waited for: 3 -> 2; matrix products, arithmetic and copies ran while one was open for 0% -> 0% of each run, Pallas kernels for 3% -> 2%
where the time goes in v8:
time: 204 us; the launch traced here: 203 us
  blocking collectives  179 us (88%)
  Pallas kernels  11.5 us (6%)
  starting transfers between devices  11.5 us (6%)
    all_to_all x11, blocking collectives, exchange(): return lax.all_to_all(value, axes, 0, 0, tiled=True)  179 us
    pallas_call x24, Pallas kernels, call(): pl.pallas_call(kernel, name=name, out_shape=[jax.ShapeDtypeStruct(s, d) f...  11.5 us
    ppermute x5, starting transfers between devices, swap_cores(): return lax.ppermute(value, 'h', [(0, 1), (1, 0)])  11.5 us
  transfers between devices with their start and end apart: 5, of which 2 were waited for; matrix products, arithmetic and copies ran while one was open for 0% of the time, Pallas kernels for 2%

profile of v8, /device:TPU:1, one launch (start us, length us, event | category | flops | bytes accessed | tf_op | source)
XLA Modules:
  0.0 203.1 jit_solution(18391935224915932062)
XLA Ops:
  0.6 1.4 start.1
  2.1 27.2 %all_to_all.121 = bf16[128,4,128]{2,1,0:T(4,128)(2,1)S(1)} all-to-all(bf16[128,4,128]{2,1,0:T(4,128)(2,1)S(1)} %bitcast.51), channel_id=1, replica_groups=mesh['y'=4,'zl'=2,'h'=2,'zh'=4,'x'=4] {'zh','x','y','zl'}, dimensions={0} | all-to-all | bytes 262144 | tf_op jit(solution)/shard_map/all_to_all | solution.py:408
  29.3 2.0 %collective-permute-start = (bf16[512,128]{1,0:T(8,128)(2,1)S(1)}, bf16[512,128]{1,0:T(8,128)(2,1)S(1)}, u32[]{:S(2)}, u32[]{:S(2)}) collective-permute-start(bf16[512,128]{1,0:T(8,128)(2,1)S(1)} %bitcast.37), channel_id=1, source_target_pairs={{0,16},{16,0},{1,17},{17,1},{2,18},{18,2},{3,19},{19,3},{4,20},{20... | collective-permute-start | bytes 393224 | tf_op jit(solution)/shard_map/ppermute | solution.py:412
  32.4 0.6 outgoing.1
  33.0 16.2 %all_to_all.122 = bf16[128,2,128]{2,1,0:T(2,128)(2,1)S(1)} all-to-all(bf16[128,2,128]{2,1,0:T(2,128)(2,1)S(1)} %bitcast.54), channel_id=1, replica_groups=mesh['y'=4,'zl'=2,'h'=2,'zh'=4,'x'=4] {'zh','x','y','zl'}, dimensions={0} | all-to-all | bytes 131072 | tf_op jit(solution)/shard_map/all_to_all | solution.py:408
  49.8 16.6 %all_to_all.123 = bf16[128,4,128]{2,1,0:T(4,128)(2,1)S(1)} all-to-all(bf16[128,4,128]{2,1,0:T(4,128)(2,1)S(1)} %bitcast.50), channel_id=1, replica_groups=mesh['y'=4,'zl'=2,'h'=2,'zh'=4,'x'=4] {'zh','x','y','zl'}, dimensions={0} | all-to-all | bytes 262144 | tf_op jit(solution)/shard_map/all_to_all | solution.py:408
  66.4 2.8 %collective-permute-start.1 = (bf16[512,128]{1,0:T(8,128)(2,1)S(1)}, bf16[512,128]{1,0:T(8,128)(2,1)S(1)}, u32[]{:S(2)}, u32[]{:S(2)}) collective-permute-start(bf16[512,128]{1,0:T(8,128)(2,1)S(1)} %bitcast.35), channel_id=1, source_target_pairs={{0,16},{16,0},{1,17},{17,1},{2,18},{18,2},{3,19},{19,3},{4,20},{20... | collective-permute-start | bytes 393224 | tf_op jit(solution)/shard_map/ppermute | solution.py:412
  70.1 0.7 incoming.1
  70.8 16.3 %all_to_all.124 = bf16[128,2,128]{2,1,0:T(2,128)(2,1)S(1)} all-to-all(bf16[128,2,128]{2,1,0:T(2,128)(2,1)S(1)} %bitcast.46), channel_id=1, replica_groups=mesh['y'=4,'zl'=2,'h'=2,'zh'=4,'x'=4] {'zh','x','y','zl'}, dimensions={0} | all-to-all | bytes 131072 | tf_op jit(solution)/shard_map/all_to_all | solution.py:408
  87.4 16.3 %all_to_all.125 = bf16[128,2,128]{2,1,0:T(2,128)(2,1)S(1)} all-to-all(bf16[128,2,128]{2,1,0:T(2,128)(2,1)S(1)} %bitcast.53), channel_id=1, replica_groups=mesh['y'=4,'zl'=2,'h'=2,'zh'=4,'x'=4] {'zh','x','y','zl'}, dimensions={0} | all-to-all | bytes 131072 | tf_op jit(solution)/shard_map/all_to_all | solution.py:408
  103.7 2.7 %collective-permute-start.2 = (bf16[256,128]{1,0:T(8,128)(2,1)S(1)}, bf16[256,128]{1,0:T(8,128)(2,1)S(1)}, u32[]{:S(2)}, u32[]{:S(2)}) collective-permute-start(bf16[256,128]{1,0:T(8,128)(2,1)S(1)} %bitcast.43), channel_id=1, source_target_pairs={{0,16},{16,0},{1,17},{17,1},{2,18},{18,2},{3,19},{19,3},{4,20},{20... | collective-permute-start | bytes 196616 | tf_op jit(solution)/shard_map/ppermute | solution.py:412
  106.8 0.8 turn_rest.1
  107.6 0.7 incoming_back.1
  108.3 17.5 %all_to_all.126 = bf16[128,4,128]{2,1,0:T(4,128)(2,1)S(1)} all-to-all(bf16[128,4,128]{2,1,0:T(4,128)(2,1)S(1)} %bitcast.39), channel_id=1, replica_groups=mesh['y'=4,'zl'=2,'h'=2,'zh'=4,'x'=4] {'zh','x','y','zl'}, dimensions={0} | all-to-all | bytes 262144 | tf_op jit(solution)/shard_map/all_to_all | solution.py:408
  126.3 16.1 %all_to_all.127 = bf16[128,2,128]{2,1,0:T(2,128)(2,1)S(1)} all-to-all(bf16[128,2,128]{2,1,0:T(2,128)(2,1)S(1)} %bitcast.52), channel_id=1, replica_groups=mesh['y'=4,'zl'=2,'h'=2,'zh'=4,'x'=4] {'zh','x','y','zl'}, dimensions={0} | all-to-all | bytes 131072 | tf_op jit(solution)/shard_map/all_to_all | solution.py:408
  142.4 2.4 %collective-permute-start.3 = (bf16[256,128]{1,0:T(8,128)(2,1)S(1)}, bf16[256,128]{1,0:T(8,128)(2,1)S(1)}, u32[]{:S(2)}, u32[]{:S(2)}) collective-permute-start(bf16[256,128]{1,0:T(8,128)(2,1)S(1)} %bitcast.47), channel_id=1, source_target_pairs={{0,16},{16,0},{1,17},{17,1},{2,18},{18,2},{3,19},{19,3},{4,20},{20... | collective-permute-start | bytes 196616 | tf_op jit(solution)/shard_map/ppermute | solution.py:412
  145.7 0.6 outgoing_back.1
  146.3 17.1 %all_to_all.128 = bf16[128,4,128]{2,1,0:T(4,128)(2,1)S(1)} all-to-all(bf16[128,4,128]{2,1,0:T(4,128)(2,1)S(1)} %bitcast.40), channel_id=1, replica_groups=mesh['y'=4,'zl'=2,'h'=2,'zh'=4,'x'=4] {'zh','x','y','zl'}, dimensions={0} | all-to-all | bytes 262144 | tf_op jit(solution)/shard_map/all_to_all | solution.py:408
  163.7 1.6 collective-permute-start.4
  165.3 1.0 end_rest.1
  166.4 10.0 %all_to_all.129 = bf16[16,48,128]{2,1,0:T(8,128)(2,1)S(1)} all-to-all(bf16[16,48,128]{2,1,0:T(8,128)(2,1)S(1)} %bitcast.32), channel_id=1, replica_groups=mesh['y'=4,'zl'=2,'h'=2,'zh'=4,'x'=4] {'x','y'}, dimensions={0} | all-to-all | bytes 393216 | tf_op jit(solution)/shard_map/all_to_all | solution.py:408
  176.5 9.3 %all_to_all.130 = bf16[8,48,128]{2,1,0:T(8,128)(2,1)S(1)} all-to-all(bf16[8,48,128]{2,1,0:T(8,128)(2,1)S(1)} %bitcast.41), channel_id=1, replica_groups=mesh['y'=4,'zl'=2,'h'=2,'zh'=4,'x'=4] {'zl','zh'}, dimensions={0} | all-to-all | bytes 196608 | tf_op jit(solution)/shard_map/all_to_all | solution.py:408
  185.8 16.2 %all_to_all.131 = bf16[32,48,128]{2,1,0:T(8,128)(2,1)S(1)} all-to-all(bf16[32,48,128]{2,1,0:T(8,128)(2,1)S(1)} %bitcast.30), channel_id=1, replica_groups=mesh['y'=4,'zl'=2,'h'=2,'zh'=4,'x'=4] {'h','x','y'}, dimensions={0} | all-to-all | bytes 786432 | tf_op jit(solution)/shard_map/all_to_all | solution.py:408
  202.0 0.9 place.1
  (29 shorter events, 5.0 us)
Async XLA Ops:
  29.3 3.0 %collective-permute-start = (bf16[512,128]{1,0:T(8,128)(2,1)S(1)}, bf16[512,128]{1,0:T(8,128)(2,1)S(1)}, u32[]{:S(2)}, u32[]{:S(2)}) collective-permute-start(bf16[512,128]{1,0:T(8,128)(2,1)S(1)} %bitcast.37), channel_id=1, source_target_pairs={{0,16},{16,0},{1,17},{17,1},{2,18},{18,2},{3,19},{19,3},{4,20},{20... | collective-permute-start | bytes 393224 | tf_op jit(solution)/shard_map/ppermute | solution.py:412
  32.3 17.0 %copy-start = (bf16[2,128,512]{2,1,0:T(8,128)(2,1)S(1)}, bf16[2,128,512]{2,1,0:T(8,128)(2,1)}, u32[]{:S(2)}) copy-start(bf16[2,128,512]{2,1,0:T(8,128)(2,1)} %w_in.5) | copy-start | bytes 786436
  33.0 16.3 %copy-start.1 = (bf16[2,128,128]{2,1,0:T(8,128)(2,1)S(1)}, bf16[2,128,128]{2,1,0:T(8,128)(2,1)}, u32[]{:S(2)}) copy-start(bf16[2,128,128]{2,1,0:T(8,128)(2,1)} %w_gate.5) | copy-start | bytes 196612
  33.0 16.3 %copy-start.2 = (bf16[2,128,128]{2,1,0:T(8,128)(2,1)S(1)}, bf16[2,128,128]{2,1,0:T(8,128)(2,1)}, u32[]{:S(2)}) copy-start(bf16[2,128,128]{2,1,0:T(8,128)(2,1)} %w_out.5) | copy-start | bytes 196612
  66.4 3.8 %collective-permute-start.1 = (bf16[512,128]{1,0:T(8,128)(2,1)S(1)}, bf16[512,128]{1,0:T(8,128)(2,1)S(1)}, u32[]{:S(2)}, u32[]{:S(2)}) collective-permute-start(bf16[512,128]{1,0:T(8,128)(2,1)S(1)} %bitcast.35), channel_id=1, source_target_pairs={{0,16},{16,0},{1,17},{17,1},{2,18},{18,2},{3,19},{19,3},{4,20},{20... | collective-permute-start | bytes 393224 | tf_op jit(solution)/shard_map/ppermute | solution.py:412
  70.8 16.3 %copy-start.3 = (bf16[16,16,128]{2,1,0:T(8,128)(2,1)S(1)}, bf16[16,16,128]{2,1,0:T(8,128)(2,1)}, u32[]{:S(2)}) copy-start(bf16[16,16,128]{2,1,0:T(8,128)(2,1)} %param.11) | copy-start | bytes 196612
  103.7 3.9 %collective-permute-start.2 = (bf16[256,128]{1,0:T(8,128)(2,1)S(1)}, bf16[256,128]{1,0:T(8,128)(2,1)S(1)}, u32[]{:S(2)}, u32[]{:S(2)}) collective-permute-start(bf16[256,128]{1,0:T(8,128)(2,1)S(1)} %bitcast.43), channel_id=1, source_target_pairs={{0,16},{16,0},{1,17},{17,1},{2,18},{18,2},{3,19},{19,3},{4,20},{20... | collective-permute-start | bytes 196616 | tf_op jit(solution)/shard_map/ppermute | solution.py:412
  142.4 3.3 %collective-permute-start.3 = (bf16[256,128]{1,0:T(8,128)(2,1)S(1)}, bf16[256,128]{1,0:T(8,128)(2,1)S(1)}, u32[]{:S(2)}, u32[]{:S(2)}) collective-permute-start(bf16[256,128]{1,0:T(8,128)(2,1)S(1)} %bitcast.47), channel_id=1, source_target_pairs={{0,16},{16,0},{1,17},{17,1},{2,18},{18,2},{3,19},{19,3},{4,20},{20... | collective-permute-start | bytes 196616 | tf_op jit(solution)/shard_map/ppermute | solution.py:412
  163.7 2.7 %collective-permute-start.4 = (bf16[768,128]{1,0:T(8,128)(2,1)S(1)}, bf16[768,128]{1,0:T(8,128)(2,1)S(1)}, u32[]{:S(2)}, u32[]{:S(2)}) collective-permute-start(bf16[768,128]{1,0:T(8,128)(2,1)S(1)} %get-tuple-element.153), channel_id=1, source_target_pairs={{0,16},{16,0},{1,17},{17,1},{2,18},{18,2},{3,19},{19,3},{4,20},{20... | collective-permute-start | bytes 589832 | tf_op jit(solution)/shard_map/ppermute | solution.py:412

commit v9 on v6

--- a/solution.py
+++ b/solution.py
@@ -44,19 +44,31 @@
     return out
 
 
-def messages_to_half(src, off, w, dst):
+def swap_at_once(tiles):
+    block = lax.broadcasted_iota(jnp.int32, tiles[0].shape, 1) // 16
+    out = []
+    for i in range(8):
+        value = tiles[i]
+        for t in range(8):
+            if t != i:
+                value = jnp.where(block == t, pltpu.roll(tiles[t], 16 * ((t - i) % 8), 1), value)
+        out.append(value)
+    return out
+
+
+def messages_to_half(src, off, w, dst, swap=swap_blocks):
     for half in range(2):
         tiles = [
             src[pl.ds(16 * t * w + off + half, 16, stride=w), :].astype(BF16) for t in range(8)
         ]
-        for t, tile in enumerate(swap_blocks(tiles)):
+        for t, tile in enumerate(swap(tiles)):
             tile = tile.astype(F32)
             for p in range(2):
                 dst[p, pl.ds(half * 8 + t, 8, stride=16), :] = tile[8 * p : 8 * (p + 1)]
     return jnp.concatenate([dst[0], dst[1]], axis=1).astype(BF16)
 
 
-def half_to_messages(value, src, dst, off, w):
+def half_to_messages(value, src, dst, off, w, swap=swap_blocks):
     for p in range(2):
         src[p] = value[p]
     for half in range(2):
@@ -64,7 +76,7 @@
         for t in range(8):
             both = [src[p, pl.ds(half * 8 + t, 8, stride=16), :] for p in range(2)]
             tiles.append(jnp.concatenate(both, axis=0).astype(BF16))
-        for t, tile in enumerate(swap_blocks(tiles)):
+        for t, tile in enumerate(swap(tiles)):
             dst[pl.ds(16 * t * w + off + half, 16, stride=w), :] = tile.astype(F32)
 
 
@@ -335,9 +347,9 @@
 
 def outgoing_kernel(other, a, x_mine, b_ref, send_ref, os, mat, send):
     os[...] = other[...].astype(F32)
-    b = messages_to_half(os, 2, 4, mat)
+    b = messages_to_half(os, 2, 4, mat, swap_at_once)
     b_ref[...] = b
-    half_to_messages(by_parity(x_mine[...], dot(a[...], b, 1, 1)), mat, send, 0, 2)
+    half_to_messages(by_parity(x_mine[...], dot(a[...], b, 1, 1)), mat, send, 0, 2, swap_at_once)
     send_ref[...] = send[...].astype(BF16)
 
 
@@ -389,9 +401,9 @@
 
 def outgoing_back_kernel(other, ga, gb_mine, a_other, send_ref, os, mat, send):
     os[...] = other[...].astype(F32)
-    gx = messages_to_half(os, 0, 2, mat)
+    gx = messages_to_half(os, 0, 2, mat, swap_at_once)
     gb = gb_mine[...] + dot(own_columns(gx), a_other[...], 0, 0)
-    half_to_messages(halves(gb), mat, send, 2, 4)
+    half_to_messages(halves(gb), mat, send, 2, 4, swap_at_once)
     for half in range(2):
         send[pl.ds(half, CH, stride=4), :] = ga[pl.ds(half, CH, stride=2), :]
     send_ref[...] = send[...].astype(BF16)

time: 203 us -> 203 us (level)
  no operation moved by 1% of the time
where the time goes in v9:
time: 203 us; the launch traced here: 202 us
  blocking collectives  173 us (85%)
  starting transfers between devices  15.4 us (8%)
  Pallas kernels  12.1 us (6%)
    all_to_all x11, blocking collectives, exchange(): return lax.all_to_all(value, axes, 0, 0, tiled=True)  173 us
    ppermute x6, starting transfers between devices, swap_cores(): return lax.ppermute(value, 'h', [(0, 1), (1, 0)])  15.4 us
    pallas_call x24, Pallas kernels, call(): pl.pallas_call(kernel, name=name, out_shape=[jax.ShapeDtypeStruct(s, d) f...  12.1 us
  transfers between devices with their start and end apart: 6, of which 3 were waited for; matrix products, arithmetic and copies ran while one was open for 0% of the time, Pallas kernels for 3%

profile of v9, /device:TPU:1, one launch (start us, length us, event | category | flops | bytes accessed | tf_op | source)
XLA Modules:
  0.0 202.1 jit_solution(5154164984960312973)
XLA Ops:
  0.6 1.4 start.1
  2.1 27.2 %all_to_all.121 = bf16[128,4,128]{2,1,0:T(4,128)(2,1)S(1)} all-to-all(bf16[128,4,128]{2,1,0:T(4,128)(2,1)S(1)} %bitcast.52), channel_id=1, replica_groups=mesh['y'=4,'zl'=2,'h'=2,'zh'=4,'x'=4] {'zh','x','y','zl'}, dimensions={0} | all-to-all | bytes 262144 | tf_op jit(solution)/shard_map/all_to_all | solution.py:425
  29.3 2.0 %collective-permute-start = (bf16[512,128]{1,0:T(8,128)(2,1)S(1)}, bf16[512,128]{1,0:T(8,128)(2,1)S(1)}, u32[]{:S(2)}, u32[]{:S(2)}) collective-permute-start(bf16[512,128]{1,0:T(8,128)(2,1)S(1)} %bitcast.39), channel_id=1, source_target_pairs={{0,16},{16,0},{1,17},{17,1},{2,18},{18,2},{3,19},{19,3},{4,20},{20... | collective-permute-start | bytes 393224 | tf_op jit(solution)/shard_map/ppermute | solution.py:429
  33.0 16.2 %all_to_all.122 = bf16[128,2,128]{2,1,0:T(2,128)(2,1)S(1)} all-to-all(bf16[128,2,128]{2,1,0:T(2,128)(2,1)S(1)} %bitcast.57), channel_id=1, replica_groups=mesh['y'=4,'zl'=2,'h'=2,'zh'=4,'x'=4] {'zh','x','y','zl'}, dimensions={0} | all-to-all | bytes 131072 | tf_op jit(solution)/shard_map/all_to_all | solution.py:425
  49.8 16.6 %all_to_all.123 = bf16[128,4,128]{2,1,0:T(4,128)(2,1)S(1)} all-to-all(bf16[128,4,128]{2,1,0:T(4,128)(2,1)S(1)} %bitcast.53), channel_id=1, replica_groups=mesh['y'=4,'zl'=2,'h'=2,'zh'=4,'x'=4] {'zh','x','y','zl'}, dimensions={0} | all-to-all | bytes 262144 | tf_op jit(solution)/shard_map/all_to_all | solution.py:425
  66.4 2.8 %collective-permute-start.1 = (bf16[512,128]{1,0:T(8,128)(2,1)S(1)}, bf16[512,128]{1,0:T(8,128)(2,1)S(1)}, u32[]{:S(2)}, u32[]{:S(2)}) collective-permute-start(bf16[512,128]{1,0:T(8,128)(2,1)S(1)} %bitcast.37), channel_id=1, source_target_pairs={{0,16},{16,0},{1,17},{17,1},{2,18},{18,2},{3,19},{19,3},{4,20},{20... | collective-permute-start | bytes 393224 | tf_op jit(solution)/shard_map/ppermute | solution.py:429
  70.2 0.7 incoming.1
  70.8 16.3 %all_to_all.124 = bf16[128,2,128]{2,1,0:T(2,128)(2,1)S(1)} all-to-all(bf16[128,2,128]{2,1,0:T(2,128)(2,1)S(1)} %bitcast.49), channel_id=1, replica_groups=mesh['y'=4,'zl'=2,'h'=2,'zh'=4,'x'=4] {'zh','x','y','zl'}, dimensions={0} | all-to-all | bytes 131072 | tf_op jit(solution)/shard_map/all_to_all | solution.py:425
  87.4 16.3 %all_to_all.125 = bf16[128,2,128]{2,1,0:T(2,128)(2,1)S(1)} all-to-all(bf16[128,2,128]{2,1,0:T(2,128)(2,1)S(1)} %bitcast.56), channel_id=1, replica_groups=mesh['y'=4,'zl'=2,'h'=2,'zh'=4,'x'=4] {'zh','x','y','zl'}, dimensions={0} | all-to-all | bytes 131072 | tf_op jit(solution)/shard_map/all_to_all | solution.py:425
  103.7 2.7 %collective-permute-start.2 = (bf16[256,128]{1,0:T(8,128)(2,1)S(1)}, bf16[256,128]{1,0:T(8,128)(2,1)S(1)}, u32[]{:S(2)}, u32[]{:S(2)}) collective-permute-start(bf16[256,128]{1,0:T(8,128)(2,1)S(1)} %bitcast.46), channel_id=1, source_target_pairs={{0,16},{16,0},{1,17},{17,1},{2,18},{18,2},{3,19},{19,3},{4,20},{20... | collective-permute-start | bytes 196616 | tf_op jit(solution)/shard_map/ppermute | solution.py:429
  106.8 0.8 turn_rest.1
  107.6 0.7 incoming_back.1
  108.3 17.5 %all_to_all.126 = bf16[128,4,128]{2,1,0:T(4,128)(2,1)S(1)} all-to-all(bf16[128,4,128]{2,1,0:T(4,128)(2,1)S(1)} %bitcast.41), channel_id=1, replica_groups=mesh['y'=4,'zl'=2,'h'=2,'zh'=4,'x'=4] {'zh','x','y','zl'}, dimensions={0} | all-to-all | bytes 262144 | tf_op jit(solution)/shard_map/all_to_all | solution.py:425
  126.3 16.1 %all_to_all.127 = bf16[128,2,128]{2,1,0:T(2,128)(2,1)S(1)} all-to-all(bf16[128,2,128]{2,1,0:T(2,128)(2,1)S(1)} %bitcast.55), channel_id=1, replica_groups=mesh['y'=4,'zl'=2,'h'=2,'zh'=4,'x'=4] {'zh','x','y','zl'}, dimensions={0} | all-to-all | bytes 131072 | tf_op jit(solution)/shard_map/all_to_all | solution.py:425
  142.5 2.3 %collective-permute-start.3 = (bf16[256,128]{1,0:T(8,128)(2,1)S(1)}, bf16[256,128]{1,0:T(8,128)(2,1)S(1)}, u32[]{:S(2)}, u32[]{:S(2)}) collective-permute-start(bf16[256,128]{1,0:T(8,128)(2,1)S(1)} %bitcast.50), channel_id=1, source_target_pairs={{0,16},{16,0},{1,17},{17,1},{2,18},{18,2},{3,19},{19,3},{4,20},{20... | collective-permute-start | bytes 196616 | tf_op jit(solution)/shard_map/ppermute | solution.py:429
  146.4 17.1 %all_to_all.128 = bf16[128,4,128]{2,1,0:T(4,128)(2,1)S(1)} all-to-all(bf16[128,4,128]{2,1,0:T(4,128)(2,1)S(1)} %bitcast.42), channel_id=1, replica_groups=mesh['y'=4,'zl'=2,'h'=2,'zh'=4,'x'=4] {'zh','x','y','zl'}, dimensions={0} | all-to-all | bytes 262144 | tf_op jit(solution)/shard_map/all_to_all | solution.py:425
  163.7 1.6 collective-permute-start.4
  165.4 1.0 end_rest.1
  166.5 10.0 %all_to_all.129 = bf16[16,48,128]{2,1,0:T(8,128)(2,1)S(1)} all-to-all(bf16[16,48,128]{2,1,0:T(8,128)(2,1)S(1)} %bitcast.33), channel_id=1, replica_groups=mesh['y'=4,'zl'=2,'h'=2,'zh'=4,'x'=4] {'x','y'}, dimensions={0} | all-to-all | bytes 393216 | tf_op jit(solution)/shard_map/all_to_all | solution.py:425
  176.5 9.3 %all_to_all.130 = bf16[8,48,128]{2,1,0:T(8,128)(2,1)S(1)} all-to-all(bf16[8,48,128]{2,1,0:T(8,128)(2,1)S(1)} %bitcast.44), channel_id=1, replica_groups=mesh['y'=4,'zl'=2,'h'=2,'zh'=4,'x'=4] {'zl','zh'}, dimensions={0} | all-to-all | bytes 196608 | tf_op jit(solution)/shard_map/all_to_all | solution.py:425
  185.9 10.4 %all_to_all.131 = bf16[16,48,128]{2,1,0:T(8,128)(2,1)S(1)} all-to-all(bf16[16,48,128]{2,1,0:T(8,128)(2,1)S(1)} %bitcast.32), channel_id=1, replica_groups=mesh['y'=4,'zl'=2,'h'=2,'zh'=4,'x'=4] {'x','y'}, dimensions={0} | all-to-all | bytes 393216 | tf_op jit(solution)/shard_map/all_to_all | solution.py:425
  196.3 3.8 %collective-permute-start.5 = (bf16[768,128]{1,0:T(8,128)(2,1)S(1)}, bf16[768,128]{1,0:T(8,128)(2,1)S(1)}, u32[]{:S(2)}, u32[]{:S(2)}) collective-permute-start(bf16[768,128]{1,0:T(8,128)(2,1)S(1)} %bitcast.29), channel_id=1, source_target_pairs={{0,16},{16,0},{1,17},{17,1},{2,18},{18,2},{3,19},{19,3},{4,20},{20... | collective-permute-start | bytes 589832 | tf_op jit(solution)/shard_map/ppermute | solution.py:429
  200.1 0.8 place_mine.1
  201.2 0.8 place_other.1
  (31 shorter events, 6.6 us)
Async XLA Ops:
  29.3 3.0 %collective-permute-start = (bf16[512,128]{1,0:T(8,128)(2,1)S(1)}, bf16[512,128]{1,0:T(8,128)(2,1)S(1)}, u32[]{:S(2)}, u32[]{:S(2)}) collective-permute-start(bf16[512,128]{1,0:T(8,128)(2,1)S(1)} %bitcast.39), channel_id=1, source_target_pairs={{0,16},{16,0},{1,17},{17,1},{2,18},{18,2},{3,19},{19,3},{4,20},{20... | collective-permute-start | bytes 393224 | tf_op jit(solution)/shard_map/ppermute | solution.py:429
  32.1 17.1 %copy-start = (bf16[2,128,512]{2,1,0:T(8,128)(2,1)S(1)}, bf16[2,128,512]{2,1,0:T(8,128)(2,1)}, u32[]{:S(2)}) copy-start(bf16[2,128,512]{2,1,0:T(8,128)(2,1)} %w_in.5) | copy-start | bytes 786436
  33.0 16.3 %copy-start.1 = (bf16[2,128,128]{2,1,0:T(8,128)(2,1)S(1)}, bf16[2,128,128]{2,1,0:T(8,128)(2,1)}, u32[]{:S(2)}) copy-start(bf16[2,128,128]{2,1,0:T(8,128)(2,1)} %w_gate.5) | copy-start | bytes 196612
  33.0 16.3 %copy-start.2 = (bf16[2,128,128]{2,1,0:T(8,128)(2,1)S(1)}, bf16[2,128,128]{2,1,0:T(8,128)(2,1)}, u32[]{:S(2)}) copy-start(bf16[2,128,128]{2,1,0:T(8,128)(2,1)} %w_out.5) | copy-start | bytes 196612
  66.4 3.8 %collective-permute-start.1 = (bf16[512,128]{1,0:T(8,128)(2,1)S(1)}, bf16[512,128]{1,0:T(8,128)(2,1)S(1)}, u32[]{:S(2)}, u32[]{:S(2)}) collective-permute-start(bf16[512,128]{1,0:T(8,128)(2,1)S(1)} %bitcast.37), channel_id=1, source_target_pairs={{0,16},{16,0},{1,17},{17,1},{2,18},{18,2},{3,19},{19,3},{4,20},{20... | collective-permute-start | bytes 393224 | tf_op jit(solution)/shard_map/ppermute | solution.py:429
  70.8 16.3 %copy-start.3 = (bf16[16,16,128]{2,1,0:T(8,128)(2,1)S(1)}, bf16[16,16,128]{2,1,0:T(8,128)(2,1)}, u32[]{:S(2)}) copy-start(bf16[16,16,128]{2,1,0:T(8,128)(2,1)} %param.11) | copy-start | bytes 196612
  103.7 3.9 %collective-permute-start.2 = (bf16[256,128]{1,0:T(8,128)(2,1)S(1)}, bf16[256,128]{1,0:T(8,128)(2,1)S(1)}, u32[]{:S(2)}, u32[]{:S(2)}) collective-permute-start(bf16[256,128]{1,0:T(8,128)(2,1)S(1)} %bitcast.46), channel_id=1, source_target_pairs={{0,16},{16,0},{1,17},{17,1},{2,18},{18,2},{3,19},{19,3},{4,20},{20... | collective-permute-start | bytes 196616 | tf_op jit(solution)/shard_map/ppermute | solution.py:429
  142.5 3.3 %collective-permute-start.3 = (bf16[256,128]{1,0:T(8,128)(2,1)S(1)}, bf16[256,128]{1,0:T(8,128)(2,1)S(1)}, u32[]{:S(2)}, u32[]{:S(2)}) collective-permute-start(bf16[256,128]{1,0:T(8,128)(2,1)S(1)} %bitcast.50), channel_id=1, source_target_pairs={{0,16},{16,0},{1,17},{17,1},{2,18},{18,2},{3,19},{19,3},{4,20},{20... | collective-permute-start | bytes 196616 | tf_op jit(solution)/shard_map/ppermute | solution.py:429
  163.7 2.7 %collective-permute-start.4 = (bf16[768,128]{1,0:T(8,128)(2,1)S(1)}, bf16[768,128]{1,0:T(8,128)(2,1)S(1)}, u32[]{:S(2)}, u32[]{:S(2)}) collective-permute-start(bf16[768,128]{1,0:T(8,128)(2,1)S(1)} %get-tuple-element.150), channel_id=1, source_target_pairs={{0,16},{16,0},{1,17},{17,1},{2,18},{18,2},{3,19},{19,3},{4,20},{20... | collective-permute-start | bytes 589832 | tf_op jit(solution)/shard_map/ppermute | solution.py:429
  196.3 4.9 %collective-permute-start.5 = (bf16[768,128]{1,0:T(8,128)(2,1)S(1)}, bf16[768,128]{1,0:T(8,128)(2,1)S(1)}, u32[]{:S(2)}, u32[]{:S(2)}) collective-permute-start(bf16[768,128]{1,0:T(8,128)(2,1)S(1)} %bitcast.29), channel_id=1, source_target_pairs={{0,16},{16,0},{1,17},{17,1},{2,18},{18,2},{3,19},{19,3},{4,20},{20... | collective-permute-start | bytes 589832 | tf_op jit(solution)/shard_map/ppermute | solution.py:429
